TPU v7x, 128 devices: a whole 4x4x4 slice. The times are simulated.
128 devices in a mesh: head: 4 (over y_lo, core), tile: 32 (over y_hi, z, x).
Axes of the slice: x: 4, y: 4 (y_hi: 2, y_lo: 2; y = y_hi * 2 + y_lo), z: 4, core: 2. Of those that a mesh axis runs over, the one named last changes fastest.
Arguments:
- queries: bfloat16 [64, 384, 3072], P('tile', 'head'), may hold values from -16 to 16
- keys: bfloat16 [64, 384, 3072], P('tile', 'head'), may hold values from -8 to 8
- values: bfloat16 [64, 384, 3072], P('tile', 'head'), may hold values from -6 to 6
- neighbours: int32 [64, 27], P('tile'), may hold values from -1 to 63, as said below
- w_out: bfloat16 [3072, 3072], P('head'), may hold values from -1.25 to 1.25
Outputs:
- projected: bfloat16 [64, 384, 3072], P('tile', 'head')
Inputs may be any that keep to these rules, and one draw needn't show every extreme that they name: `neighbours`: tile s lies at time s % 2, height s // 2 // 8 and width s // 2 % 8 of a grid of 2 x 4 x 8 tiles. Entry j of row s is either -1 or the tile at offset (j // 9 - 1, j // 3 % 3 - 1, j % 3 - 1) from tile s in that grid; it is -1 where that tile lies outside the grid and may be -1 elsewhere too; entry 13 (the tile itself) is never -1.
All inputs are finite; a program needn't handle non-finite values.
Results may differ from a plain program's by a relative error of at most 0.017.
Values may be sent and summed in bfloat16 or wider, within the bound.
No kernel may reach another device: no remote copies, remote signals or barrier semaphores. Data moves between devices by JAX's collectives and lax.ppermute only.
A program may use at most 192 MiB of HBM per device.

v0:
```python
import jax
import jax.numpy as jnp
from jax import lax
from jax.sharding import PartitionSpec as P

HEAD_DIM = 128
DEV_H = 4


def from_behind(block, axis, distance):
    devices = range(lax.axis_size(axis))
    route = [(i - distance, i) for i in devices if i - distance in devices]
    return lax.ppermute(block, axis, route)


def on_device(queries, keys, values, neighbours, w_out):
    q_heads, k_heads, v_heads = (
        lax.all_to_all(queries, "head", split_axis=2, concat_axis=1, tiled=True),
        lax.all_to_all(keys, "head", split_axis=2, concat_axis=1, tiled=True),
        lax.all_to_all(values, "head", split_axis=2, concat_axis=1, tiled=True),
    )
    tile_count, tile_rows, local_width = q_heads.shape
    heads_here = local_width // HEAD_DIM
    score_scale = HEAD_DIM ** (-0.5)
    owners = lax.axis_size("tile")
    my_index = lax.axis_index("tile")
    grid_width = owners // DEV_H
    own_row = my_index // grid_width
    own_column = my_index % grid_width
    query_rows = q_heads.reshape(tile_count * tile_rows, heads_here, HEAD_DIM)
    key_value = jnp.stack([k_heads, v_heads])

    def tile_step(running, tile_item):
        key_tile, value_tile, tile_id = tile_item
        allowed = jnp.any(neighbours == tile_id, axis=1)
        row_mask = jnp.repeat(allowed, tile_rows)[:, None, None]
        row_max, row_sum, weighted = running
        scores = (
            jnp.einsum(
                "qhd,khd->qhk",
                query_rows,
                key_tile.reshape(tile_rows, heads_here, HEAD_DIM),
                preferred_element_type=jnp.float32,
            )
            * score_scale
        )
        scores = jnp.where(row_mask, scores, jnp.float32(-1e30))
        new_max = jnp.maximum(row_max, jnp.max(scores, axis=2))
        weights = jnp.where(row_mask, jnp.exp(scores - new_max[:, :, None]), jnp.float32(0.0))
        factor = jnp.exp(row_max - new_max)
        row_sum = row_sum * factor + jnp.sum(weights, axis=2)
        update = jnp.einsum(
            "qhk,khd->qhd",
            weights.astype(jnp.bfloat16),
            value_tile.reshape(tile_rows, heads_here, HEAD_DIM),
            preferred_element_type=jnp.float32,
        )
        weighted = weighted * factor[:, :, None] + update
        running = (new_max, row_sum, weighted)
        return (running, None)

    def absorb(running, kv_block, first_tile):
        tile_ids = first_tile + jnp.arange(kv_block.shape[1], dtype=jnp.int32)
        running, unused = lax.scan(tile_step, running, (kv_block[0], kv_block[1], tile_ids))
        return running

    query_total = tile_count * tile_rows
    initial = (
        jnp.full((query_total, heads_here), -1e30, jnp.float32),
        jnp.zeros((query_total, heads_here), jnp.float32),
        jnp.zeros((query_total, heads_here, HEAD_DIM), jnp.float32),
    )
    running = absorb(initial, key_value, my_index * tile_count)
    for row_step in (-1, 0, 1):
        for column_step in (-1, 0, 1):
            if row_step != 0 or column_step != 0:
                shifted = from_behind(key_value, "tile", -(row_step * grid_width + column_step))
                source = my_index + row_step * grid_width + column_step
                row_next = own_row + row_step
                column_next = own_column + column_step
                present = (
                    (row_next >= 0)
                    & (row_next < DEV_H)
                    & (column_next >= 0)
                    & (column_next < grid_width)
                )
                running = absorb(
                    running, shifted, jnp.where(present, source * tile_count, -2 * tile_count - 8)
                )
    row_max, row_sum, weighted = running
    attention = (
        (weighted / row_sum[:, :, None])
        .astype(jnp.bfloat16)
        .reshape(tile_count, tile_rows, local_width)
    )
    group_count = lax.axis_size("head")
    arranged = attention.reshape(tile_count, group_count, tile_rows // group_count, local_width)
    arranged = arranged.transpose(1, 0, 2, 3).reshape(
        group_count * tile_count * (tile_rows // group_count), local_width
    )
    projected = lax.psum_scatter(
        jnp.dot(arranged, w_out, preferred_element_type=jnp.float32).astype(jnp.bfloat16),
        "head",
        scatter_dimension=0,
        tiled=True,
    )
    return projected.reshape(tile_count, tile_rows // group_count, w_out.shape[1])


def solution(mesh):
    placed = (
        P("tile", "head", None),
        P("tile", "head", None),
        P("tile", "head", None),
        P("tile", None),
        P("head", None),
    )
    return jax.shard_map(
        on_device, mesh=mesh, in_specs=placed, out_specs=P("tile", "head", None), check_vma=False
    )
```

profile of v0, /device:TPU:6, one launch (start us, length us, event | category | flops | bytes accessed | tf_op | source)
XLA Modules:
  0.0 642.5 jit_solution(3179706577540834179)
XLA Ops:
  6.5 4.6 copy.193
  11.1 3.6 all-to-all-start
  17.7 17.0 %all-to-all-done = bf16[2,96,3072]{1,0,2:T(2,128)(2,1)S(1)} async-done(((bf16[2,96,3072]{1,0,2:T(2,128)(2,1)}), bf16[2,96,3072]{1,0,2:T(2,128)(2,1)S(1)}, u32[]{:S(2)}, u32[]{:S(2)}) %all-to-all-start) | async-done | bytes 1179680 | tf_op jit(solution)/shard_map/all_to_all | solution.py:19
  34.7 4.4 all-to-all-start.2
  42.2 17.1 %all-to-all-done.2 = bf16[2,96,3072]{1,0,2:T(2,128)(2,1)} async-done(((bf16[2,96,3072]{1,0,2:T(2,128)(2,1)}), bf16[2,96,3072]{1,0,2:T(2,128)(2,1)}, u32[]{:S(2)}, u32[]{:S(2)}) %all-to-all-start.2) | async-done | bytes 1179680 | tf_op jit(solution)/shard_map/all_to_all | solution.py:20
  59.2 4.3 all-to-all-start.1
  68.6 4.0 copy.251
  75.5 7.3 %collective-permute-start = (bf16[2,2,384,768]{3,2,1,0:T(8,128)(2,1)}, bf16[2,2,384,768]{3,2,1,0:T(8,128)(2,1)}, u32[]{:S(2)}, u32[]{:S(2)}) collective-permute-start(bf16[2,2,384,768]{3,2,1,0:T(8,128)(2,1)} %pad_maximum_fusion), channel_id=1, source_target_pairs={{0,9},{1,10},{2,11},{3,12},{4,13},{5,14},{6,15},{7,16},{8,17},{9,1... | collective-permute-start | bytes 7077896 | tf_op jit(solution)/shard_map/ppermute | solution.py:13
  82.8 4.6 collective-permute-start.1
  87.4 6.3 collective-permute-start.2
  99.5 3.6 copy.197
  106.9 38.4 %while.135 = (s32[]{:T(128)}, f32[768,6]{0,1:T(8,128)S(1)}, f32[768,6]{0,1:T(8,128)S(1)}, f32[768,6,128]{0,2,1:T(8,128)}, s32[2]{0:T(128)S(1)}, /*index=5*/s32[2...) while((s32[]{:T(128)}, f32[768,6]{0,1:T(8,128)S(1)}, ...), condition=%wide.region_4.5_spmd.clone, body=%wide.region_0.4_spmd.clone.sunk | while | flops 930765440 | bytes 42767260 | solution.py:64
  110.0 4.1 bitcast_reduce_fusion.26
  114.2 4.6 fusion.237
  119.2 6.6 %bitcast_add_fusion.26 = f32[768,6,128]{0,2,1:T(8,128)} fusion(f32[768,6,128]{0,2,1:T(8,128)} %get-tuple-element.1737, bf16[384,6,128]{0,2,1:T(8,128)(2,1)S(1)} %bitcast.444, f32[6,384,768]{2,1,0:T(8,128)} %get-tuple-element.1719, f32[768,6]{0,1:T(8,128)S(1)} %select_maximum_fusion.2, pred[768]{0:T(1024)(128)(4,1)S(1)} %broadcast_in_dim.679, ...), kind=kOutput, calls=%fused_computation.162.clone.1 | convolution fusion | flops 463601664 | bytes 12423937 | tf_op jit(solution)/shard_map/while/body/eval_jaxpr/qhk,khd->qhd/dot_general | solution.py:52
  128.9 4.1 bitcast_reduce_fusion.26
  133.0 4.6 fusion.237
  138.0 7.3 %bitcast_add_fusion.26 = f32[768,6,128]{0,2,1:T(8,128)} fusion(f32[768,6,128]{0,2,1:T(8,128)} %get-tuple-element.1737, bf16[384,6,128]{0,2,1:T(8,128)(2,1)S(1)} %bitcast.444, f32[6,384,768]{2,1,0:T(8,128)} %get-tuple-element.1719, f32[768,6]{0,1:T(8,128)S(1)} %select_maximum_fusion.2, pred[768]{0:T(1024)(128)(4,1)S(1)} %broadcast_in_dim.679, ...), kind=kOutput, calls=%fused_computation.162.clone.1 | convolution fusion | flops 463601664 | bytes 12423937 | tf_op jit(solution)/shard_map/while/body/eval_jaxpr/qhk,khd->qhd/dot_general | solution.py:52
  145.3 23.5 %collective-permute-done = bf16[2,2,384,768]{3,2,1,0:T(8,128)(2,1)} collective-permute-done((bf16[2,2,384,768]{3,2,1,0:T(8,128)(2,1)}, bf16[2,2,384,768]{3,2,1,0:T(8,128)(2,1)}, u32[]{:S(2)}, u32[]{:S(2)}) %collective-permute-start) | collective-permute-done | bytes 2359328 | tf_op jit(solution)/shard_map/ppermute | solution.py:13
  173.5 29.1 %while.127 = (s32[]{:T(128)}, f32[768,6]{0,1:T(8,128)S(1)}, f32[768,6]{0,1:T(8,128)S(1)}, f32[768,6,128]{0,2,1:T(8,128)}, s32[2]{0:T(128)S(1)}, /*index=5*/s32[2...) while((s32[]{:T(128)}, f32[768,6]{0,1:T(8,128)S(1)}, ...), condition=%wide.region_9.10_spmd, body=%wide.region_5.9_spmd.sunk | while | flops 930161792 | bytes 61641584 | solution.py:64
  180.9 7.1 %bitcast_add_fusion.18 = f32[768,6,128]{0,2,1:T(8,128)} fusion(f32[768,6,128]{0,2,1:T(8,128)} %get-tuple-element.1769, bf16[384,6,128]{0,2,1:T(8,128)(2,1)S(1)} %bitcast.445, f32[6,384,768]{2,1,0:T(8,128)} %copy-done, f32[768,6]{0,1:T(8,128)S(1)} %max.38, pred[768]{0:T(1024)(128)(4,1)S(1)} %broadcast_in_dim.583, f32[768,6]{0,1:T(8,128)S(1)} %get-tuple-element.1602), kind=kOutput, calls=%fused_computation.10.clone.1 | convolution fusion | flops 463011840 | bytes 12423936 | tf_op jit(solution)/shard_map/while/body/eval_jaxpr/qhk,khd->qhd/dot_general | solution.py:52
  195.5 7.1 %bitcast_add_fusion.18 = f32[768,6,128]{0,2,1:T(8,128)} fusion(f32[768,6,128]{0,2,1:T(8,128)} %get-tuple-element.1769, bf16[384,6,128]{0,2,1:T(8,128)(2,1)S(1)} %bitcast.445, f32[6,384,768]{2,1,0:T(8,128)} %copy-done, f32[768,6]{0,1:T(8,128)S(1)} %max.38, pred[768]{0:T(1024)(128)(4,1)S(1)} %broadcast_in_dim.583, f32[768,6]{0,1:T(8,128)S(1)} %get-tuple-element.1602), kind=kOutput, calls=%fused_computation.10.clone.1 | convolution fusion | flops 463011840 | bytes 12423936 | tf_op jit(solution)/shard_map/while/body/eval_jaxpr/qhk,khd->qhd/dot_general | solution.py:52
  202.6 32.0 %collective-permute-done.1 = bf16[2,2,384,768]{3,2,1,0:T(8,128)(2,1)} collective-permute-done((bf16[2,2,384,768]{3,2,1,0:T(8,128)(2,1)}, bf16[2,2,384,768]{3,2,1,0:T(8,128)(2,1)}, u32[]{:S(2)}, u32[]{:S(2)}) %collective-permute-start.1) | collective-permute-done | bytes 2359328 | tf_op jit(solution)/shard_map/ppermute | solution.py:13
  239.1 29.5 %while.128 = (s32[]{:T(128)}, f32[768,6]{0,1:T(8,128)S(1)}, f32[768,6]{0,1:T(8,128)S(1)}, f32[768,6,128]{0,2,1:T(8,128)}, s32[2]{0:T(128)S(1)}, /*index=5*/s32[2...) while((s32[]{:T(128)}, f32[768,6]{0,1:T(8,128)S(1)}, ...), condition=%wide.region_14.15_spmd, body=%wide.region_10.14_spmd.sunk | while | flops 930161792 | bytes 61641584 | solution.py:64
  246.7 7.1 %bitcast_add_fusion.19 = f32[768,6,128]{0,2,1:T(8,128)} fusion(f32[768,6,128]{0,2,1:T(8,128)} %get-tuple-element.1799, bf16[384,6,128]{0,2,1:T(8,128)(2,1)S(1)} %bitcast.446, f32[6,384,768]{2,1,0:T(8,128)} %copy-done.1, f32[768,6]{0,1:T(8,128)S(1)} %max.39, pred[768]{0:T(1024)(128)(4,1)S(1)} %broadcast_in_dim.595, f32[768,6]{0,1:T(8,128)S(1)} %get-tuple-element.1617), kind=kOutput, calls=%fused_computation.29.clone.1 | convolution fusion | flops 463011840 | bytes 12423936 | tf_op jit(solution)/shard_map/while/body/eval_jaxpr/qhk,khd->qhd/dot_general | solution.py:52
  261.4 7.1 %bitcast_add_fusion.19 = f32[768,6,128]{0,2,1:T(8,128)} fusion(f32[768,6,128]{0,2,1:T(8,128)} %get-tuple-element.1799, bf16[384,6,128]{0,2,1:T(8,128)(2,1)S(1)} %bitcast.446, f32[6,384,768]{2,1,0:T(8,128)} %copy-done.1, f32[768,6]{0,1:T(8,128)S(1)} %max.39, pred[768]{0:T(1024)(128)(4,1)S(1)} %broadcast_in_dim.595, f32[768,6]{0,1:T(8,128)S(1)} %get-tuple-element.1617), kind=kOutput, calls=%fused_computation.29.clone.1 | convolution fusion | flops 463011840 | bytes 12423936 | tf_op jit(solution)/shard_map/while/body/eval_jaxpr/qhk,khd->qhd/dot_general | solution.py:52
  273.3 29.6 %while.129 = (s32[]{:T(128)}, f32[768,6]{0,1:T(8,128)S(1)}, f32[768,6]{0,1:T(8,128)S(1)}, f32[768,6,128]{0,2,1:T(8,128)}, s32[2]{0:T(128)S(1)}, /*index=5*/s32[2...) while((s32[]{:T(128)}, f32[768,6]{0,1:T(8,128)S(1)}, ...), condition=%wide.region_19.20_spmd, body=%wide.region_15.19_spmd.sunk | while | flops 930161792 | bytes 61641584 | solution.py:64
  281.0 7.1 %bitcast_add_fusion.20 = f32[768,6,128]{0,2,1:T(8,128)} fusion(f32[768,6,128]{0,2,1:T(8,128)} %get-tuple-element.1829, bf16[384,6,128]{0,2,1:T(8,128)(2,1)S(1)} %bitcast.447, f32[6,384,768]{2,1,0:T(8,128)} %copy-done.2, f32[768,6]{0,1:T(8,128)S(1)} %max.40, pred[768]{0:T(1024)(128)(4,1)S(1)} %broadcast_in_dim.607, f32[768,6]{0,1:T(8,128)S(1)} %get-tuple-element.1632), kind=kOutput, calls=%fused_computation.48.clone.1 | convolution fusion | flops 463011840 | bytes 12423936 | tf_op jit(solution)/shard_map/while/body/eval_jaxpr/qhk,khd->qhd/dot_general | solution.py:52
  295.8 7.1 %bitcast_add_fusion.20 = f32[768,6,128]{0,2,1:T(8,128)} fusion(f32[768,6,128]{0,2,1:T(8,128)} %get-tuple-element.1829, bf16[384,6,128]{0,2,1:T(8,128)(2,1)S(1)} %bitcast.447, f32[6,384,768]{2,1,0:T(8,128)} %copy-done.2, f32[768,6]{0,1:T(8,128)S(1)} %max.40, pred[768]{0:T(1024)(128)(4,1)S(1)} %broadcast_in_dim.607, f32[768,6]{0,1:T(8,128)S(1)} %get-tuple-element.1632), kind=kOutput, calls=%fused_computation.48.clone.1 | convolution fusion | flops 463011840 | bytes 12423936 | tf_op jit(solution)/shard_map/while/body/eval_jaxpr/qhk,khd->qhd/dot_general | solution.py:52
  302.9 3.2 slice_bitcast_fusion.8
  306.1 29.2 %while.130 = (s32[]{:T(128)}, f32[768,6]{0,1:T(8,128)S(1)}, f32[768,6]{0,1:T(8,128)S(1)}, f32[768,6,128]{0,2,1:T(8,128)}, s32[2]{0:T(128)S(1)}, /*index=5*/s32[2...) while((s32[]{:T(128)}, f32[768,6]{0,1:T(8,128)S(1)}, ...), condition=%wide.region_24.25_spmd, body=%wide.region_20.24_spmd.sunk | while | flops 930161792 | bytes 61641584 | solution.py:64
  313.6 7.1 %bitcast_add_fusion.21 = f32[768,6,128]{0,2,1:T(8,128)} fusion(f32[768,6,128]{0,2,1:T(8,128)} %get-tuple-element.1859, bf16[384,6,128]{0,2,1:T(8,128)(2,1)S(1)} %bitcast.448, f32[6,384,768]{2,1,0:T(8,128)} %copy-done.3, f32[768,6]{0,1:T(8,128)S(1)} %max.41, pred[768]{0:T(1024)(128)(4,1)S(1)} %broadcast_in_dim.619, f32[768,6]{0,1:T(8,128)S(1)} %get-tuple-element.1647), kind=kOutput, calls=%fused_computation.67.clone.1 | convolution fusion | flops 463011840 | bytes 12423936 | tf_op jit(solution)/shard_map/while/body/eval_jaxpr/qhk,khd->qhd/dot_general | solution.py:52
  328.2 7.1 %bitcast_add_fusion.21 = f32[768,6,128]{0,2,1:T(8,128)} fusion(f32[768,6,128]{0,2,1:T(8,128)} %get-tuple-element.1859, bf16[384,6,128]{0,2,1:T(8,128)(2,1)S(1)} %bitcast.448, f32[6,384,768]{2,1,0:T(8,128)} %copy-done.3, f32[768,6]{0,1:T(8,128)S(1)} %max.41, pred[768]{0:T(1024)(128)(4,1)S(1)} %broadcast_in_dim.619, f32[768,6]{0,1:T(8,128)S(1)} %get-tuple-element.1647), kind=kOutput, calls=%fused_computation.67.clone.1 | convolution fusion | flops 463011840 | bytes 12423936 | tf_op jit(solution)/shard_map/while/body/eval_jaxpr/qhk,khd->qhd/dot_general | solution.py:52
  335.4 3.2 slice_bitcast_fusion.6
  338.6 29.8 %while.131 = (s32[]{:T(128)}, f32[768,6]{0,1:T(8,128)S(1)}, f32[768,6]{0,1:T(8,128)S(1)}, f32[768,6,128]{0,2,1:T(8,128)}, s32[2]{0:T(128)S(1)}, /*index=5*/s32[2...) while((s32[]{:T(128)}, f32[768,6]{0,1:T(8,128)S(1)}, ...), condition=%wide.region_29.30_spmd, body=%wide.region_25.29_spmd.sunk | while | flops 930161792 | bytes 61641584 | solution.py:64
  346.5 7.1 %bitcast_add_fusion.22 = f32[768,6,128]{0,2,1:T(8,128)} fusion(f32[768,6,128]{0,2,1:T(8,128)} %get-tuple-element.1889, bf16[384,6,128]{0,2,1:T(8,128)(2,1)S(1)} %bitcast.449, f32[6,384,768]{2,1,0:T(8,128)} %copy-done.4, f32[768,6]{0,1:T(8,128)S(1)} %max.42, pred[768]{0:T(1024)(128)(4,1)S(1)} %broadcast_in_dim.631, f32[768,6]{0,1:T(8,128)S(1)} %get-tuple-element.1662), kind=kOutput, calls=%fused_computation.86.clone.1 | convolution fusion | flops 463011840 | bytes 12423936 | tf_op jit(solution)/shard_map/while/body/eval_jaxpr/qhk,khd->qhd/dot_general | solution.py:52
  361.2 7.1 %bitcast_add_fusion.22 = f32[768,6,128]{0,2,1:T(8,128)} fusion(f32[768,6,128]{0,2,1:T(8,128)} %get-tuple-element.1889, bf16[384,6,128]{0,2,1:T(8,128)(2,1)S(1)} %bitcast.449, f32[6,384,768]{2,1,0:T(8,128)} %copy-done.4, f32[768,6]{0,1:T(8,128)S(1)} %max.42, pred[768]{0:T(1024)(128)(4,1)S(1)} %broadcast_in_dim.631, f32[768,6]{0,1:T(8,128)S(1)} %get-tuple-element.1662), kind=kOutput, calls=%fused_computation.86.clone.1 | convolution fusion | flops 463011840 | bytes 12423936 | tf_op jit(solution)/shard_map/while/body/eval_jaxpr/qhk,khd->qhd/dot_general | solution.py:52
  371.5 29.6 %while.132 = (s32[]{:T(128)}, f32[768,6]{0,1:T(8,128)S(1)}, f32[768,6]{0,1:T(8,128)S(1)}, f32[768,6,128]{0,2,1:T(8,128)}, s32[2]{0:T(128)S(1)}, /*index=5*/s32[2...) while((s32[]{:T(128)}, f32[768,6]{0,1:T(8,128)S(1)}, ...), condition=%wide.region_34.35_spmd, body=%wide.region_30.34_spmd.sunk | while | flops 930161792 | bytes 61641584 | solution.py:64
  379.2 7.1 %bitcast_add_fusion.23 = f32[768,6,128]{0,2,1:T(8,128)} fusion(f32[768,6,128]{0,2,1:T(8,128)} %get-tuple-element.1919, bf16[384,6,128]{0,2,1:T(8,128)(2,1)S(1)} %bitcast.450, f32[6,384,768]{2,1,0:T(8,128)} %copy-done.5, f32[768,6]{0,1:T(8,128)S(1)} %max.43, pred[768]{0:T(1024)(128)(4,1)S(1)} %broadcast_in_dim.643, f32[768,6]{0,1:T(8,128)S(1)} %get-tuple-element.1677), kind=kOutput, calls=%fused_computation.105.clone.1 | convolution fusion | flops 463011840 | bytes 12423936 | tf_op jit(solution)/shard_map/while/body/eval_jaxpr/qhk,khd->qhd/dot_general | solution.py:52
  394.1 7.1 %bitcast_add_fusion.23 = f32[768,6,128]{0,2,1:T(8,128)} fusion(f32[768,6,128]{0,2,1:T(8,128)} %get-tuple-element.1919, bf16[384,6,128]{0,2,1:T(8,128)(2,1)S(1)} %bitcast.450, f32[6,384,768]{2,1,0:T(8,128)} %copy-done.5, f32[768,6]{0,1:T(8,128)S(1)} %max.43, pred[768]{0:T(1024)(128)(4,1)S(1)} %broadcast_in_dim.643, f32[768,6]{0,1:T(8,128)S(1)} %get-tuple-element.1677), kind=kOutput, calls=%fused_computation.105.clone.1 | convolution fusion | flops 463011840 | bytes 12423936 | tf_op jit(solution)/shard_map/while/body/eval_jaxpr/qhk,khd->qhd/dot_general | solution.py:52
  404.4 29.8 %while.133 = (s32[]{:T(128)}, f32[768,6]{0,1:T(8,128)S(1)}, f32[768,6]{0,1:T(8,128)S(1)}, f32[768,6,128]{0,2,1:T(8,128)}, s32[2]{0:T(128)S(1)}, /*index=5*/s32[2...) while((s32[]{:T(128)}, f32[768,6]{0,1:T(8,128)S(1)}, ...), condition=%wide.region_39.40_spmd, body=%wide.region_35.39_spmd.sunk | while | flops 930161792 | bytes 61641584 | solution.py:64
  412.2 7.1 %bitcast_add_fusion.24 = f32[768,6,128]{0,2,1:T(8,128)} fusion(f32[768,6,128]{0,2,1:T(8,128)} %get-tuple-element.1949, bf16[384,6,128]{0,2,1:T(8,128)(2,1)S(1)} %bitcast.451, f32[6,384,768]{2,1,0:T(8,128)} %copy-done.6, f32[768,6]{0,1:T(8,128)S(1)} %max.44, pred[768]{0:T(1024)(128)(4,1)S(1)} %broadcast_in_dim.655, f32[768,6]{0,1:T(8,128)S(1)} %get-tuple-element.1692), kind=kOutput, calls=%fused_computation.124.clone.1 | convolution fusion | flops 463011840 | bytes 12423936 | tf_op jit(solution)/shard_map/while/body/eval_jaxpr/qhk,khd->qhd/dot_general | solution.py:52
  427.0 7.1 %bitcast_add_fusion.24 = f32[768,6,128]{0,2,1:T(8,128)} fusion(f32[768,6,128]{0,2,1:T(8,128)} %get-tuple-element.1949, bf16[384,6,128]{0,2,1:T(8,128)(2,1)S(1)} %bitcast.451, f32[6,384,768]{2,1,0:T(8,128)} %copy-done.6, f32[768,6]{0,1:T(8,128)S(1)} %max.44, pred[768]{0:T(1024)(128)(4,1)S(1)} %broadcast_in_dim.655, f32[768,6]{0,1:T(8,128)S(1)} %get-tuple-element.1692), kind=kOutput, calls=%fused_computation.124.clone.1 | convolution fusion | flops 463011840 | bytes 12423936 | tf_op jit(solution)/shard_map/while/body/eval_jaxpr/qhk,khd->qhd/dot_general | solution.py:52
  437.4 29.4 %while.134 = (s32[]{:T(128)}, f32[768,6]{0,1:T(8,128)S(1)}, f32[768,6]{0,1:T(8,128)S(1)}, f32[768,6,128]{0,2,1:T(8,128)}, s32[2]{0:T(128)S(1)}, /*index=5*/s32[2...) while((s32[]{:T(128)}, f32[768,6]{0,1:T(8,128)S(1)}, ...), condition=%wide.region_44.45_spmd, body=%wide.region_40.44_spmd.sunk | while | flops 930161792 | bytes 61641584 | solution.py:64
  444.9 7.1 %bitcast_add_fusion.25 = f32[768,6,128]{0,2,1:T(8,128)} fusion(f32[768,6,128]{0,2,1:T(8,128)} %get-tuple-element.1979, bf16[384,6,128]{0,2,1:T(8,128)(2,1)S(1)} %bitcast.452, f32[6,384,768]{2,1,0:T(8,128)} %copy-done.7, f32[768,6]{0,1:T(8,128)S(1)} %max.45, pred[768]{0:T(1024)(128)(4,1)S(1)} %broadcast_in_dim.667, f32[768,6]{0,1:T(8,128)S(1)} %get-tuple-element.1707), kind=kOutput, calls=%fused_computation.143.clone.1 | convolution fusion | flops 463011840 | bytes 12423936 | tf_op jit(solution)/shard_map/while/body/eval_jaxpr/qhk,khd->qhd/dot_general | solution.py:52
  459.6 7.1 %bitcast_add_fusion.25 = f32[768,6,128]{0,2,1:T(8,128)} fusion(f32[768,6,128]{0,2,1:T(8,128)} %get-tuple-element.1979, bf16[384,6,128]{0,2,1:T(8,128)(2,1)S(1)} %bitcast.452, f32[6,384,768]{2,1,0:T(8,128)} %copy-done.7, f32[768,6]{0,1:T(8,128)S(1)} %max.45, pred[768]{0:T(1024)(128)(4,1)S(1)} %broadcast_in_dim.667, f32[768,6]{0,1:T(8,128)S(1)} %get-tuple-element.1707), kind=kOutput, calls=%fused_computation.143.clone.1 | convolution fusion | flops 463011840 | bytes 12423936 | tf_op jit(solution)/shard_map/while/body/eval_jaxpr/qhk,khd->qhd/dot_general | solution.py:52
  471.4 7.8 %convolution_convert_fusion = bf16[768,3072]{1,0:T(8,128)(2,1)} fusion(bf16[768,768]{1,0:T(8,128)(2,1)S(1)} %bitcast.457, bf16[768,3072]{1,0:T(8,128)(2,1)} %param.27), kind=kOutput, calls=%fused_computation.174 | convolution fusion | flops 3626237952 | bytes 10616832 | tf_op jit(solution)/shard_map/dot_general | solution.py:102
  479.2 156.3 %reduce-scatter.2.cloned.1.call-done = bf16[192,3072]{1,0:T(8,128)(2,1)} async-done(((bf16[768,3072]{1,0:T(8,128)(2,1)}), bf16[192,3072]{1,0:T(8,128)(2,1)}) %reduce-scatter.2.cloned.1.call-update) | async-done | bytes 1179664 | tf_op jit(solution)/shard_map/reduce_scatter | solution.py:101
  (315 shorter events, 179.0 us)
Async XLA Ops:
  6.5 8.1 %copy-start.12 = (bf16[2,96,3072]{2,1,0:T(8,128)(2,1)S(1)}, bf16[2,96,3072]{2,1,0:T(8,128)(2,1)}, u32[]{:S(2)}) copy-start(bf16[2,96,3072]{2,1,0:T(8,128)(2,1)} %param.25) | copy-start | bytes 3538948
  11.1 23.6 %all-to-all-start = ((bf16[2,96,3072]{1,0,2:T(2,128)(2,1)}), bf16[2,96,3072]{1,0,2:T(2,128)(2,1)S(1)}, u32[]{:S(2)}, u32[]{:S(2)}) async-start(bf16[2,96,3072]{1,0,2:T(2,128)(2,1)} %copy.193), calls=%async_computation | async-start | bytes 3145728 | tf_op jit(solution)/shard_map/all_to_all | solution.py:19
  17.7 21.4 %copy-start.13 = (bf16[2,96,3072]{2,1,0:T(8,128)(2,1)S(1)}, bf16[2,96,3072]{2,1,0:T(8,128)(2,1)}, u32[]{:S(2)}) copy-start(bf16[2,96,3072]{2,1,0:T(8,128)(2,1)} %param.23) | copy-start | bytes 3538948
  34.7 24.5 %all-to-all-start.2 = ((bf16[2,96,3072]{1,0,2:T(2,128)(2,1)}), bf16[2,96,3072]{1,0,2:T(2,128)(2,1)}, u32[]{:S(2)}, u32[]{:S(2)}) async-start(bf16[2,96,3072]{1,0,2:T(2,128)(2,1)} %copy.198), calls=%async_computation.2 | async-start | bytes 3145728 | tf_op jit(solution)/shard_map/all_to_all | solution.py:20
  59.2 40.3 %all-to-all-start.1 = ((bf16[2,96,3072]{1,0,2:T(2,128)(2,1)}), bf16[2,96,3072]{1,0,2:T(2,128)(2,1)}, u32[]{:S(2)}, u32[]{:S(2)}) async-start(bf16[2,96,3072]{1,0,2:T(2,128)(2,1)} %copy.196), calls=%async_computation.1 | async-start | bytes 3145728 | tf_op jit(solution)/shard_map/all_to_all | solution.py:18
  63.6 571.9 %reduce-scatter.2.cloned.1.call-start = ((), (), s32[]{:S(2)}) async-start(), calls=%async_computation.4 | async-start | bytes 5898240 | tf_op jit(solution)/shard_map/reduce_scatter | solution.py:101
  72.8 1.0 copy-start.10
  75.5 93.3 %collective-permute-start = (bf16[2,2,384,768]{3,2,1,0:T(8,128)(2,1)}, bf16[2,2,384,768]{3,2,1,0:T(8,128)(2,1)}, u32[]{:S(2)}, u32[]{:S(2)}) collective-permute-start(bf16[2,2,384,768]{3,2,1,0:T(8,128)(2,1)} %pad_maximum_fusion), channel_id=1, source_target_pairs={{0,9},{1,10},{2,11},{3,12},{4,13},{5,14},{6,15},{7,16},{8,17},{9,1... | collective-permute-start | bytes 7077896 | tf_op jit(solution)/shard_map/ppermute | solution.py:13
  82.8 151.8 %collective-permute-start.1 = (bf16[2,2,384,768]{3,2,1,0:T(8,128)(2,1)}, bf16[2,2,384,768]{3,2,1,0:T(8,128)(2,1)}, u32[]{:S(2)}, u32[]{:S(2)}) collective-permute-start(bf16[2,2,384,768]{3,2,1,0:T(8,128)(2,1)} %pad_maximum_fusion), channel_id=1, source_target_pairs={{0,8},{1,9},{2,10},{3,11},{4,12},{5,13},{6,14},{7,15},{8,16},{9,17... | collective-permute-start | bytes 7077896 | tf_op jit(solution)/shard_map/ppermute | solution.py:13
  87.4 181.2 %collective-permute-start.2 = (bf16[2,2,384,768]{3,2,1,0:T(8,128)(2,1)}, bf16[2,2,384,768]{3,2,1,0:T(8,128)(2,1)}, u32[]{:S(2)}, u32[]{:S(2)}) collective-permute-start(bf16[2,2,384,768]{3,2,1,0:T(8,128)(2,1)} %pad_maximum_fusion), channel_id=1, source_target_pairs={{0,7},{1,8},{2,9},{3,10},{4,11},{5,12},{6,13},{7,14},{8,15},{9,16}... | collective-permute-start | bytes 7077896 | tf_op jit(solution)/shard_map/ppermute | solution.py:13
  93.6 209.3 %collective-permute-start.3 = (bf16[2,2,384,768]{3,2,1,0:T(8,128)(2,1)}, bf16[2,2,384,768]{3,2,1,0:T(8,128)(2,1)}, u32[]{:S(2)}, u32[]{:S(2)}) collective-permute-start(bf16[2,2,384,768]{3,2,1,0:T(8,128)(2,1)} %pad_maximum_fusion), channel_id=1, source_target_pairs={{0,1},{1,2},{2,3},{3,4},{4,5},{5,6},{6,7},{7,8},{8,9},{9,10},{10,1... | collective-permute-start | bytes 7077896 | tf_op jit(solution)/shard_map/ppermute | solution.py:13
  96.8 238.6 %collective-permute-start.4 = (bf16[2,2,384,768]{3,2,1,0:T(8,128)(2,1)}, bf16[2,2,384,768]{3,2,1,0:T(8,128)(2,1)}, u32[]{:S(2)}, u32[]{:S(2)}) collective-permute-start(bf16[2,2,384,768]{3,2,1,0:T(8,128)(2,1)} %pad_maximum_fusion), channel_id=1, source_target_pairs={{1,0},{2,1},{3,2},{4,3},{5,4},{6,5},{7,6},{8,7},{9,8},{10,9},{11,1... | collective-permute-start | bytes 7077896 | tf_op jit(solution)/shard_map/ppermute | solution.py:13
  99.5 7.4 %copy-start.11 = (s32[2,27]{1,0:T(2,128)S(1)}, s32[2,27]{1,0:T(2,128)}, u32[]{:S(2)}) copy-start(s32[2,27]{1,0:T(2,128)} %param.26) | copy-start | bytes 652
  106.9 1.5 copy-start.8
  119.2 6.6 %copy-start.9 = (bf16[2,384,768]{2,1,0:T(8,128)(2,1)S(1)}, bf16[2,384,768]{2,1,0:T(8,128)(2,1)}, u32[]{:S(2)}) copy-start(bf16[2,384,768]{2,1,0:T(8,128)(2,1)} %copy-done.8) | copy-start | bytes 3538948 | tf_op jit(solution)/shard_map/while
  125.8 1.5 copy-start.8
  138.0 7.3 %copy-start.9 = (bf16[2,384,768]{2,1,0:T(8,128)(2,1)S(1)}, bf16[2,384,768]{2,1,0:T(8,128)(2,1)}, u32[]{:S(2)}) copy-start(bf16[2,384,768]{2,1,0:T(8,128)(2,1)} %copy-done.8) | copy-start | bytes 3538948 | tf_op jit(solution)/shard_map/while
  168.8 199.5 %collective-permute-start.5 = (bf16[2,2,384,768]{3,2,1,0:T(8,128)(2,1)}, bf16[2,2,384,768]{3,2,1,0:T(8,128)(2,1)}, u32[]{:S(2)}, u32[]{:S(2)}) collective-permute-start(bf16[2,2,384,768]{3,2,1,0:T(8,128)(2,1)} %pad_maximum_fusion), channel_id=1, source_target_pairs={{7,0},{8,1},{9,2},{10,3},{11,4},{12,5},{13,6},{14,7},{15,8},{16,9}... | collective-permute-start | bytes 7077896 | tf_op jit(solution)/shard_map/ppermute | solution.py:13
  177.7 2.9 copy-start
  192.2 2.9 copy-start
  234.6 166.6 %collective-permute-start.6 = (bf16[2,2,384,768]{3,2,1,0:T(8,128)(2,1)}, bf16[2,2,384,768]{3,2,1,0:T(8,128)(2,1)}, u32[]{:S(2)}, u32[]{:S(2)}) collective-permute-start(bf16[2,2,384,768]{3,2,1,0:T(8,128)(2,1)} %pad_maximum_fusion), channel_id=1, source_target_pairs={{8,0},{9,1},{10,2},{11,3},{12,4},{13,5},{14,6},{15,7},{16,8},{17,9... | collective-permute-start | bytes 7077896 | tf_op jit(solution)/shard_map/ppermute | solution.py:13
  243.5 2.9 copy-start.1
  258.2 2.9 copy-start.1
  268.6 4.7 copy-start.19
  268.6 165.6 %collective-permute-start.7 = (bf16[2,2,384,768]{3,2,1,0:T(8,128)(2,1)}, bf16[2,2,384,768]{3,2,1,0:T(8,128)(2,1)}, u32[]{:S(2)}, u32[]{:S(2)}) collective-permute-start(bf16[2,2,384,768]{3,2,1,0:T(8,128)(2,1)} %pad_maximum_fusion), channel_id=1, source_target_pairs={{9,0},{10,1},{11,2},{12,3},{13,4},{14,5},{15,6},{16,7},{17,8},{18,... | collective-permute-start | bytes 7077896 | tf_op jit(solution)/shard_map/ppermute | solution.py:13
  277.7 2.9 copy-start.2
  292.5 2.9 copy-start.2
  302.9 3.2 copy-start.18
  310.4 2.9 copy-start.3
  325.0 2.9 copy-start.3
  335.3 3.2 copy-start.17
  343.3 2.9 copy-start.4
  358.0 2.9 copy-start.4
  368.4 3.2 copy-start.16
  376.0 2.9 copy-start.5
  390.8 2.9 copy-start.5
  401.2 3.2 copy-start.15
  409.0 2.9 copy-start.6
  423.8 2.9 copy-start.6
  434.2 3.2 copy-start.14
  441.7 2.9 copy-start.7
  456.4 2.9 copy-start.7
Sparse Core Ops, SparseCore 0:
  479.3 156.1 reduce-scatter.1
where the time goes:
time: 652 us; the launch traced here: 642 us
  waiting for transfers between devices  246 us (38%)
  matrix products  164 us (25%)
  local copies, waits for them, and re-layouts  121 us (19%)
  other arithmetic  55.8 us (9%)
  starting transfers between devices  40.5 us (6%)
  between operations  14 us (2%)
    reduce_scatter x1, waiting for transfers between devices, on_device(): lax.psum_scatter(jnp.dot(arranged, w_out, preferred_element_type=jnp.floa...  156 us
    dot_general x18, matrix products, tile_step(): jnp.einsum('qhk,khd->qhd', weights.astype(jnp.bfloat16), value_tile.resha...  128 us
    ppermute x8, waiting for transfers between devices, from_behind(): return lax.ppermute(block, axis, route)  55.5 us
    dynamic_slice x72, local copies, waits for them, and re-layouts, absorb(): lax.scan(tile_step, running, (kv_block[0], kv_block[1], tile_ids))  46.1 us
    reduce_sum x18, other arithmetic, tile_step(): row_sum = row_sum * factor + jnp.sum(weights, axis=2)  35.4 us
    ppermute x8, starting transfers between devices, from_behind(): return lax.ppermute(block, axis, route)  28.2 us
    dot_general x18, matrix products, tile_step(): jnp.einsum('qhd,khd->qhk', query_rows, key_tile.reshape(tile_rows, heads_...  28.2 us
    squeeze x8, local copies, waits for them, and re-layouts, absorb(): kv_block[1]  25.5 us
  transfers between devices with their start and end apart: 12, of which 5 were waited for; matrix products, arithmetic and copies ran while one was open for 42% of the time, Pallas kernels for 0%

commit v1 on v0

v1 whole, which is shorter than its diff:
```python
import functools

import jax
import jax.numpy as jnp
from jax import lax
from jax.experimental import pallas as pl
from jax.experimental.pallas import tpu as pltpu
from jax.sharding import Mesh, PartitionSpec as P

HEAD_DIM = 128
HEADS = 24
GROUPS = 8
GROUP_HEADS = HEADS // GROUPS
ROWS = 4
COLUMNS = 8
TIMES = 2
PART = 96
D = HEADS * HEAD_DIM
NEIGH = 27
COEF = HEAD_DIM ** (-0.5) * 1.4426950408889634
LOW = -1e30
CHUNKS = ((0, 1, 2),)

AXES = ("yl", "c", "yh", "zh", "zl", "x")
SIZES = (2, 2, 2, 2, 2, 4)
COLUMN_AXES = ("yh", "zh", "yl")


def places():
    for flat in range(128):
        left, coords = flat, []
        for size in reversed(SIZES):
            coords.append(left % size)
            left //= size
        yield flat, tuple(reversed(coords))


def flat_of(coords):
    flat = 0
    for coord, size in zip(coords, SIZES):
        flat = flat * size + coord
    return flat


def route(target):
    pairs = []
    for flat, coords in places():
        to = target(*coords)
        if to is not None:
            pairs.append((flat, flat_of(to)))
    return pairs


def column_step(step):
    def target(yl, c, yh, zh, zl, x):
        column = zl * 4 + x + step
        if not 0 <= column < COLUMNS:
            return None
        return (yl, c, yh, zh, column // 4, column % 4)

    return target


def y_step(step):
    def target(yl, c, yh, zh, zl, x):
        y = (yh * 2 + yl + step) % 4
        return (y % 2, c, y // 2, zh, zl, x)

    return target


RIGHT = route(column_step(1))
LEFT = route(column_step(-1))
UP = route(y_step(1))
DOWN = route(y_step(-1))
OTHER_CORE = route(lambda yl, c, yh, zh, zl, x: (yl, 1 - c, yh, zh, zl, x))


def permute(array, pairs):
    return lax.ppermute(array, AXES, pairs)


def exchange(array):
    return lax.all_to_all(array, COLUMN_AXES, 0, 0)


def arrange_kernel(q_ref, k_ref, v_ref, *out_refs):
    for at, chunk in enumerate(CHUNKS):
        q_out, kv_out = out_refs[2 * at], out_refs[2 * at + 1]
        lanes = pl.ds(chunk[0] * HEAD_DIM, len(chunk) * HEAD_DIM)
        q_out[0] = q_ref[:, :, lanes]
        kv_out[0, 0] = k_ref[:, :, lanes]
        kv_out[0, 1] = v_ref[:, :, lanes]


def arrange(queries, keys, values):
    shapes, specs = [], []
    for chunk in CHUNKS:
        width = len(chunk) * HEAD_DIM
        shapes.append(jax.ShapeDtypeStruct((GROUPS, TIMES, PART, width), jnp.bfloat16))
        specs.append(pl.BlockSpec((1, TIMES, PART, width), lambda g: (g, 0, 0, 0)))
        shapes.append(jax.ShapeDtypeStruct((GROUPS, 2, TIMES, PART, width), jnp.bfloat16))
        specs.append(pl.BlockSpec((1, 2, TIMES, PART, width), lambda g: (g, 0, 0, 0, 0)))
    block = pl.BlockSpec((TIMES, PART, GROUP_HEADS * HEAD_DIM), lambda g: (0, 0, g))
    return pl.pallas_call(
        arrange_kernel,
        grid=(GROUPS,),
        in_specs=[block] * 3,
        out_specs=specs,
        out_shape=shapes,
        name="arrange",
    )(queries, keys, values)


def attend_kernel(lists, q_ref, *refs):
    kv_refs, o_ref = refs[:6], refs[6]
    m_ref, l_ref, acc_ref = refs[7:]
    row = pl.program_id(1)
    half = 2 * PART
    q = jnp.concatenate([q_ref[:, t].reshape(half, HEAD_DIM) for t in range(TIMES)], axis=0)
    m_ref[...] = jnp.full(m_ref.shape, LOW, jnp.float32)
    l_ref[...] = jnp.zeros(l_ref.shape, jnp.float32)
    acc_ref[...] = jnp.zeros(acc_ref.shape, jnp.float32)

    def flag(t, t2, row_step, column_step):
        entry = (t2 - t + 1) * 9 + (row_step + 1) * 3 + column_step + 1
        return lists[(row * TIMES + t) * NEIGH + entry] >= 0

    for column in (0, -1, 1):
        own, other = kv_refs[2 * (column % 3)], kv_refs[2 * (column % 3) + 1]

        def step(index, carry, own=own, other=other, column=column):
            row_step = index - 1
            key_row = row + row_step
            flags = [[flag(t, t2, row_step, column) for t in range(TIMES)] for t2 in range(TIMES)]
            some = flags[0][0] | flags[0][1] | flags[1][0] | flags[1][1]

            @pl.when((key_row >= 0) & (key_row < ROWS) & some)
            def _():
                at = pl.ds(2 * key_row, 2)

                def tile(which, t2):
                    return [own[at, which, t2].reshape(half, HEAD_DIM), other[at, which, t2].reshape(half, HEAD_DIM)]

                k = jnp.concatenate(tile(0, 0) + tile(0, 1), axis=0)
                v = jnp.concatenate(tile(1, 0) + tile(1, 1), axis=0)
                s = lax.dot_general(q, k, (((1,), (1,)), ((), ())), preferred_element_type=jnp.float32)
                keys = 4 * PART
                m_old = m_ref[...]
                tops, shifts = [], []
                for t in range(TIMES):
                    best = m_old[t * half : (t + 1) * half, :1]
                    for t2 in range(TIMES):
                        part = s[t * half : (t + 1) * half, t2 * keys : (t2 + 1) * keys]
                        top = jnp.max(part, axis=1, keepdims=True)
                        best = jnp.maximum(best, jnp.where(flags[t2][t], top, LOW))
                    tops.append(best)
                m_new = jnp.concatenate(tops, axis=0)
                probs = []
                for t2 in range(TIMES):
                    shift = jnp.concatenate(
                        [jnp.where(flags[t2][t], tops[t] * COEF, -LOW) for t in range(TIMES)], axis=0
                    )
                    probs.append(jnp.exp2(s[:, t2 * keys : (t2 + 1) * keys] * COEF - shift))
                p = jnp.concatenate(probs, axis=1)
                factor = jnp.exp2((m_old - m_new) * COEF)
                total = p[:, :HEAD_DIM]
                for lane in range(1, p.shape[1] // HEAD_DIM):
                    total = total + p[:, lane * HEAD_DIM : (lane + 1) * HEAD_DIM]
                l_ref[...] = l_ref[...] * factor + total
                update = jnp.dot(p.astype(jnp.bfloat16), v, preferred_element_type=jnp.float32)
                acc_ref[...] = acc_ref[...] * factor + update
                m_ref[...] = jnp.broadcast_to(m_new, m_ref.shape)

            return carry

        lax.fori_loop(0, 3, step, 0)
    row_sum = jnp.sum(l_ref[...], axis=1, keepdims=True)
    out = (acc_ref[...] / row_sum).astype(jnp.bfloat16)
    for t in range(TIMES):
        o_ref[:, t] = out[t * half : (t + 1) * half].reshape(2, PART, HEAD_DIM)


def attend(lists, q, blocks):
    heads = q.shape[-1] // HEAD_DIM
    q_spec = pl.BlockSpec((2, TIMES, PART, HEAD_DIM), lambda h, r, s: (r, 0, 0, h))
    kv_spec = pl.BlockSpec((GROUPS, 2, TIMES, PART, HEAD_DIM), lambda h, r, s: (0, 0, 0, 0, h))
    tile_rows = 4 * PART
    return pl.pallas_call(
        attend_kernel,
        grid_spec=pltpu.PrefetchScalarGridSpec(
            num_scalar_prefetch=1,
            grid=(heads, ROWS),
            in_specs=[q_spec] + [kv_spec] * 6,
            out_specs=q_spec,
            scratch_shapes=[pltpu.VMEM((tile_rows, HEAD_DIM), jnp.float32)] * 3,
        ),
        out_shape=jax.ShapeDtypeStruct(q.shape, jnp.bfloat16),
        compiler_params=pltpu.CompilerParams(vmem_limit_bytes=40 * 1024 * 1024),
        cost_estimate=pl.CostEstimate(
            flops=heads * 30 * 384 * 768 * 128 * 4,
            bytes_accessed=heads * 6 * 786432,
            transcendentals=heads * 30 * 384 * 768,
        ),
        name="attend",
    )(lists, q, *blocks)


def project_kernel(ids, *refs):
    att_refs = refs[: len(CHUNKS)]
    w_refs, o_ref = refs[len(CHUNKS) : -1], refs[-1]
    total = None
    for shard in range(4):
        for part in range(2):
            group = ids[shard] * 2 + part
            rows = jnp.concatenate(
                [ref[group].reshape(TIMES * PART, ref.shape[-1]) for ref in att_refs], axis=1
            )
            w = w_refs[2 * shard + part][...]
            term = jnp.dot(rows, w, preferred_element_type=jnp.float32)
            total = term if total is None else total + term
    o_ref[...] = total.astype(jnp.bfloat16).reshape(TIMES, PART, total.shape[1])


def project(ids, parts, w_own, w_other, w_above, w_below, w_above_other, w_below_other):
    block = 512
    group_rows = D // GROUPS
    specs = []
    for part in parts:
        specs.append(pl.BlockSpec(part.shape, lambda n, s: (0, 0, 0, 0)))
    first = pl.BlockSpec((group_rows, block), lambda n, s: (0, n))
    second = pl.BlockSpec((group_rows, block), lambda n, s: (1, n))
    specs += [first, second, first, second, first, first, first, first]
    return pl.pallas_call(
        project_kernel,
        grid_spec=pltpu.PrefetchScalarGridSpec(
            num_scalar_prefetch=1,
            grid=(D // block,),
            in_specs=specs,
            out_specs=pl.BlockSpec((TIMES, PART, block), lambda n, s: (0, 0, n)),
        ),
        out_shape=jax.ShapeDtypeStruct((TIMES, PART, D), jnp.bfloat16),
        compiler_params=pltpu.CompilerParams(vmem_limit_bytes=40 * 1024 * 1024),
        cost_estimate=pl.CostEstimate(
            flops=2 * TIMES * PART * D * D, bytes_accessed=2 * D * D, transcendentals=0
        ),
        name="project",
    )(ids, *parts, w_own, w_own, w_other, w_other, w_above, w_below, w_above_other, w_below_other)


def on_device(queries, keys, values, neighbours, w_out):
    lists = lax.all_gather(neighbours, ("yh", "zh")).reshape(-1)
    arranged = arrange(queries, keys, values)
    results = []
    half = w_out.shape[0] // 2
    w_above = permute(w_out[:half], DOWN)
    w_below = permute(w_out[half:], UP)
    w_other = permute(w_out, OTHER_CORE)
    w_above_other = permute(w_above, OTHER_CORE)
    w_below_other = permute(w_below, OTHER_CORE)
    for at in range(len(CHUNKS)):
        kv = exchange(arranged[2 * at + 1])
        from_left = permute(kv, RIGHT)
        from_right = permute(kv, LEFT)
        q = exchange(arranged[2 * at])
        blocks = []
        for block in (kv, from_right, from_left):
            blocks += [block, permute(block, OTHER_CORE)]
        results.append(exchange(attend(lists, q, blocks)))
    yl, c = lax.axis_index("yl"), lax.axis_index("c")
    ids = jnp.stack([2 * yl + c, 2 * yl + 1 - c, 2 * (1 - yl) + c, 2 * (1 - yl) + 1 - c]).astype(jnp.int32)
    return project(ids, results, w_out, w_other, w_above, w_below, w_above_other, w_below_other)


def solution(mesh):
    fine = Mesh(mesh.devices.reshape(SIZES), AXES)
    tile, head = ("yh", "zh", "zl", "x"), ("yl", "c")
    placed = (
        P(tile, head, None),
        P(tile, head, None),
        P(tile, head, None),
        P(tile, None),
        P(head, None),
    )
    return jax.shard_map(
        on_device, mesh=fine, in_specs=placed, out_specs=P(tile, head, None), check_vma=False
    )
```

time: 652 us -> 261 us (0.40); the launches traced: 642 us -> 259 us
  matrix products: 164 us -> 0 us
  waiting for transfers between devices: 246 us -> 99.7 us
  local copies, waits for them, and re-layouts: 121 us -> 5.97 us
  Pallas kernels: 0 us -> 103 us
  other arithmetic: 55.8 us -> 0.08 us
  blocking collectives: 0 us -> 22.9 us
  between operations: 14 us -> 0.09 us
  starting transfers between devices: 40.5 us -> 26.8 us
    dot_general x37 -> x0, matrix products: 164 us -> none  [the longest x18 128 us: tile_step(): jnp.einsum('qhk,khd->qhd', weights.astype(jnp.bfloat16), value_tile.resha...]
    reduce_scatter x1 -> x0, waiting for transfers between devices: 156 us -> none  [on_device(): lax.psum_scatter(jnp.dot(arranged, w_out, preferred_element_type=jnp.floa...]
    pallas_call x0 -> x3, Pallas kernels: none -> 103 us  [the longest x1 85.8 us: attend(): pl.pallas_call(attend_kernel, grid_spec=pltpu.PrefetchScalarGridSpec(num_...]
    dynamic_slice x72 -> x0, local copies, waits for them, and re-layouts: 46.1 us -> none  [absorb(): lax.scan(tile_step, running, (kv_block[0], kv_block[1], tile_ids))]
    reduce_sum x18 -> x0, other arithmetic: 35.4 us -> none  [tile_step(): row_sum = row_sum * factor + jnp.sum(weights, axis=2)]
    squeeze x8 -> x0, local copies, waits for them, and re-layouts: 25.5 us -> none  [absorb(): kv_block[1]]
    all_gather x0 -> x1, blocking collectives: none -> 22.9 us  [on_device(): lists = lax.all_gather(neighbours, ('yh', 'zh')).reshape(-1)]
    while x58 -> x0, local copies, waits for them, and re-layouts: 20.1 us -> none
  transfers between devices with their start and end apart: 12 -> 13, of which waited for: 5 -> 5; matrix products, arithmetic and copies ran while one was open for 42% -> 2% of each run, Pallas kernels for 0% -> 33%
where the time goes in v1:
time: 261 us; the launch traced here: 259 us
  Pallas kernels  103 us (39%)
  waiting for transfers between devices  99.7 us (38%)
  starting transfers between devices  26.8 us (10%)
  blocking collectives  22.9 us (9%)
  local copies, waits for them, and re-layouts  5.97 us (2%)
    pallas_call x1, Pallas kernels, attend(): pl.pallas_call(attend_kernel, grid_spec=pltpu.PrefetchScalarGridSpec(num_...  85.8 us
    ppermute x10, waiting for transfers between devices, permute(): return lax.ppermute(array, AXES, pairs)  51.7 us
    all_to_all x3, waiting for transfers between devices, exchange(): return lax.all_to_all(array, COLUMN_AXES, 0, 0)  48 us
    all_gather x1, blocking collectives, on_device(): lists = lax.all_gather(neighbours, ('yh', 'zh')).reshape(-1)  22.9 us
    all_to_all x3, starting transfers between devices, exchange(): return lax.all_to_all(array, COLUMN_AXES, 0, 0)  18.2 us
    pallas_call x1, Pallas kernels, project(): pl.pallas_call(project_kernel, grid_spec=pltpu.PrefetchScalarGridSpec(num...  10.9 us
    ppermute x10, starting transfers between devices, permute(): return lax.ppermute(array, AXES, pairs)  8.61 us
    pallas_call x1, Pallas kernels, arrange(): pl.pallas_call(arrange_kernel, grid=(GROUPS,), in_specs=[block] * 3, out_...  6.43 us
  transfers between devices with their start and end apart: 13, of which 5 were waited for; matrix products, arithmetic and copies ran while one was open for 2% of the time, Pallas kernels for 33%

profile of v1, /device:TPU:6, one launch (start us, length us, event | category | flops | bytes accessed | tf_op | source)
XLA Modules:
  0.0 258.7 jit_solution(17976678326949269714)
XLA Ops:
  0.0 6.4 %arrange.1 = (bf16[8,2,96,384]{3,2,1,0:T(8,128)(2,1)}, bf16[8,2,2,96,384]{4,3,2,1,0:T(8,128)(2,1)}) custom-call(bf16[2,96,3072]{2,1,0:T(8,128)(2,1)} %q_ref.1, bf16[2,96,3072]{2,1,0:T(8,128)(2,1)} %k_ref.1, bf16[2,96,3072]{2,1,0:T(8,128)(2,1)} %v_ref.1), custom_call_target="tpu_custom_call" | custom-call | tf_op jit(solution)/shard_map/arrange/pallas_call | solution.py:105
  6.4 7.8 %all-to-all-start.1 = ((bf16[8,2,2,96,384]{4,3,2,1,0:T(8,128)(2,1)}), bf16[8,2,2,96,384]{4,3,2,1,0:T(8,128)(2,1)}, u32[]{:S(2)}, u32[]{:S(2)}) async-start(bf16[8,2,2,96,384]{4,3,2,1,0:T(8,128)(2,1)} %get-tuple-element.8), calls=%async_computation.1 | async-start | bytes 4718592 | tf_op jit(solution)/shard_map/all_to_all | solution.py:84
  14.2 4.9 %fusion = (bf16[384,3072]{1,0:T(8,128)(2,1)}, bf16[384,3072]{1,0:T(8,128)(2,1)}) fusion(bf16[768,3072]{1,0:T(8,128)(2,1)} %refs_2_.1), kind=kLoop, calls=%fused_computation.1 | loop fusion | bytes 9437184 | tf_op jit(solution)/shard_map/slice | solution.py:257
  19.1 0.0 copy-start.1
  19.1 2.0 collective-permute-start.7
  21.1 31.7 %all-to-all-done.1.refs_0_ = bf16[8,2,2,96,384]{4,3,2,1,0:T(8,128)(2,1)} async-done(((bf16[8,2,2,96,384]{4,3,2,1,0:T(8,128)(2,1)}), bf16[8,2,2,96,384]{4,3,2,1,0:T(8,128)(2,1)}, u32[]{:S(2)}, u32[]{:S(2)}) %all-to-all-start.1) | async-done | bytes 2359328 | tf_op jit(solution)/shard_map/all_to_all | solution.py:84
  52.8 2.8 %collective-permute-start.3 = (bf16[8,2,2,96,384]{4,3,2,1,0:T(8,128)(2,1)}, bf16[8,2,2,96,384]{4,3,2,1,0:T(8,128)(2,1)}, u32[]{:S(2)}, u32[]{:S(2)}) collective-permute-start(bf16[8,2,2,96,384]{4,3,2,1,0:T(8,128)(2,1)} %all-to-all-done.1.refs_0_), channel_id=1, source_target_pairs={{0,1},{1,2},{2,3},{3,4},{4,5},{5,6},{6,7},{8,9},{9,10},{10,11},{11... | collective-permute-start | bytes 7077896 | tf_op jit(solution)/shard_map/ppermute | solution.py:80
  55.7 3.0 %collective-permute-start.1 = (bf16[8,2,2,96,384]{4,3,2,1,0:T(8,128)(2,1)}, bf16[8,2,2,96,384]{4,3,2,1,0:T(8,128)(2,1)}, u32[]{:S(2)}, u32[]{:S(2)}) collective-permute-start(bf16[8,2,2,96,384]{4,3,2,1,0:T(8,128)(2,1)} %all-to-all-done.1.refs_0_), channel_id=1, source_target_pairs={{1,0},{2,1},{3,2},{4,3},{5,4},{6,5},{7,6},{9,8},{10,9},{11,10},{12... | collective-permute-start | bytes 7077896 | tf_op jit(solution)/shard_map/ppermute | solution.py:80
  58.7 0.1 collective-permute-start.6
  58.8 0.1 collective-permute-start
  58.9 37.1 %collective-permute-done.7.refs_6_ = bf16[384,3072]{1,0:T(8,128)(2,1)S(1)} collective-permute-done((bf16[384,3072]{1,0:T(8,128)(2,1)}, bf16[384,3072]{1,0:T(8,128)(2,1)S(1)}, u32[]{:S(2)}, u32[]{:S(2)}) %collective-permute-start.7) | collective-permute-done | bytes 2359328 | tf_op jit(solution)/shard_map/ppermute | solution.py:80
  96.0 0.0 collective-permute-start.5
  96.0 9.9 %collective-permute-done.3.refs_4_ = bf16[8,2,2,96,384]{4,3,2,1,0:T(8,128)(2,1)} collective-permute-done((bf16[8,2,2,96,384]{4,3,2,1,0:T(8,128)(2,1)}, bf16[8,2,2,96,384]{4,3,2,1,0:T(8,128)(2,1)}, u32[]{:S(2)}, u32[]{:S(2)}) %collective-permute-start.3) | collective-permute-done | bytes 2359328 | tf_op jit(solution)/shard_map/ppermute | solution.py:80
  105.9 0.0 collective-permute-start.4
  105.9 4.7 %collective-permute-done.1.refs_2_ = bf16[8,2,2,96,384]{4,3,2,1,0:T(8,128)(2,1)} collective-permute-done((bf16[8,2,2,96,384]{4,3,2,1,0:T(8,128)(2,1)}, bf16[8,2,2,96,384]{4,3,2,1,0:T(8,128)(2,1)}, u32[]{:S(2)}, u32[]{:S(2)}) %collective-permute-start.1) | collective-permute-done | bytes 2359328 | tf_op jit(solution)/shard_map/ppermute | solution.py:80
  110.5 0.0 collective-permute-start.2
  110.5 4.8 %all-to-all-start = ((bf16[8,2,96,384]{3,2,1,0:T(8,128)(2,1)}), bf16[8,2,96,384]{3,2,1,0:T(8,128)(2,1)S(1)}, u32[]{:S(2)}, u32[]{:S(2)}) async-start(bf16[8,2,96,384]{3,2,1,0:T(8,128)(2,1)} %get-tuple-element.7), calls=%async_computation | async-start | bytes 2359296 | tf_op jit(solution)/shard_map/all_to_all | solution.py:84
  115.4 0.0 collective-permute-done.6.refs_5_
  115.4 0.3 collective-permute-start.9
  115.7 0.0 collective-permute-done.refs_1_
  115.7 0.3 collective-permute-start.8
  116.0 0.0 copy-done.1
  116.0 22.9 %all-gather.1 = s32[4,2,27]{2,1,0:T(2,128)S(1)} all-gather(s32[1,2,27]{2,1,0:T(2,128)S(1)} %bitcast.5), channel_id=2, replica_groups=mesh['yl'=2,'c'=2,'yh'=2,'zh'=2,'zl'=2,'x'=4] {'yh','zh'}, dimensions={0}, use_global_device_ids=true | all-gather | bytes 1080 | tf_op jit(solution)/shard_map/all_gather | solution.py:252
  138.9 0.1 reshape.3.lists
  139.0 0.0 all-to-all-done.q_ref
  139.0 0.0 collective-permute-done.4.refs_5_
  139.0 0.0 collective-permute-done.2.refs_3_
  139.0 85.8 %attend.1 = bf16[8,2,96,384]{3,2,1,0:T(8,128)(2,1)S(1)} custom-call(s32[216]{0:T(256)S(1)} %reshape.3.lists, bf16[8,2,96,384]{3,2,1,0:T(8,128)(2,1)S(1)} %all-to-all-done.q_ref, bf16[8,2,2,96,384]{4,3,2,1,0:T(8,128)(2,1)} %all-to-all-done.1.refs_0_, bf16[8,2,2,96,384]{4,3,2,1,0:T(8,128)(2,1)} %collective-permute-done.refs_1_, ...), custom_call_target="tpu_custom_call" | custom-call | flops 13589544960 | bytes 14155776 | tf_op jit(solution)/shard_map/attend/pallas_call | solution.py:189
  224.8 0.0 copy-start
  224.9 1.0 copy-done
  225.9 5.6 %all-to-all-start.2 = ((bf16[8,2,96,384]{3,2,1,0:T(8,128)(2,1)}), bf16[8,2,96,384]{3,2,1,0:T(8,128)(2,1)S(1)}, u32[]{:S(2)}, u32[]{:S(2)}) async-start(bf16[8,2,96,384]{3,2,1,0:T(8,128)(2,1)} %copy-done), calls=%async_computation.2 | async-start | bytes 2359296 | tf_op jit(solution)/shard_map/all_to_all | solution.py:84
  231.5 0.1 pad_add_fusion.ids
  231.5 0.0 collective-permute-done.9.refs_8_
  231.5 0.0 collective-permute-done.8.refs_7_
  231.5 0.0 collective-permute-done.5.refs_3_.refs_4_
  231.6 16.2 %all-to-all-done.2.refs_0_ = bf16[8,2,96,384]{3,2,1,0:T(8,128)(2,1)S(1)} async-done(((bf16[8,2,96,384]{3,2,1,0:T(8,128)(2,1)}), bf16[8,2,96,384]{3,2,1,0:T(8,128)(2,1)S(1)}, u32[]{:S(2)}, u32[]{:S(2)}) %all-to-all-start.2) | async-done | bytes 1179680 | tf_op jit(solution)/shard_map/all_to_all | solution.py:84
  247.8 10.9 %project.1 = bf16[2,96,3072]{2,1,0:T(8,128)(2,1)} custom-call(s32[4]{0:T(128)S(1)} %pad_add_fusion.ids, bf16[8,2,96,384]{3,2,1,0:T(8,128)(2,1)S(1)} %all-to-all-done.2.refs_0_, bf16[768,3072]{1,0:T(8,128)(2,1)} %refs_2_.1, bf16[768,3072]{1,0:T(8,128)(2,1)} %refs_2_.1, bf16[768,3072]{1,0:T(8,128)(2,1)} %collective-permute-done.5.refs_3_.refs_4_, ...), custom_call_target="tpu_custom_call" | custom-call | flops 3623878656 | bytes 18874368 | tf_op jit(solution)/shard_map/project/pallas_call | solution.py:234
Async XLA Ops:
  6.4 46.4 %all-to-all-start.1 = ((bf16[8,2,2,96,384]{4,3,2,1,0:T(8,128)(2,1)}), bf16[8,2,2,96,384]{4,3,2,1,0:T(8,128)(2,1)}, u32[]{:S(2)}, u32[]{:S(2)}) async-start(bf16[8,2,2,96,384]{4,3,2,1,0:T(8,128)(2,1)} %get-tuple-element.8), calls=%async_computation.1 | async-start | bytes 4718592 | tf_op jit(solution)/shard_map/all_to_all | solution.py:84
  19.1 96.9 %copy-start.1 = (s32[2,27]{1,0:T(2,128)S(1)}, s32[2,27]{1,0:T(2,128)}, u32[]{:S(2)}) copy-start(s32[2,27]{1,0:T(2,128)} %param.8) | copy-start | bytes 652
  19.1 76.9 %collective-permute-start.7 = (bf16[384,3072]{1,0:T(8,128)(2,1)}, bf16[384,3072]{1,0:T(8,128)(2,1)S(1)}, u32[]{:S(2)}, u32[]{:S(2)}) collective-permute-start(bf16[384,3072]{1,0:T(8,128)(2,1)} %get-tuple-element.9), channel_id=1, source_target_pairs={{0,64},{1,65},{2,66},{3,67},{4,68},{5,69},{6,70},{7,71},{8,72},{9,... | collective-permute-start | bytes 7077896 | tf_op jit(solution)/shard_map/ppermute | solution.py:80
  52.8 53.0 %collective-permute-start.3 = (bf16[8,2,2,96,384]{4,3,2,1,0:T(8,128)(2,1)}, bf16[8,2,2,96,384]{4,3,2,1,0:T(8,128)(2,1)}, u32[]{:S(2)}, u32[]{:S(2)}) collective-permute-start(bf16[8,2,2,96,384]{4,3,2,1,0:T(8,128)(2,1)} %all-to-all-done.1.refs_0_), channel_id=1, source_target_pairs={{0,1},{1,2},{2,3},{3,4},{4,5},{5,6},{6,7},{8,9},{9,10},{10,11},{11... | collective-permute-start | bytes 7077896 | tf_op jit(solution)/shard_map/ppermute | solution.py:80
  55.7 54.9 %collective-permute-start.1 = (bf16[8,2,2,96,384]{4,3,2,1,0:T(8,128)(2,1)}, bf16[8,2,2,96,384]{4,3,2,1,0:T(8,128)(2,1)}, u32[]{:S(2)}, u32[]{:S(2)}) collective-permute-start(bf16[8,2,2,96,384]{4,3,2,1,0:T(8,128)(2,1)} %all-to-all-done.1.refs_0_), channel_id=1, source_target_pairs={{1,0},{2,1},{3,2},{4,3},{5,4},{6,5},{7,6},{9,8},{10,9},{11,10},{12... | collective-permute-start | bytes 7077896 | tf_op jit(solution)/shard_map/ppermute | solution.py:80
  58.7 56.7 %collective-permute-start.6 = (bf16[384,3072]{1,0:T(8,128)(2,1)}, bf16[384,3072]{1,0:T(8,128)(2,1)}, u32[]{:S(2)}, u32[]{:S(2)}) collective-permute-start(bf16[384,3072]{1,0:T(8,128)(2,1)} %get-tuple-element.10), channel_id=1, source_target_pairs={{0,80},{1,81},{2,82},{3,83},{4,84},{5,85},{6,86},{7,87},{8,88},{9,... | collective-permute-start | bytes 7077896 | tf_op jit(solution)/shard_map/ppermute | solution.py:80
  58.8 56.9 %collective-permute-start = (bf16[8,2,2,96,384]{4,3,2,1,0:T(8,128)(2,1)}, bf16[8,2,2,96,384]{4,3,2,1,0:T(8,128)(2,1)}, u32[]{:S(2)}, u32[]{:S(2)}) collective-permute-start(bf16[8,2,2,96,384]{4,3,2,1,0:T(8,128)(2,1)} %all-to-all-done.1.refs_0_), channel_id=1, source_target_pairs={{0,32},{1,33},{2,34},{3,35},{4,36},{5,37},{6,38},{7,39},{8,40},{9,... | collective-permute-start | bytes 7077896 | tf_op jit(solution)/shard_map/ppermute | solution.py:80
  96.0 135.5 %collective-permute-start.5 = (bf16[768,3072]{1,0:T(8,128)(2,1)}, bf16[768,3072]{1,0:T(8,128)(2,1)}, u32[]{:S(2)}, u32[]{:S(2)}) collective-permute-start(bf16[768,3072]{1,0:T(8,128)(2,1)} %refs_2_.1), channel_id=1, source_target_pairs={{0,32},{1,33},{2,34},{3,35},{4,36},{5,37},{6,38},{7,39},{8,40},{9,... | collective-permute-start | bytes 14155784 | tf_op jit(solution)/shard_map/ppermute | solution.py:80
  105.9 33.1 %collective-permute-start.4 = (bf16[8,2,2,96,384]{4,3,2,1,0:T(8,128)(2,1)}, bf16[8,2,2,96,384]{4,3,2,1,0:T(8,128)(2,1)}, u32[]{:S(2)}, u32[]{:S(2)}) collective-permute-start(bf16[8,2,2,96,384]{4,3,2,1,0:T(8,128)(2,1)} %collective-permute-done.3.refs_4_), channel_id=1, source_target_pairs={{0,32},{1,33},{2,34},{3,35},{4,36},{5,37},{6,38},{7,39},{8,40},{9,... | collective-permute-start | bytes 7077896 | tf_op jit(solution)/shard_map/ppermute | solution.py:80
  110.5 28.4 %collective-permute-start.2 = (bf16[8,2,2,96,384]{4,3,2,1,0:T(8,128)(2,1)}, bf16[8,2,2,96,384]{4,3,2,1,0:T(8,128)(2,1)}, u32[]{:S(2)}, u32[]{:S(2)}) collective-permute-start(bf16[8,2,2,96,384]{4,3,2,1,0:T(8,128)(2,1)} %collective-permute-done.1.refs_2_), channel_id=1, source_target_pairs={{0,32},{1,33},{2,34},{3,35},{4,36},{5,37},{6,38},{7,39},{8,40},{9,... | collective-permute-start | bytes 7077896 | tf_op jit(solution)/shard_map/ppermute | solution.py:80
  110.5 28.4 %all-to-all-start = ((bf16[8,2,96,384]{3,2,1,0:T(8,128)(2,1)}), bf16[8,2,96,384]{3,2,1,0:T(8,128)(2,1)S(1)}, u32[]{:S(2)}, u32[]{:S(2)}) async-start(bf16[8,2,96,384]{3,2,1,0:T(8,128)(2,1)} %get-tuple-element.7), calls=%async_computation | async-start | bytes 2359296 | tf_op jit(solution)/shard_map/all_to_all | solution.py:84
  115.4 116.1 %collective-permute-start.9 = (bf16[384,3072]{1,0:T(8,128)(2,1)S(1)}, bf16[384,3072]{1,0:T(8,128)(2,1)}, u32[]{:S(2)}, u32[]{:S(2)}) collective-permute-start(bf16[384,3072]{1,0:T(8,128)(2,1)S(1)} %collective-permute-done.7.refs_6_), channel_id=1, source_target_pairs={{0,32},{1,33},{2,34},{3,35},{4,36},{5,37},{6,38},{7,39},{8,40},{9,... | collective-permute-start | bytes 7077896 | tf_op jit(solution)/shard_map/ppermute | solution.py:80
  115.7 115.8 %collective-permute-start.8 = (bf16[384,3072]{1,0:T(8,128)(2,1)}, bf16[384,3072]{1,0:T(8,128)(2,1)}, u32[]{:S(2)}, u32[]{:S(2)}) collective-permute-start(bf16[384,3072]{1,0:T(8,128)(2,1)} %collective-permute-done.6.refs_5_), channel_id=1, source_target_pairs={{0,32},{1,33},{2,34},{3,35},{4,36},{5,37},{6,38},{7,39},{8,40},{9,... | collective-permute-start | bytes 7077896 | tf_op jit(solution)/shard_map/ppermute | solution.py:80
  224.8 1.0 copy-start
  225.9 21.9 %all-to-all-start.2 = ((bf16[8,2,96,384]{3,2,1,0:T(8,128)(2,1)}), bf16[8,2,96,384]{3,2,1,0:T(8,128)(2,1)S(1)}, u32[]{:S(2)}, u32[]{:S(2)}) async-start(bf16[8,2,96,384]{3,2,1,0:T(8,128)(2,1)} %copy-done), calls=%async_computation.2 | async-start | bytes 2359296 | tf_op jit(solution)/shard_map/all_to_all | solution.py:84

commit v2 on v1

v2 whole, which is shorter than its diff:
```python
import functools

import jax
import jax.numpy as jnp
from jax import lax
from jax.experimental import pallas as pl
from jax.experimental.pallas import tpu as pltpu
from jax.sharding import Mesh, PartitionSpec as P

HEAD_DIM = 128
HEADS = 24
GROUPS = 8
GROUP_HEADS = HEADS // GROUPS
ROWS = 4
COLUMNS = 8
TIMES = 2
PART = 96
D = HEADS * HEAD_DIM
NEIGH = 27
COEF = HEAD_DIM ** (-0.5) * 1.4426950408889634
LOW = -1e30
TILE = 4 * PART
CELL = TIMES * TILE
PAIRS = 10
PARTS = ((0,), (1, 2))
Q_AT = 1

AXES = ("yl", "c", "yh", "zh", "zl", "x")
SIZES = (2, 2, 2, 2, 2, 4)
COLUMN_AXES = ("yh", "zh", "yl")


def places():
    for flat in range(128):
        left, coords = flat, []
        for size in reversed(SIZES):
            coords.append(left % size)
            left //= size
        yield flat, tuple(reversed(coords))


def flat_of(coords):
    flat = 0
    for coord, size in zip(coords, SIZES):
        flat = flat * size + coord
    return flat


def route(target):
    pairs = []
    for flat, coords in places():
        to = target(*coords)
        if to is not None:
            pairs.append((flat, flat_of(to)))
    return pairs


def column_step(step):
    def target(yl, c, yh, zh, zl, x):
        column = zl * 4 + x + step
        if not 0 <= column < COLUMNS:
            return None
        return (yl, c, yh, zh, column // 4, column % 4)

    return target


def y_step(step):
    def target(yl, c, yh, zh, zl, x):
        y = (yh * 2 + yl + step) % 4
        return (y % 2, c, y // 2, zh, zl, x)

    return target


RIGHT = route(column_step(1))
LEFT = route(column_step(-1))
FAR = route(lambda yl, c, yh, zh, zl, x: y_step(1 if c else -1)(yl, c, yh, zh, zl, x))
FLIP_Z = route(lambda yl, c, yh, zh, zl, x: (yl, c, yh, 1 - zh, zl, x))
FLIP_Y = route(lambda yl, c, yh, zh, zl, x: (yl, c, 1 - yh, zh, zl, x))
FLIP_BOTH = route(lambda yl, c, yh, zh, zl, x: (yl, c, 1 - yh, 1 - zh, zl, x))
OTHER_CORE = route(lambda yl, c, yh, zh, zl, x: (yl, 1 - c, yh, zh, zl, x))


def permute(array, pairs):
    return lax.ppermute(array, AXES, pairs)


def exchange(array):
    return lax.all_to_all(array, COLUMN_AXES, 0, 0)


def arrange(*arrays):
    ins, outs, shapes, count = [], [], [], []
    for stack, heads in arrays:
        lanes = len(heads) * HEAD_DIM
        inner = (TIMES, PART, lanes) if len(stack) == 1 else (len(stack), TIMES, PART, lanes)
        shapes.append(jax.ShapeDtypeStruct((GROUPS,) + inner, jnp.bfloat16))
        outs.append(pl.BlockSpec((1,) + inner, lambda g, size=len(inner): (g,) + (0,) * size))
        for array in stack:
            ins.append(array)
        count.append((len(stack), heads))

    def kernel(*refs):
        at = 0
        for out_ref, (size, heads) in zip(refs[len(ins) :], count):
            lanes = pl.ds(heads[0] * HEAD_DIM, len(heads) * HEAD_DIM)
            for which in range(size):
                value = refs[at][:, :, lanes]
                if size == 1:
                    out_ref[0] = value
                else:
                    out_ref[0, which] = value
                at += 1

    block = pl.BlockSpec((TIMES, PART, GROUP_HEADS * HEAD_DIM), lambda g: (0, 0, g))
    return pl.pallas_call(
        kernel,
        grid=(GROUPS,),
        in_specs=[block] * len(ins),
        out_specs=outs,
        out_shape=shapes,
        compiler_params=pltpu.CompilerParams(vmem_limit_bytes=58 * 1024 * 1024),
        name="arrange",
    )(*ins)


def attend_kernel(plan, lists, q_ref, *refs):
    units, slots, sources, taken, given, done, passed = plan
    pass_refs, refs = refs[:passed], refs[passed:]
    kv_refs, refs = refs[:sources], refs[sources:]
    state_in, refs = refs[: 3 * taken], refs[3 * taken :]
    o_refs, refs = refs[:done], refs[done:]
    state_out, refs = refs[: 3 * given], refs[3 * given :]
    kv_ref, vt_ref, qt_ref, m_ref, l_ref, acc_ref, s_refs, p_refs, top_refs, factor_refs, sems = refs
    half = 2 * PART

    def load(unit, core):
        slot, column, pair, lane = units[unit]
        source = kv_refs[pair[core]].at[:, :, :, :, pl.ds(lane * HEAD_DIM, HEAD_DIM)]
        return pltpu.make_async_copy(source, kv_ref.at[unit, core], sems.at[unit, core])

    for unit in range(len(units)):
        for core in range(2):
            load(unit, core).start()

    fresh = 0
    for slot, (lane, begin, end) in enumerate(slots):
        mine = pl.ds(slot * ROWS, ROWS)
        if begin is None:
            m_ref[mine] = jnp.full((ROWS, 1, TILE), LOW, jnp.float32)
            l_ref[mine] = jnp.zeros((ROWS, 8, TILE), jnp.float32)
            acc_ref[mine] = jnp.zeros((ROWS, HEAD_DIM, TILE), jnp.float32)
        else:
            for at, ref in enumerate((m_ref, l_ref, acc_ref)):
                ref[mine] = state_in[3 * begin + at][...]
        for row in range(ROWS):
            lanes = slice(lane * HEAD_DIM, (lane + 1) * HEAD_DIM)
            q = [q_ref[2 * row : 2 * row + 2, t, :, lanes].reshape(half, HEAD_DIM) for t in range(TIMES)]
            qt_ref[slot * ROWS + row] = jnp.concatenate(q, axis=0).T
    for at, ref in enumerate(pass_refs):
        o_refs[0][:, :, :, at * HEAD_DIM : (at + 1) * HEAD_DIM] = ref[...]
    factor_refs[1][...] = jnp.ones(factor_refs[1].shape, jnp.float32)
    p_refs[1][...] = jnp.zeros(p_refs[1].shape, jnp.bfloat16)
    first = lax.broadcasted_iota(jnp.int32, (1, TILE), 1) < half

    def choose(unit, values):
        result = jnp.int32(values[0])
        for at in range(1, len(values)):
            result = jnp.where(unit >= at, jnp.int32(values[at]), result)
        return result

    slot_of = [unit[0] for unit in units]
    column_of = [unit[1] + 1 for unit in units]

    def cell(which, unit, key_row):
        parts = []
        for t2 in range(TIMES):
            for core in range(2):
                for yl in range(2):
                    parts.append(kv_ref[unit, core, 2 * key_row + yl, which, t2])
        return jnp.concatenate(parts, axis=0)

    def turn(unit):
        def body(key_row, carry):
            vt_ref[unit * ROWS + key_row] = cell(1, unit, key_row).T
            return carry

        lax.fori_loop(0, ROWS, body, 0)

    def place(at):
        at = jnp.clip(at, 0, len(units) * PAIRS - 1)
        unit, spot = at // PAIRS, at % PAIRS + 1
        row, step = spot // 3, spot % 3
        return unit, row, row + step - 1, step

    def score(at, s_ref, top_ref):
        unit, row, key_row, step = place(at)
        qt = qt_ref[choose(unit, slot_of) * ROWS + row]
        s = jnp.dot(cell(0, unit, key_row), qt, preferred_element_type=jnp.float32)
        s_ref[...] = s
        for t2 in range(TIMES):
            top_ref[t2] = jnp.max(s[t2 * TILE : (t2 + 1) * TILE].reshape(TILE // 8, 8, TILE), axis=0)

    def weigh(at, s_ref, top_ref, p_ref, factor_ref):
        unit, row, key_row, step = place(at)
        spot = choose(unit, slot_of) * ROWS + row
        start = (lists[ROWS * TIMES * NEIGH] ^ row) * (TIMES * NEIGH) + step * 3 + choose(unit, column_of)
        oks = []
        for t2 in range(TIMES):
            use = [lists[start + t * NEIGH + (t2 - t + 1) * 9] for t in range(TIMES)]
            oks.append(jnp.where(first, use[0], use[1]) >= 0)
        m_old = m_ref[spot]
        best = m_old
        for t2 in range(TIMES):
            top = jnp.max(top_ref[t2], axis=0, keepdims=True)
            best = jnp.maximum(best, jnp.where(oks[t2], top, LOW))
        m_ref[spot] = best
        factor = jnp.exp2((m_old - best) * COEF)
        factor_ref[...] = factor
        l = l_ref[spot] * factor
        shifts = [jnp.where(ok, best * COEF, -LOW) for ok in oks]
        for piece in range(6):
            rows = slice(piece * 128, (piece + 1) * 128)
            p = jnp.exp2(s_ref[rows] * COEF - shifts[piece // 3])
            l = l + jnp.sum(p.reshape(16, 8, TILE), axis=0)
            p_ref[rows] = p.astype(jnp.bfloat16)
        l_ref[spot] = l

    def absorb(at, p_ref, factor_ref):
        unit, row, key_row, step = place(at)
        spot = choose(unit, slot_of) * ROWS + row
        update = jnp.dot(vt_ref[unit * ROWS + key_row], p_ref[...], preferred_element_type=jnp.float32)
        acc_ref[spot] = acc_ref[spot] * factor_ref[...] + update

    for core in range(2):
        load(0, core).wait()
    turn(0)
    score(0, s_refs[0], top_refs[0])
    rounds = PAIRS // 2

    def round_of(index, carry):
        at = 2 * index
        for unit in range(1, len(units)):

            @pl.when(index == rounds * unit - 1)
            def _(unit=unit):
                for core in range(2):
                    load(unit, core).wait()

        @pl.when((index % rounds == rounds - 1) & (index < rounds * len(units) - 1))
        def _():
            turn(index // rounds + 1)

        score(at + 1, s_refs[1], top_refs[1])
        absorb(at - 1, p_refs[1], factor_refs[1])
        weigh(at, s_refs[0], top_refs[0], p_refs[0], factor_refs[0])
        score(at + 2, s_refs[0], top_refs[0])
        absorb(at, p_refs[0], factor_refs[0])
        weigh(at + 1, s_refs[1], top_refs[1], p_refs[1], factor_refs[1])
        return carry

    lax.fori_loop(0, rounds * len(units), round_of, 0)
    absorb(len(units) * PAIRS - 1, p_refs[1], factor_refs[1])
    for slot, (lane, begin, end) in enumerate(slots):
        if end[0] == "state":
            for at, ref in enumerate((m_ref, l_ref, acc_ref)):
                state_out[3 * end[1] + at][...] = ref[pl.ds(slot * ROWS, ROWS)]
            continue
        for row in range(ROWS):
            spot = slot * ROWS + row
            out = (acc_ref[spot] / jnp.sum(l_ref[spot], axis=0, keepdims=True)).T.astype(jnp.bfloat16)
            lanes = slice(end[2] * HEAD_DIM, (end[2] + 1) * HEAD_DIM)
            for t in range(TIMES):
                o_refs[end[1]][2 * row : 2 * row + 2, t, :, lanes] = out[t * half : (t + 1) * half].reshape(
                    2, PART, HEAD_DIM
                )


def attend(lists, q, blocks, units, slots, states, passed):
    given = sum(1 for slot in slots if slot[2][0] == "state")
    widths = {0: len(passed) * HEAD_DIM}
    for slot in slots:
        if slot[2][0] == "out":
            widths[slot[2][1]] = widths.get(slot[2][1], 0) + HEAD_DIM
    state_shapes = [(ROWS, 1, TILE), (ROWS, 8, TILE), (ROWS, HEAD_DIM, TILE)]
    shapes = [jax.ShapeDtypeStruct((GROUPS, TIMES, PART, widths[at]), jnp.bfloat16) for at in range(len(widths))]
    shapes += [jax.ShapeDtypeStruct(shape, jnp.float32) for shape in state_shapes] * given
    vmem, anywhere = pl.BlockSpec(memory_space=pltpu.VMEM), pl.BlockSpec(memory_space=pl.ANY)
    plan = (units, slots, len(blocks), len(states) // 3, given, len(widths), len(passed))
    count, spots = len(units), len(slots) * ROWS
    return pl.pallas_call(
        functools.partial(attend_kernel, plan),
        in_specs=[pl.BlockSpec(memory_space=pltpu.SMEM), vmem] + [vmem] * len(passed) + [anywhere] * len(blocks) + [vmem] * len(states),
        out_specs=[vmem] * len(shapes),
        scratch_shapes=[
            pltpu.VMEM((count, 2, GROUPS, 2, TIMES, PART, HEAD_DIM), jnp.bfloat16),
            pltpu.VMEM((count * ROWS, HEAD_DIM, CELL), jnp.bfloat16),
            pltpu.VMEM((spots, HEAD_DIM, TILE), jnp.bfloat16),
            pltpu.VMEM((spots, 1, TILE), jnp.float32),
            pltpu.VMEM((spots, 8, TILE), jnp.float32),
            pltpu.VMEM((spots, HEAD_DIM, TILE), jnp.float32),
            [pltpu.VMEM((CELL, TILE), jnp.float32)] * 2,
            [pltpu.VMEM((CELL, TILE), jnp.bfloat16)] * 2,
            [pltpu.VMEM((2, 8, TILE), jnp.float32)] * 2,
            [pltpu.VMEM((1, TILE), jnp.float32)] * 2,
            pltpu.SemaphoreType.DMA((count, 2)),
        ],
        out_shape=shapes,
        compiler_params=pltpu.CompilerParams(vmem_limit_bytes=58 * 1024 * 1024),
        cost_estimate=pl.CostEstimate(
            flops=count * PAIRS * 384 * 768 * 128 * 4,
            bytes_accessed=count * 2 * 786432,
            transcendentals=count * PAIRS * 384 * 768,
        ),
        name="attend",
    )(lists, q, *passed, *blocks, *states)


def project_kernel(ids, att_ref, *refs):
    w_refs, o_ref = refs[:-1], refs[-1]
    total = None
    for shard in range(4):
        for part in range(2):
            rows = att_ref[ids[shard] * 2 + part].reshape(TIMES * PART, GROUP_HEADS * HEAD_DIM)
            term = jnp.dot(rows, w_refs[2 * shard + part][...], preferred_element_type=jnp.float32)
            total = term if total is None else total + term
    o_ref[...] = total.astype(jnp.bfloat16).reshape(TIMES, PART, total.shape[1])


def project(ids, att, *shards):
    block = 512
    rows = D // GROUPS
    specs, pieces = [pl.BlockSpec(att.shape, lambda n, s: (0, 0, 0, 0))], []
    for shard in shards:
        for part in range(2):
            specs.append(pl.BlockSpec((rows, block), lambda n, s, part=part: (part, n)))
            pieces.append(shard)
    return pl.pallas_call(
        project_kernel,
        grid_spec=pltpu.PrefetchScalarGridSpec(
            num_scalar_prefetch=1,
            grid=(D // block,),
            in_specs=specs,
            out_specs=pl.BlockSpec((TIMES, PART, block), lambda n, s: (0, 0, n)),
        ),
        out_shape=jax.ShapeDtypeStruct((TIMES, PART, D), jnp.bfloat16),
        compiler_params=pltpu.CompilerParams(vmem_limit_bytes=58 * 1024 * 1024),
        cost_estimate=pl.CostEstimate(
            flops=2 * TIMES * PART * D * D, bytes_accessed=2 * D * D, transcendentals=0
        ),
        name="project",
    )(ids, att, *pieces)


def on_device(queries, keys, values, neighbours, w_out):
    live = {"w": w_out, "near": neighbours, "qkv": (queries, keys, values)}

    def fence():
        names = list(live)
        for name, value in zip(names, lax.optimization_barrier([live[name] for name in names])):
            live[name] = value

    def sides(at):
        kv = live["kv", at]
        live["left", at], live["right", at] = permute(kv, RIGHT), permute(kv, LEFT)

    def swap(*names):
        for name, at in names:
            live[name + "_other", at] = permute(live[name, at], OTHER_CORE)

    def work(units, slots, states, passed):
        blocks, spots, found = [], {}, []
        for slot, column, name, at, lane in units:
            for end in (name, name + "_other"):
                if (end, at) not in spots:
                    spots[end, at] = len(blocks)
                    blocks.append(live[end, at])
            found.append((slot, column, (spots[name, at], spots[name + "_other", at]), lane))
        return attend(live["lists"], live["q"], blocks, tuple(found), tuple(slots), states, passed)

    (live["part", 0],) = arrange(((keys, values), PARTS[0]))
    fence()
    queries, keys, values = live.pop("qkv")
    live["kv", 0] = exchange(live.pop(("part", 0)))
    live["part", 1], q_part = arrange(((keys, values), PARTS[1]), ((queries,), range(GROUP_HEADS)))
    if Q_AT == 0:
        live["q"] = exchange(q_part)
    else:
        live["q_part"] = q_part
    row = lax.axis_index("yh") * 2 + lax.axis_index("zh")
    flips = [live["near"].reshape(-1)]
    for pairs in (FLIP_Z, FLIP_Y, FLIP_BOTH):
        flips.append(permute(live["near"], pairs).reshape(-1))
    live["lists"] = jnp.concatenate(flips + [row.astype(jnp.int32).reshape(1)])
    live["w_other", 0] = permute(live["w"], OTHER_CORE)
    fence()
    live["kv", 1] = exchange(live.pop(("part", 1)))
    if Q_AT == 1:
        live["q"] = exchange(live.pop("q_part"))
    sides(0)
    swap(("kv", 0))
    fence()
    if Q_AT == 2:
        live["q"] = exchange(live.pop("q_part"))
    sides(1)
    swap(("kv", 1), ("left", 0), ("right", 0))
    live["far", 0] = permute(live["w"], FAR)
    units = [(0, 0, "kv", 0, 0), (1, 0, "kv", 1, 0), (2, 0, "kv", 1, 1), (0, -1, "left", 0, 0), (0, 1, "right", 0, 0)]
    slots = [(0, None, ("out", 0, 0)), (1, None, ("state", 0)), (2, None, ("state", 1))]
    done, *states = work(units, slots, [], [])
    live["done"] = done
    for at, state in enumerate(states):
        live["state", at] = state
    fence()
    swap(("left", 1), ("right", 1))
    fence()
    swap(("far", 0))
    units = [(0, -1, "left", 1, 0), (1, -1, "left", 1, 1), (0, 1, "right", 1, 0), (1, 1, "right", 1, 1)]
    slots = [(1, 0, ("out", 0, 1)), (2, 1, ("out", 0, 2))]
    (live["att"],) = work(units, slots, [live.pop(("state", at)) for at in range(6)], [live.pop("done")])
    fence()
    att = exchange(live["att"])
    yl, c = lax.axis_index("yl"), lax.axis_index("c")
    ids = jnp.stack([2 * yl + c, 2 * yl + 1 - c, 2 * (1 - yl) + c, 2 * (1 - yl) + 1 - c]).astype(jnp.int32)
    return project(ids, att, live["w"], live["w_other", 0], live["far", 0], live["far_other", 0])


def solution(mesh):
    fine = Mesh(mesh.devices.reshape(SIZES), AXES)
    tile, head = ("yh", "zh", "zl", "x"), ("yl", "c")
    placed = (
        P(tile, head, None),
        P(tile, head, None),
        P(tile, head, None),
        P(tile, None),
        P(head, None),
    )
    return jax.shard_map(
        on_device, mesh=fine, in_specs=placed, out_specs=P(tile, head, None), check_vma=False
    )
```

time: 261 us -> 217 us (0.83)
  waiting for transfers between devices: 99.7 us -> 67.6 us
  Pallas kernels: 103 us -> 77.3 us
  starting transfers between devices: 26.8 us -> 41.6 us
    all_to_all x3, waiting for transfers between devices: 48 us -> 18.8 us  [exchange(): return lax.all_to_all(array, COLUMN_AXES, 0, 0)]
    pallas_call x2 -> x4, Pallas kernels: 92.3 us -> 65 us  [the longest x2 53.3 us: attend(): pl.pallas_call(functools.partial(attend_kernel, plan), in_specs=[pl.Block...]
    all_gather x1 -> x0, blocking collectives: 22.9 us -> none  [on_device(): lists = lax.all_gather(neighbours, ('yh', 'zh')).reshape(-1)]
    all_to_all x0 -> x1, blocking collectives: none -> 22.2 us  [exchange(): return lax.all_to_all(array, COLUMN_AXES, 0, 0)]
    ppermute x10 -> x16, starting transfers between devices: 8.61 us -> 23.9 us  [permute(): return lax.ppermute(array, AXES, pairs)]
    slice x1 -> x0, local copies, waits for them, and re-layouts: 4.88 us -> none  [on_device(): w_below = permute(w_out[half:], UP)]
    unnamed x4 -> x18, local copies, waits for them, and re-layouts: 1.01 us -> 4.28 us
    ppermute x10 -> x16, waiting for transfers between devices: 51.7 us -> 48.7 us  [permute(): return lax.ppermute(array, AXES, pairs)]
  transfers between devices with their start and end apart: 13 -> 19, of which waited for: 5 -> 9; matrix products, arithmetic and copies ran while one was open for 2% -> 1% of each run, Pallas kernels for 33% -> 28%
where the time goes in v2:
time: 217 us; the launch traced here: 215 us
  Pallas kernels  77.3 us (36%)
  waiting for transfers between devices  67.6 us (31%)
  starting transfers between devices  41.6 us (19%)
  blocking collectives  22.2 us (10%)
  local copies, waits for them, and re-layouts  5.28 us (2%)
    pallas_call x2, Pallas kernels, attend(): pl.pallas_call(functools.partial(attend_kernel, plan), in_specs=[pl.Block...  53.3 us
    ppermute x16, waiting for transfers between devices, permute(): return lax.ppermute(array, AXES, pairs)  48.7 us
    ppermute x16, starting transfers between devices, permute(): return lax.ppermute(array, AXES, pairs)  23.9 us
    all_to_all x1, blocking collectives, exchange(): return lax.all_to_all(array, COLUMN_AXES, 0, 0)  22.2 us
    all_to_all x3, waiting for transfers between devices, exchange(): return lax.all_to_all(array, COLUMN_AXES, 0, 0)  18.8 us
    all_to_all x3, starting transfers between devices, exchange(): return lax.all_to_all(array, COLUMN_AXES, 0, 0)  17.8 us
    pallas_call x1, Pallas kernels, project(): pl.pallas_call(project_kernel, grid_spec=pltpu.PrefetchScalarGridSpec(num...  12.3 us
    pallas_call x2, Pallas kernels, arrange(): pl.pallas_call(kernel, grid=(GROUPS,), in_specs=[block] * len(ins), out_s...  11.7 us
  transfers between devices with their start and end apart: 19, of which 9 were waited for; matrix products, arithmetic and copies ran while one was open for 1% of the time, Pallas kernels for 28%

profile of v2, /device:TPU:6, one launch (start us, length us, event | category | flops | bytes accessed | tf_op | source)
XLA Modules:
  0.0 214.9 jit_solution(15393736190082448288)
XLA Ops:
  0.0 5.5 %arrange.2 = bf16[8,2,2,96,128]{4,3,2,1,0:T(8,128)(2,1)} custom-call(bf16[2,96,3072]{2,1,0:T(8,128)(2,1)} %refs_0_.2, bf16[2,96,3072]{2,1,0:T(8,128)(2,1)} %refs_1_.2), custom_call_target="tpu_custom_call" | custom-call | tf_op jit(solution)/shard_map/arrange/pallas_call | solution.py:117
  5.5 7.9 %all-to-all-start = ((bf16[8,2,2,96,128]{4,3,2,1,0:T(8,128)(2,1)}), bf16[8,2,2,96,128]{4,3,2,1,0:T(8,128)(2,1)S(1)}, u32[]{:S(2)}, u32[]{:S(2)}) async-start(bf16[8,2,2,96,128]{4,3,2,1,0:T(8,128)(2,1)} %arrange.2), calls=%async_computation | async-start | bytes 1572864 | tf_op jit(solution)/shard_map/all_to_all | solution.py:90
  13.5 5.9 %collective-permute-start.2 = (s32[2,27]{1,0:T(2,128)S(1)}, s32[2,27]{1,0:T(2,128)S(1)}, u32[]{:S(2)}, u32[]{:S(2)}) collective-permute-start(s32[2,27]{1,0:T(2,128)S(1)} %copy-done.8), channel_id=1, source_target_pairs={{0,24},{1,25},{2,26},{3,27},{4,28},{5,29},{6,30},{7,31},{8,16},{9,... | collective-permute-start | bytes 656 | tf_op jit(solution)/shard_map/ppermute | solution.py:86
  19.4 0.6 collective-permute-start.1
  20.0 0.1 collective-permute-start
  20.1 0.1 reshape.15
  20.1 6.2 %arrange.3 = (bf16[8,2,2,96,256]{4,3,2,1,0:T(8,128)(2,1)}, bf16[8,2,96,384]{3,2,1,0:T(8,128)(2,1)}) custom-call(bf16[2,96,3072]{2,1,0:T(8,128)(2,1)} %refs_0_.2, bf16[2,96,3072]{2,1,0:T(8,128)(2,1)} %refs_1_.2, bf16[2,96,3072]{2,1,0:T(8,128)(2,1)} %refs_2_), custom_call_target="tpu_custom_call" | custom-call | tf_op jit(solution)/shard_map/arrange/pallas_call | solution.py:117
  26.3 2.7 %collective-permute-done.2 = s32[2,27]{1,0:T(2,128)S(1)} collective-permute-done((s32[2,27]{1,0:T(2,128)S(1)}, s32[2,27]{1,0:T(2,128)S(1)}, u32[]{:S(2)}, u32[]{:S(2)}) %collective-permute-start.2) | collective-permute-done | bytes 248 | tf_op jit(solution)/shard_map/ppermute | solution.py:86
  29.0 0.1 reshape.18
  29.1 0.0 collective-permute-done.1
  29.1 0.1 reshape.17
  29.2 0.0 collective-permute-done
  29.2 0.1 reshape.16
  29.3 0.7 concatenate.3.lists
  30.0 22.2 %all_to_all.20.q_ref = bf16[8,2,96,384]{3,2,1,0:T(8,128)(2,1)} all-to-all(bf16[8,2,96,384]{3,2,1,0:T(8,128)(2,1)} %get-tuple-element.83), channel_id=1, replica_groups=mesh['yl'=2,'c'=2,'yh'=2,'zh'=2,'zl'=2,'x'=4] {'yh','zh','yl'}, dimensions={0} | all-to-all | bytes 2359296 | tf_op jit(solution)/shard_map/all_to_all | solution.py:90
  52.2 4.3 %all-to-all-start.1 = ((bf16[8,2,2,96,256]{4,3,2,1,0:T(8,128)(2,1)}), bf16[8,2,2,96,256]{4,3,2,1,0:T(8,128)(2,1)}, u32[]{:S(2)}, u32[]{:S(2)}) async-start(bf16[8,2,2,96,256]{4,3,2,1,0:T(8,128)(2,1)} %get-tuple-element.82), calls=%async_computation.1 | async-start | bytes 3145728 | tf_op jit(solution)/shard_map/all_to_all | solution.py:90
  56.5 0.1 collective-permute-start.6
  56.6 2.7 %collective-permute-start.5 = (bf16[8,2,2,96,128]{4,3,2,1,0:T(8,128)(2,1)S(1)}, bf16[8,2,2,96,128]{4,3,2,1,0:T(8,128)(2,1)S(1)}, u32[]{:S(2)}, u32[]{:S(2)}) collective-permute-start(bf16[8,2,2,96,128]{4,3,2,1,0:T(8,128)(2,1)S(1)} %all-to-all-done.refs_0_), channel_id=1, source_target_pairs={{1,0},{2,1},{3,2},{4,3},{5,4},{6,5},{7,6},{9,8},{10,9},{11,10},{12... | collective-permute-start | bytes 2359304 | tf_op jit(solution)/shard_map/ppermute | solution.py:86
  59.3 5.2 %collective-permute-start.4 = (bf16[8,2,2,96,128]{4,3,2,1,0:T(8,128)(2,1)S(1)}, bf16[8,2,2,96,128]{4,3,2,1,0:T(8,128)(2,1)}, u32[]{:S(2)}, u32[]{:S(2)}) collective-permute-start(bf16[8,2,2,96,128]{4,3,2,1,0:T(8,128)(2,1)S(1)} %all-to-all-done.refs_0_), channel_id=1, source_target_pairs={{0,1},{1,2},{2,3},{3,4},{4,5},{5,6},{6,7},{8,9},{9,10},{10,11},{11... | collective-permute-start | bytes 2359304 | tf_op jit(solution)/shard_map/ppermute | solution.py:86
  64.6 0.0 collective-permute-done.6.refs_1_
  64.6 0.0 copy-start.5
  64.6 25.2 %collective-permute-done.5.refs_6_ = bf16[8,2,2,96,128]{4,3,2,1,0:T(8,128)(2,1)S(1)} collective-permute-done((bf16[8,2,2,96,128]{4,3,2,1,0:T(8,128)(2,1)S(1)}, bf16[8,2,2,96,128]{4,3,2,1,0:T(8,128)(2,1)S(1)}, u32[]{:S(2)}, u32[]{:S(2)}) %collective-permute-start.5) | collective-permute-done | bytes 786464 | tf_op jit(solution)/shard_map/ppermute | solution.py:86
  89.8 0.9 copy-done.6
  90.7 0.0 collective-permute-start.12
  90.7 0.1 collective-permute-start.10
  90.8 0.5 collective-permute-start.9
  91.3 1.9 collective-permute-start.8
  93.2 6.0 %collective-permute-start.7 = (bf16[8,2,2,96,256]{4,3,2,1,0:T(8,128)(2,1)}, bf16[8,2,2,96,256]{4,3,2,1,0:T(8,128)(2,1)}, u32[]{:S(2)}, u32[]{:S(2)}) collective-permute-start(bf16[8,2,2,96,256]{4,3,2,1,0:T(8,128)(2,1)} %all-to-all-done.1.refs_2_), channel_id=1, source_target_pairs={{0,1},{1,2},{2,3},{3,4},{4,5},{5,6},{6,7},{8,9},{9,10},{10,11},{11... | collective-permute-start | bytes 4718600 | tf_op jit(solution)/shard_map/ppermute | solution.py:86
  99.2 0.0 collective-permute-done.10.refs_5_
  99.2 0.1 collective-permute-start.11
  99.3 2.6 %collective-permute-done.11.refs_7_ = bf16[8,2,2,96,128]{4,3,2,1,0:T(8,128)(2,1)} collective-permute-done((bf16[8,2,2,96,128]{4,3,2,1,0:T(8,128)(2,1)}, bf16[8,2,2,96,128]{4,3,2,1,0:T(8,128)(2,1)}, u32[]{:S(2)}, u32[]{:S(2)}) %collective-permute-start.11) | collective-permute-done | bytes 786464 | tf_op jit(solution)/shard_map/ppermute | solution.py:86
  101.9 0.0 collective-permute-done.9.refs_3_
  102.0 28.9 %attend.2 = (bf16[8,2,96,128]{3,2,1,0:T(8,128)(2,1)}, f32[4,1,384]{2,1,0:T(1,128)}, f32[4,8,384]{2,1,0:T(8,128)}, f32[4,128,384]{2,1,0:T(8,128)}, f32[4,1,384]{2...) custom-call(s32[217]{0:T(256)} %concatenate.3.lists, bf16[8,2,96,384]{3,2,1,0:T(8,128)(2,1)} %all_to_all.20.q_ref, ...), custom_call_target="tpu_custom_call" | custom-call | flops 7549747200 | bytes 7864320 | tf_op jit(solution)/shard_map/attend/pallas_call | solution.py:292
  130.9 1.1 collective-permute-done.8.refs_3_
  132.0 1.2 collective-permute-done.7.refs_1_
  133.1 11.9 %collective-permute-done.12.refs_4_.refs_5_ = bf16[768,3072]{1,0:T(8,128)(2,1)S(1)} collective-permute-done((bf16[768,3072]{1,0:T(8,128)(2,1)}, bf16[768,3072]{1,0:T(8,128)(2,1)S(1)}, u32[]{:S(2)}, u32[]{:S(2)}) %collective-permute-start.12) | collective-permute-done | bytes 4718624 | tf_op jit(solution)/shard_map/ppermute | solution.py:86
  145.0 0.5 collective-permute-start.14
  145.5 3.1 %collective-permute-done.13.refs_2_ = bf16[8,2,2,96,256]{4,3,2,1,0:T(8,128)(2,1)S(1)} collective-permute-done((bf16[8,2,2,96,256]{4,3,2,1,0:T(8,128)(2,1)}, bf16[8,2,2,96,256]{4,3,2,1,0:T(8,128)(2,1)S(1)}, u32[]{:S(2)}, u32[]{:S(2)}) %collective-permute-start.13) | collective-permute-done | bytes 1572896 | tf_op jit(solution)/shard_map/ppermute | solution.py:86
  148.6 1.2 copy-done.3
  149.8 1.0 collective-permute-done.14.refs_4_
  150.9 1.1 copy-done.4
  152.0 0.1 collective-permute-start.15
  152.2 24.4 %attend.3 = bf16[8,2,96,384]{3,2,1,0:T(8,128)(2,1)} custom-call(s32[217]{0:T(256)} %concatenate.3.lists, bf16[8,2,96,384]{3,2,1,0:T(8,128)(2,1)} %all_to_all.20.q_ref, bf16[8,2,96,128]{3,2,1,0:T(8,128)(2,1)} %get-tuple-element.123.refs_0_, bf16[8,2,2,96,256]{4,3,2,1,0:T(8,128)(2,1)} %collective-permute-done.7.refs_1_, bf16[8,2,2,96,256]{4,3,2,1,0:T(8,128)(2,1)} %copy-done.3, ...), custom_call_target="tpu_custom_call" | custom-call | flops 6039797760 | bytes 6291456 | tf_op jit(solution)/shard_map/attend/pallas_call | solution.py:292
  176.5 5.5 %all-to-all-start.3 = ((bf16[8,2,96,384]{3,2,1,0:T(8,128)(2,1)}), bf16[8,2,96,384]{3,2,1,0:T(8,128)(2,1)S(1)}, u32[]{:S(2)}, u32[]{:S(2)}) async-start(bf16[8,2,96,384]{3,2,1,0:T(8,128)(2,1)} %attend.3), calls=%async_computation.3 | async-start | bytes 2359296 | tf_op jit(solution)/shard_map/all_to_all | solution.py:90
  182.1 0.6 pad_add_fusion.ids
  182.7 18.8 %all-to-all-done.3.att_ref = bf16[8,2,96,384]{3,2,1,0:T(8,128)(2,1)S(1)} async-done(((bf16[8,2,96,384]{3,2,1,0:T(8,128)(2,1)}), bf16[8,2,96,384]{3,2,1,0:T(8,128)(2,1)S(1)}, u32[]{:S(2)}, u32[]{:S(2)}) %all-to-all-start.3) | async-done | bytes 1179680 | tf_op jit(solution)/shard_map/all_to_all | solution.py:90
  201.5 1.0 copy-done.1
  202.6 12.3 %project.1 = bf16[2,96,3072]{2,1,0:T(8,128)(2,1)} custom-call(s32[4]{0:T(128)} %pad_add_fusion.ids, bf16[8,2,96,384]{3,2,1,0:T(8,128)(2,1)} %copy-done.1, bf16[768,3072]{1,0:T(8,128)(2,1)} %refs_1_.3, bf16[768,3072]{1,0:T(8,128)(2,1)} %refs_1_.3, bf16[768,3072]{1,0:T(8,128)(2,1)} %collective-permute-done.3.refs_2_.refs_3_, ...), custom_call_target="tpu_custom_call" | custom-call | flops 3623878656 | bytes 18874368 | tf_op jit(solution)/shard_map/project/pallas_call | solution.py:339
  (20 shorter events, 0.0 us)
Async XLA Ops:
  5.5 7.9 %copy-start.8 = (s32[2,27]{1,0:T(2,128)S(1)}, s32[2,27]{1,0:T(2,128)}, u32[]{:S(2)}) copy-start(s32[2,27]{1,0:T(2,128)} %param.8) | copy-start | bytes 652
  5.5 24.4 %collective-permute-start.3 = (bf16[768,3072]{1,0:T(8,128)(2,1)}, bf16[768,3072]{1,0:T(8,128)(2,1)}, u32[]{:S(2)}, u32[]{:S(2)}) collective-permute-start(bf16[768,3072]{1,0:T(8,128)(2,1)} %refs_1_.3), channel_id=1, source_target_pairs={{0,32},{1,33},{2,34},{3,35},{4,36},{5,37},{6,38},{7,39},{8,40},{9,... | collective-permute-start | bytes 14155784 | tf_op jit(solution)/shard_map/ppermute | solution.py:86
  5.5 24.4 %all-to-all-start = ((bf16[8,2,2,96,128]{4,3,2,1,0:T(8,128)(2,1)}), bf16[8,2,2,96,128]{4,3,2,1,0:T(8,128)(2,1)S(1)}, u32[]{:S(2)}, u32[]{:S(2)}) async-start(bf16[8,2,2,96,128]{4,3,2,1,0:T(8,128)(2,1)} %arrange.2), calls=%async_computation | async-start | bytes 1572864 | tf_op jit(solution)/shard_map/all_to_all | solution.py:90
  13.5 15.5 %collective-permute-start.2 = (s32[2,27]{1,0:T(2,128)S(1)}, s32[2,27]{1,0:T(2,128)S(1)}, u32[]{:S(2)}, u32[]{:S(2)}) collective-permute-start(s32[2,27]{1,0:T(2,128)S(1)} %copy-done.8), channel_id=1, source_target_pairs={{0,24},{1,25},{2,26},{3,27},{4,28},{5,29},{6,30},{7,31},{8,16},{9,... | collective-permute-start | bytes 656 | tf_op jit(solution)/shard_map/ppermute | solution.py:86
  19.4 9.7 %collective-permute-start.1 = (s32[2,27]{1,0:T(2,128)S(1)}, s32[2,27]{1,0:T(2,128)S(1)}, u32[]{:S(2)}, u32[]{:S(2)}) collective-permute-start(s32[2,27]{1,0:T(2,128)S(1)} %copy-done.8), channel_id=1, source_target_pairs={{0,16},{1,17},{2,18},{3,19},{4,20},{5,21},{6,22},{7,23},{8,24},{9,... | collective-permute-start | bytes 656 | tf_op jit(solution)/shard_map/ppermute | solution.py:86
  20.0 9.2 %collective-permute-start = (s32[2,27]{1,0:T(2,128)S(1)}, s32[2,27]{1,0:T(2,128)S(1)}, u32[]{:S(2)}, u32[]{:S(2)}) collective-permute-start(s32[2,27]{1,0:T(2,128)S(1)} %copy-done.8), channel_id=1, source_target_pairs={{0,8},{1,9},{2,10},{3,11},{4,12},{5,13},{6,14},{7,15},{8,0},{9,1},... | collective-permute-start | bytes 656 | tf_op jit(solution)/shard_map/ppermute | solution.py:86
  29.9 29.4 %copy-start.2 = (bf16[8,2,2,96,128]{4,3,2,1,0:T(8,128)(2,1)}, bf16[8,2,2,96,128]{4,3,2,1,0:T(8,128)(2,1)S(1)}, u32[]{:S(2)}) copy-start(bf16[8,2,2,96,128]{4,3,2,1,0:T(8,128)(2,1)S(1)} %all-to-all-done.refs_0_) | copy-start | bytes 2359300
  52.2 38.5 %all-to-all-start.1 = ((bf16[8,2,2,96,256]{4,3,2,1,0:T(8,128)(2,1)}), bf16[8,2,2,96,256]{4,3,2,1,0:T(8,128)(2,1)}, u32[]{:S(2)}, u32[]{:S(2)}) async-start(bf16[8,2,2,96,256]{4,3,2,1,0:T(8,128)(2,1)} %get-tuple-element.82), calls=%async_computation.1 | async-start | bytes 3145728 | tf_op jit(solution)/shard_map/all_to_all | solution.py:90
  56.5 8.1 %collective-permute-start.6 = (bf16[8,2,2,96,128]{4,3,2,1,0:T(8,128)(2,1)S(1)}, bf16[8,2,2,96,128]{4,3,2,1,0:T(8,128)(2,1)S(1)}, u32[]{:S(2)}, u32[]{:S(2)}) collective-permute-start(bf16[8,2,2,96,128]{4,3,2,1,0:T(8,128)(2,1)S(1)} %all-to-all-done.refs_0_), channel_id=1, source_target_pairs={{0,32},{1,33},{2,34},{3,35},{4,36},{5,37},{6,38},{7,39},{8,40},{9,... | collective-permute-start | bytes 2359304 | tf_op jit(solution)/shard_map/ppermute | solution.py:86
  56.6 33.2 %collective-permute-start.5 = (bf16[8,2,2,96,128]{4,3,2,1,0:T(8,128)(2,1)S(1)}, bf16[8,2,2,96,128]{4,3,2,1,0:T(8,128)(2,1)S(1)}, u32[]{:S(2)}, u32[]{:S(2)}) collective-permute-start(bf16[8,2,2,96,128]{4,3,2,1,0:T(8,128)(2,1)S(1)} %all-to-all-done.refs_0_), channel_id=1, source_target_pairs={{1,0},{2,1},{3,2},{4,3},{5,4},{6,5},{7,6},{9,8},{10,9},{11,10},{12... | collective-permute-start | bytes 2359304 | tf_op jit(solution)/shard_map/ppermute | solution.py:86
  59.3 31.3 %collective-permute-start.4 = (bf16[8,2,2,96,128]{4,3,2,1,0:T(8,128)(2,1)S(1)}, bf16[8,2,2,96,128]{4,3,2,1,0:T(8,128)(2,1)}, u32[]{:S(2)}, u32[]{:S(2)}) collective-permute-start(bf16[8,2,2,96,128]{4,3,2,1,0:T(8,128)(2,1)S(1)} %all-to-all-done.refs_0_), channel_id=1, source_target_pairs={{0,1},{1,2},{2,3},{3,4},{4,5},{5,6},{6,7},{8,9},{9,10},{10,11},{11... | collective-permute-start | bytes 2359304 | tf_op jit(solution)/shard_map/ppermute | solution.py:86
  64.6 25.2 %copy-start.5 = (bf16[8,2,2,96,128]{4,3,2,1,0:T(8,128)(2,1)}, bf16[8,2,2,96,128]{4,3,2,1,0:T(8,128)(2,1)S(1)}, u32[]{:S(2)}) copy-start(bf16[8,2,2,96,128]{4,3,2,1,0:T(8,128)(2,1)S(1)} %collective-permute-done.6.refs_1_) | copy-start | bytes 2359300
  89.8 0.9 copy-start.6
  90.7 54.3 %collective-permute-start.12 = (bf16[768,3072]{1,0:T(8,128)(2,1)}, bf16[768,3072]{1,0:T(8,128)(2,1)S(1)}, u32[]{:S(2)}, u32[]{:S(2)}) collective-permute-start(bf16[768,3072]{1,0:T(8,128)(2,1)} %refs_1_.3), channel_id=1, source_target_pairs={{0,80},{1,81},{2,82},{3,83},{4,84},{5,85},{6,86},{7,87},{8,88},{9,... | collective-permute-start | bytes 14155784 | tf_op jit(solution)/shard_map/ppermute | solution.py:86
  90.7 8.6 %collective-permute-start.10 = (bf16[8,2,2,96,128]{4,3,2,1,0:T(8,128)(2,1)}, bf16[8,2,2,96,128]{4,3,2,1,0:T(8,128)(2,1)S(1)}, u32[]{:S(2)}, u32[]{:S(2)}) collective-permute-start(bf16[8,2,2,96,128]{4,3,2,1,0:T(8,128)(2,1)} %collective-permute-done.4.refs_4_), channel_id=1, source_target_pairs={{0,32},{1,33},{2,34},{3,35},{4,36},{5,37},{6,38},{7,39},{8,40},{9,... | collective-permute-start | bytes 2359304 | tf_op jit(solution)/shard_map/ppermute | solution.py:86
  90.8 11.2 %collective-permute-start.9 = (bf16[8,2,2,96,256]{4,3,2,1,0:T(8,128)(2,1)}, bf16[8,2,2,96,256]{4,3,2,1,0:T(8,128)(2,1)}, u32[]{:S(2)}, u32[]{:S(2)}) collective-permute-start(bf16[8,2,2,96,256]{4,3,2,1,0:T(8,128)(2,1)} %all-to-all-done.1.refs_2_), channel_id=1, source_target_pairs={{0,32},{1,33},{2,34},{3,35},{4,36},{5,37},{6,38},{7,39},{8,40},{9,... | collective-permute-start | bytes 4718600 | tf_op jit(solution)/shard_map/ppermute | solution.py:86
  91.3 40.7 %collective-permute-start.8 = (bf16[8,2,2,96,256]{4,3,2,1,0:T(8,128)(2,1)}, bf16[8,2,2,96,256]{4,3,2,1,0:T(8,128)(2,1)}, u32[]{:S(2)}, u32[]{:S(2)}) collective-permute-start(bf16[8,2,2,96,256]{4,3,2,1,0:T(8,128)(2,1)} %all-to-all-done.1.refs_2_), channel_id=1, source_target_pairs={{1,0},{2,1},{3,2},{4,3},{5,4},{6,5},{7,6},{9,8},{10,9},{11,10},{12... | collective-permute-start | bytes 4718600 | tf_op jit(solution)/shard_map/ppermute | solution.py:86
  93.2 40.0 %collective-permute-start.7 = (bf16[8,2,2,96,256]{4,3,2,1,0:T(8,128)(2,1)}, bf16[8,2,2,96,256]{4,3,2,1,0:T(8,128)(2,1)}, u32[]{:S(2)}, u32[]{:S(2)}) collective-permute-start(bf16[8,2,2,96,256]{4,3,2,1,0:T(8,128)(2,1)} %all-to-all-done.1.refs_2_), channel_id=1, source_target_pairs={{0,1},{1,2},{2,3},{3,4},{4,5},{5,6},{6,7},{8,9},{9,10},{10,11},{11... | collective-permute-start | bytes 4718600 | tf_op jit(solution)/shard_map/ppermute | solution.py:86
  99.2 2.7 %copy-start.7 = (bf16[8,2,2,96,128]{4,3,2,1,0:T(8,128)(2,1)}, bf16[8,2,2,96,128]{4,3,2,1,0:T(8,128)(2,1)S(1)}, u32[]{:S(2)}) copy-start(bf16[8,2,2,96,128]{4,3,2,1,0:T(8,128)(2,1)S(1)} %collective-permute-done.10.refs_5_) | copy-start | bytes 2359300
  99.2 2.7 %collective-permute-start.11 = (bf16[8,2,2,96,128]{4,3,2,1,0:T(8,128)(2,1)}, bf16[8,2,2,96,128]{4,3,2,1,0:T(8,128)(2,1)}, u32[]{:S(2)}, u32[]{:S(2)}) collective-permute-start(bf16[8,2,2,96,128]{4,3,2,1,0:T(8,128)(2,1)} %copy-done.6), channel_id=1, source_target_pairs={{0,32},{1,33},{2,34},{3,35},{4,36},{5,37},{6,38},{7,39},{8,40},{9,... | collective-permute-start | bytes 2359304 | tf_op jit(solution)/shard_map/ppermute | solution.py:86
  145.0 31.5 %copy-start = (bf16[768,3072]{1,0:T(8,128)(2,1)}, bf16[768,3072]{1,0:T(8,128)(2,1)S(1)}, u32[]{:S(2)}) copy-start(bf16[768,3072]{1,0:T(8,128)(2,1)S(1)} %collective-permute-done.12.refs_4_.refs_5_) | copy-start | bytes 14155780
  145.0 3.6 %collective-permute-start.13 = (bf16[8,2,2,96,256]{4,3,2,1,0:T(8,128)(2,1)}, bf16[8,2,2,96,256]{4,3,2,1,0:T(8,128)(2,1)S(1)}, u32[]{:S(2)}, u32[]{:S(2)}) collective-permute-start(bf16[8,2,2,96,256]{4,3,2,1,0:T(8,128)(2,1)} %collective-permute-done.7.refs_1_), channel_id=1, source_target_pairs={{0,32},{1,33},{2,34},{3,35},{4,36},{5,37},{6,38},{7,39},{8,40},{9,... | collective-permute-start | bytes 4718600 | tf_op jit(solution)/shard_map/ppermute | solution.py:86
  145.0 5.9 %collective-permute-start.14 = (bf16[8,2,2,96,256]{4,3,2,1,0:T(8,128)(2,1)}, bf16[8,2,2,96,256]{4,3,2,1,0:T(8,128)(2,1)S(1)}, u32[]{:S(2)}, u32[]{:S(2)}) collective-permute-start(bf16[8,2,2,96,256]{4,3,2,1,0:T(8,128)(2,1)} %collective-permute-done.8.refs_3_), channel_id=1, source_target_pairs={{0,32},{1,33},{2,34},{3,35},{4,36},{5,37},{6,38},{7,39},{8,40},{9,... | collective-permute-start | bytes 4718600 | tf_op jit(solution)/shard_map/ppermute | solution.py:86
  148.6 1.2 copy-start.3
  150.9 1.1 copy-start.4
  152.0 24.5 %collective-permute-start.15 = (bf16[768,3072]{1,0:T(8,128)(2,1)S(1)}, bf16[768,3072]{1,0:T(8,128)(2,1)}, u32[]{:S(2)}, u32[]{:S(2)}) collective-permute-start(bf16[768,3072]{1,0:T(8,128)(2,1)S(1)} %collective-permute-done.12.refs_4_.refs_5_), channel_id=1, source_target_pairs={{0,32},{1,33},{2,34},{3,35},{4,36},{5,37},{6,38},{7,39},{8,40},{9,... | collective-permute-start | bytes 14155784 | tf_op jit(solution)/shard_map/ppermute | solution.py:86
  176.5 25.0 %all-to-all-start.3 = ((bf16[8,2,96,384]{3,2,1,0:T(8,128)(2,1)}), bf16[8,2,96,384]{3,2,1,0:T(8,128)(2,1)S(1)}, u32[]{:S(2)}, u32[]{:S(2)}) async-start(bf16[8,2,96,384]{3,2,1,0:T(8,128)(2,1)} %attend.3), calls=%async_computation.3 | async-start | bytes 2359296 | tf_op jit(solution)/shard_map/all_to_all | solution.py:90
  201.5 1.0 copy-start.1

commit v3 on v2

v3 whole, which is shorter than its diff:
```python
import functools

import jax
import jax.numpy as jnp
from jax import lax
from jax.experimental import pallas as pl
from jax.experimental.pallas import tpu as pltpu
from jax.sharding import Mesh, PartitionSpec as P

HEAD_DIM = 128
HEADS = 24
GROUPS = 8
GROUP_HEADS = HEADS // GROUPS
ROWS = 4
COLUMNS = 8
TIMES = 2
PART = 96
D = HEADS * HEAD_DIM
NEIGH = 27
COEF = HEAD_DIM ** (-0.5) * 1.4426950408889634
LOW = -1e30
TILE = 4 * PART
CELL = TIMES * TILE
PAIRS = 10
ALL = tuple(range(GROUP_HEADS))
QUARTER = 2 * PART
ATT_VMEM = 32
PROJ_VMEM = 58

AXES = ("yl", "c", "yh", "zh", "zl", "x")
SIZES = (2, 2, 2, 2, 2, 4)
COLUMN_AXES = ("yh", "zh", "yl")


def places():
    for flat in range(128):
        left, coords = flat, []
        for size in reversed(SIZES):
            coords.append(left % size)
            left //= size
        yield flat, tuple(reversed(coords))


def flat_of(coords):
    flat = 0
    for coord, size in zip(coords, SIZES):
        flat = flat * size + coord
    return flat


def route(target):
    pairs = []
    for flat, coords in places():
        to = target(*coords)
        if to is not None:
            pairs.append((flat, flat_of(to)))
    return pairs


def column_step(step):
    def target(yl, c, yh, zh, zl, x):
        column = zl * 4 + x + step
        if not 0 <= column < COLUMNS:
            return None
        return (yl, c, yh, zh, column // 4, column % 4)

    return target


def y_step(step):
    def target(yl, c, yh, zh, zl, x):
        y = (yh * 2 + yl + step) % 4
        return (y % 2, c, y // 2, zh, zl, x)

    return target


RIGHT = route(column_step(1))
LEFT = route(column_step(-1))
FAR = route(lambda yl, c, yh, zh, zl, x: y_step(1 if c else -1)(yl, c, yh, zh, zl, x))
FLIP_Z = route(lambda yl, c, yh, zh, zl, x: (yl, c, yh, 1 - zh, zl, x))
FLIP_Y = route(lambda yl, c, yh, zh, zl, x: (yl, c, 1 - yh, zh, zl, x))
FLIP_BOTH = route(lambda yl, c, yh, zh, zl, x: (yl, c, 1 - yh, 1 - zh, zl, x))
OTHER_CORE = route(lambda yl, c, yh, zh, zl, x: (yl, 1 - c, yh, zh, zl, x))


def permute(array, pairs):
    return lax.ppermute(array, AXES, pairs)


def exchange(array):
    return lax.all_to_all(array, COLUMN_AXES, 0, 0)


def arrange(*arrays):
    ins, outs, shapes, count = [], [], [], []
    for stack, heads in arrays:
        lanes = len(heads) * HEAD_DIM
        inner = (TIMES, PART, lanes) if len(stack) == 1 else (len(stack), TIMES, PART, lanes)
        shapes.append(jax.ShapeDtypeStruct((GROUPS,) + inner, jnp.bfloat16))
        outs.append(pl.BlockSpec((1,) + inner, lambda g, size=len(inner): (g,) + (0,) * size))
        for array in stack:
            ins.append(array)
        count.append((len(stack), heads))

    def kernel(*refs):
        at = 0
        for out_ref, (size, heads) in zip(refs[len(ins) :], count):
            lanes = pl.ds(heads[0] * HEAD_DIM, len(heads) * HEAD_DIM)
            for which in range(size):
                value = refs[at][:, :, lanes]
                if size == 1:
                    out_ref[0] = value
                else:
                    out_ref[0, which] = value
                at += 1

    block = pl.BlockSpec((TIMES, PART, GROUP_HEADS * HEAD_DIM), lambda g: (0, 0, g))
    return pl.pallas_call(
        kernel,
        grid=(GROUPS,),
        in_specs=[block] * len(ins),
        out_specs=outs,
        out_shape=shapes,
        compiler_params=pltpu.CompilerParams(vmem_limit_bytes=58 * 1024 * 1024),
        name="arrange",
    )(*ins)


def attend_kernel(plan, lists, q_ref, *refs):
    sides, taken, last = plan
    kv_refs, refs = refs[:2], refs[2:]
    state_in, refs = refs[:taken], refs[taken:]
    if last:
        o_ref, m_ref, l_ref, acc_ref = refs[:4]
    else:
        m_ref, l_ref, acc_ref = refs[:3]
    kv_ref, vt_ref, qt_ref, s_refs, p_refs, top_refs, factor_refs, sems = refs[-8:]
    heads = kv_ref.shape[0]

    def load(head, which):
        lanes = pl.ds(head * HEAD_DIM, HEAD_DIM)
        return [
            pltpu.make_async_copy(
                kv_refs[side].at[:, which, :, :, lanes], kv_ref.at[head, which, side], sems.at[head, which, side]
            )
            for side in range(2)
        ]

    for head in range(heads):
        for which in range(2):
            for copy in load(head, which):
                copy.start()

    if taken:
        for ref, given in zip((m_ref, l_ref, acc_ref), state_in):
            ref[...] = given[...]
    else:
        m_ref[...] = jnp.full(m_ref.shape, LOW, jnp.float32)
        l_ref[...] = jnp.zeros(l_ref.shape, jnp.float32)
        acc_ref[...] = jnp.zeros(acc_ref.shape, jnp.float32)
    for head in range(heads):
        lanes = slice(head * HEAD_DIM, (head + 1) * HEAD_DIM)
        for row in range(ROWS):
            q = [q_ref[2 * row : 2 * row + 2, t, :, lanes].reshape(QUARTER, HEAD_DIM) for t in range(TIMES)]
            qt_ref[head * ROWS + row] = jnp.concatenate(q, axis=0).T
    for part in range(2):
        factor_refs[part][...] = jnp.ones(factor_refs[part].shape, jnp.float32)
        p_refs[part][...] = jnp.zeros(p_refs[part].shape, jnp.bfloat16)
    first = lax.broadcasted_iota(jnp.int32, (1, TILE), 1) < QUARTER

    def cell(which, head, key_row):
        parts = []
        for side in range(2):
            for t2 in range(TIMES):
                for yl in range(2):
                    parts.append(kv_ref[head, which, side, 2 * key_row + yl, t2])
        return jnp.concatenate(parts, axis=0)

    def turn(head):
        def body(key_row, carry):
            vt_ref[head * ROWS + key_row] = cell(1, head, key_row).T
            return carry

        lax.fori_loop(0, ROWS, body, 0)

    def place(at):
        row, step = (at + 1) // 3, (at + 1) % 3
        return row, row + step - 1, step

    def score(head, at):
        row, key_row, step = place(at)
        s_ref, top_ref = s_refs[at % 2], top_refs[at % 2]
        s = jnp.dot(cell(0, head, key_row), qt_ref[head * ROWS + row], preferred_element_type=jnp.float32)
        s_ref[...] = s
        for part in range(4):
            rows = s[part * QUARTER : (part + 1) * QUARTER]
            top_ref[part] = jnp.max(rows.reshape(QUARTER // 8, 8, TILE), axis=0)

    def weigh(head, at):
        row, key_row, step = place(at)
        s_ref, top_ref, p_ref = s_refs[at % 2], top_refs[at % 2], p_refs[at % 2]
        spot = head * ROWS + row
        start = (lists[ROWS * TIMES * NEIGH] ^ row) * (TIMES * NEIGH) + step * 3
        oks = []
        for side in range(2):
            for t2 in range(TIMES):
                entry = start + (sides[side] + 1)
                use = [lists[entry + (t * NEIGH + (t2 - t + 1) * 9)] for t in range(TIMES)]
                oks.append(jnp.where(first, use[0], use[1]) >= 0)
        m_old = m_ref[spot]
        best = m_old
        for part in range(4):
            top = jnp.max(top_ref[part], axis=0, keepdims=True)
            best = jnp.maximum(best, jnp.where(oks[part], top, LOW))
        m_ref[spot] = best
        factor = jnp.exp2((m_old - best) * COEF)
        factor_refs[at % 2][...] = factor
        l = l_ref[spot] * factor
        shifts = [jnp.where(ok, best * COEF, -LOW) for ok in oks]
        for piece in range(8):
            rows = slice(piece * PART, (piece + 1) * PART)
            p = jnp.exp2(s_ref[rows] * COEF - shifts[piece // 2])
            l = l + jnp.sum(p.reshape(PART // 8, 8, TILE), axis=0)
            p_ref[rows] = p.astype(jnp.bfloat16)
        l_ref[spot] = l

    def absorb(head, at):
        row, key_row, step = place(at)
        spot = head * ROWS + row
        update = jnp.dot(vt_ref[head * ROWS + key_row], p_refs[at % 2][...], preferred_element_type=jnp.float32)
        acc_ref[spot] = acc_ref[spot] * factor_refs[at % 2][...] + update

    for copy in load(0, 0):
        copy.wait()
    score(0, 0)
    score(0, 1)

    def per_head(index, carry):
        for head in range(heads):

            @pl.when(index == head)
            def _(head=head):
                for copy in load(head, 1):
                    copy.wait()
                if head + 1 < heads:
                    for copy in load(head + 1, 0):
                        copy.wait()

        turn(index)
        before, following = jnp.maximum(index - 1, 0), jnp.minimum(index + 1, heads - 1)
        for at in range(PAIRS):
            if at < 2:
                absorb(before, at + PAIRS - 2)
            else:
                absorb(index, at - 2)
            weigh(index, at)
            if at + 2 < PAIRS:
                score(index, at + 2)
            else:
                score(following, at + 2 - PAIRS)
        return carry

    lax.fori_loop(0, heads, per_head, 0)
    absorb(heads - 1, PAIRS - 2)
    absorb(heads - 1, PAIRS - 1)
    if last:
        for head in range(heads):
            lanes = slice(head * HEAD_DIM, (head + 1) * HEAD_DIM)
            for row in range(ROWS):
                spot = head * ROWS + row
                out = (acc_ref[spot] / jnp.sum(l_ref[spot], axis=0, keepdims=True)).T.astype(jnp.bfloat16)
                for t in range(TIMES):
                    rows = out[t * QUARTER : (t + 1) * QUARTER].reshape(2, PART, HEAD_DIM)
                    o_ref[2 * row : 2 * row + 2, t, :, lanes] = rows


def attend(lists, q, blocks, sides, state=(), last=False):
    heads = q.shape[-1] // HEAD_DIM
    spots = heads * ROWS
    state_shapes = [(spots, 1, TILE), (spots, 8, TILE), (spots, HEAD_DIM, TILE)]
    vmem, anywhere = pl.BlockSpec(memory_space=pltpu.VMEM), pl.BlockSpec(memory_space=pl.ANY)
    scratch = []
    if last:
        shapes = [jax.ShapeDtypeStruct(q.shape, jnp.bfloat16)]
        scratch = [pltpu.VMEM(shape, jnp.float32) for shape in state_shapes]
    else:
        shapes = [jax.ShapeDtypeStruct(shape, jnp.float32) for shape in state_shapes]
    return pl.pallas_call(
        functools.partial(attend_kernel, (sides, len(state), last)),
        in_specs=[pl.BlockSpec(memory_space=pltpu.SMEM), vmem] + [anywhere] * 2 + [vmem] * len(state),
        out_specs=[vmem] * len(shapes),
        scratch_shapes=scratch
        + [
            pltpu.VMEM((heads, 2, 2, GROUPS, TIMES, PART, HEAD_DIM), jnp.bfloat16),
            pltpu.VMEM((spots, HEAD_DIM, CELL), jnp.bfloat16),
            pltpu.VMEM((spots, HEAD_DIM, TILE), jnp.bfloat16),
            [pltpu.VMEM((CELL, TILE), jnp.float32)] * 2,
            [pltpu.VMEM((CELL, TILE), jnp.bfloat16)] * 2,
            [pltpu.VMEM((4, 8, TILE), jnp.float32)] * 2,
            [pltpu.VMEM((1, TILE), jnp.float32)] * 2,
            pltpu.SemaphoreType.DMA((heads, 2, 2)),
        ],
        out_shape=shapes,
        compiler_params=pltpu.CompilerParams(vmem_limit_bytes=ATT_VMEM * 1024 * 1024),
        cost_estimate=pl.CostEstimate(
            flops=heads * PAIRS * 384 * 768 * 128 * 4,
            bytes_accessed=heads * 2 * 786432,
            transcendentals=heads * PAIRS * 384 * 768,
        ),
        name="attend",
    )(lists, q, *blocks, *state)


def project_kernel(ids, att_ref, *refs):
    w_refs, o_ref = refs[:-1], refs[-1]
    total = None
    for shard in range(4):
        for part in range(2):
            rows = att_ref[ids[shard] * 2 + part].reshape(TIMES * PART, GROUP_HEADS * HEAD_DIM)
            term = jnp.dot(rows, w_refs[2 * shard + part][...], preferred_element_type=jnp.float32)
            total = term if total is None else total + term
    o_ref[...] = total.astype(jnp.bfloat16).reshape(TIMES, PART, total.shape[1])


def project(ids, att, *shards):
    block = 512
    rows = D // GROUPS
    specs, pieces = [pl.BlockSpec(att.shape, lambda n, s: (0, 0, 0, 0))], []
    for shard in shards:
        for part in range(2):
            specs.append(pl.BlockSpec((rows, block), lambda n, s, part=part: (part, n)))
            pieces.append(shard)
    return pl.pallas_call(
        project_kernel,
        grid_spec=pltpu.PrefetchScalarGridSpec(
            num_scalar_prefetch=1,
            grid=(D // block,),
            in_specs=specs,
            out_specs=pl.BlockSpec((TIMES, PART, block), lambda n, s: (0, 0, n)),
        ),
        out_shape=jax.ShapeDtypeStruct((TIMES, PART, D), jnp.bfloat16),
        compiler_params=pltpu.CompilerParams(vmem_limit_bytes=PROJ_VMEM * 1024 * 1024),
        cost_estimate=pl.CostEstimate(
            flops=2 * TIMES * PART * D * D, bytes_accessed=2 * D * D, transcendentals=0
        ),
        name="project",
    )(ids, att, *pieces)


def on_device(queries, keys, values, neighbours, w_out):
    live = {"w": w_out, "near": neighbours, "queries": queries, "keys": keys, "values": values}

    def fence():
        names = list(live)
        for name, value in zip(names, lax.optimization_barrier([live[name] for name in names])):
            live[name] = value

    def swap(name):
        live[name + "_other"] = permute(live[name], OTHER_CORE)

    def work(left, right, state=(), last=False):
        blocks = [live[left[0]], live[right[0]]]
        return attend(live["lists"], live["q"], blocks, (left[1], right[1]), state, last)

    (live["q"],) = arrange(((live.pop("queries"),), ALL))
    fence()
    live["q"] = exchange(live["q"])
    (live["kv"],) = arrange(((live.pop("keys"), live.pop("values")), ALL))
    row = lax.axis_index("yh") * 2 + lax.axis_index("zh")
    flips = [live["near"].reshape(-1)]
    for pairs in (FLIP_Z, FLIP_Y, FLIP_BOTH):
        flips.append(permute(live["near"], pairs).reshape(-1))
    live["lists"] = jnp.concatenate(flips + [row.astype(jnp.int32).reshape(1)])
    fence()
    live["kv"] = exchange(live["kv"])
    swap("w")
    fence()
    live["left"], live["right"] = permute(live["kv"], RIGHT), permute(live["kv"], LEFT)
    swap("kv")
    live["far"] = permute(live["w"], FAR)
    state = work(("kv", 0), ("kv_other", 0))
    for at in range(3):
        live["state", at] = state[at]
    fence()
    swap("left")
    swap("right")
    state = work(("left", -1), ("right", 1), [live.pop(("state", at)) for at in range(3)])
    for at in range(3):
        live["state", at] = state[at]
    fence()
    swap("far")
    (live["att"],) = work(("left_other", -1), ("right_other", 1), [live.pop(("state", at)) for at in range(3)], True)
    fence()
    att = exchange(live["att"])
    yl, c = lax.axis_index("yl"), lax.axis_index("c")
    ids = jnp.stack([2 * yl + c, 2 * yl + 1 - c, 2 * (1 - yl) + c, 2 * (1 - yl) + 1 - c]).astype(jnp.int32)
    return project(ids, att, live["w"], live["w_other"], live["far"], live["far_other"])


def solution(mesh):
    fine = Mesh(mesh.devices.reshape(SIZES), AXES)
    tile, head = ("yh", "zh", "zl", "x"), ("yl", "c")
    placed = (
        P(tile, head, None),
        P(tile, head, None),
        P(tile, head, None),
        P(tile, None),
        P(head, None),
    )
    return jax.shard_map(
        on_device, mesh=fine, in_specs=placed, out_specs=P(tile, head, None), check_vma=False
    )
```

time: 217 us -> 200 us (0.922)
  starting transfers between devices: 41.6 us -> 26.5 us
  blocking collectives: 22.2 us -> 35.1 us
  Pallas kernels: 77.3 us -> 66.5 us
    all_to_all x1, blocking collectives: 22.2 us -> 35.1 us  [exchange(): return lax.all_to_all(array, COLUMN_AXES, 0, 0)]
    pallas_call x2 -> x3, Pallas kernels: 53.3 us -> 43 us  [attend(): pl.pallas_call(functools.partial(attend_kernel, (sides, len(state), last)...]
    ppermute x16 -> x11, starting transfers between devices: 23.9 us -> 14.4 us  [permute(): return lax.ppermute(array, AXES, pairs)]
    all_to_all x3 -> x2, starting transfers between devices: 17.8 us -> 12.1 us  [exchange(): return lax.all_to_all(array, COLUMN_AXES, 0, 0)]
    all_to_all x3 -> x2, waiting for transfers between devices: 18.8 us -> 18.6 us  [exchange(): return lax.all_to_all(array, COLUMN_AXES, 0, 0)]
    ppermute x16 -> x11, waiting for transfers between devices: 48.7 us -> 48.7 us  [permute(): return lax.ppermute(array, AXES, pairs)]
  transfers between devices with their start and end apart: 19 -> 13, of which waited for: 9 -> 5; matrix products, arithmetic and copies ran while one was open for 1% -> 1% of each run, Pallas kernels for 28% -> 25%
where the time goes in v3:
time: 200 us
  waiting for transfers between devices  67.2 us (34%)
  Pallas kernels  66.5 us (33%)
  blocking collectives  35.1 us (18%)
  starting transfers between devices  26.5 us (13%)
  local copies, waits for them, and re-layouts  3.55 us (2%)
    ppermute x11, waiting for transfers between devices, permute(): return lax.ppermute(array, AXES, pairs)  48.7 us
    pallas_call x3, Pallas kernels, attend(): pl.pallas_call(functools.partial(attend_kernel, (sides, len(state), last)...  43 us
    all_to_all x1, blocking collectives, exchange(): return lax.all_to_all(array, COLUMN_AXES, 0, 0)  35.1 us
    all_to_all x2, waiting for transfers between devices, exchange(): return lax.all_to_all(array, COLUMN_AXES, 0, 0)  18.6 us
    ppermute x11, starting transfers between devices, permute(): return lax.ppermute(array, AXES, pairs)  14.4 us
    pallas_call x1, Pallas kernels, project(): pl.pallas_call(project_kernel, grid_spec=pltpu.PrefetchScalarGridSpec(num...  12.3 us
    all_to_all x2, starting transfers between devices, exchange(): return lax.all_to_all(array, COLUMN_AXES, 0, 0)  12.1 us
    pallas_call x2, Pallas kernels, arrange(): pl.pallas_call(kernel, grid=(GROUPS,), in_specs=[block] * len(ins), out_s...  11.2 us
  transfers between devices with their start and end apart: 13, of which 5 were waited for; matrix products, arithmetic and copies ran while one was open for 1% of the time, Pallas kernels for 25%

profile of v3, /device:TPU:6, one launch (start us, length us, event | category | flops | bytes accessed | tf_op | source)
XLA Modules:
  0.0 199.7 jit_solution(4798541787277460096)
XLA Ops:
  0.0 0.0 copy-start.3
  0.0 5.3 %arrange.2 = bf16[8,2,96,384]{3,2,1,0:T(8,128)(2,1)} custom-call(bf16[2,96,3072]{2,1,0:T(8,128)(2,1)} %refs_0_.1), custom_call_target="tpu_custom_call" | custom-call | tf_op jit(solution)/shard_map/arrange/pallas_call | solution.py:119
  5.3 7.8 %all-to-all-start = ((bf16[8,2,96,384]{3,2,1,0:T(8,128)(2,1)}), bf16[8,2,96,384]{3,2,1,0:T(8,128)(2,1)S(1)}, u32[]{:S(2)}, u32[]{:S(2)}) async-start(bf16[8,2,96,384]{3,2,1,0:T(8,128)(2,1)} %arrange.2), calls=%async_computation | async-start | bytes 2359296 | tf_op jit(solution)/shard_map/all_to_all | solution.py:92
  13.0 0.0 copy-done.3
  13.0 3.5 %collective-permute-start = (s32[2,27]{1,0:T(2,128)S(1)}, s32[2,27]{1,0:T(2,128)S(1)}, u32[]{:S(2)}, u32[]{:S(2)}) collective-permute-start(s32[2,27]{1,0:T(2,128)S(1)} %copy-done.3), channel_id=1, source_target_pairs={{0,8},{1,9},{2,10},{3,11},{4,12},{5,13},{6,14},{7,15},{8,0},{9,1},... | collective-permute-start | bytes 656 | tf_op jit(solution)/shard_map/ppermute | solution.py:88
  16.6 3.0 %collective-permute-start.1 = (s32[2,27]{1,0:T(2,128)S(1)}, s32[2,27]{1,0:T(2,128)S(1)}, u32[]{:S(2)}, u32[]{:S(2)}) collective-permute-start(s32[2,27]{1,0:T(2,128)S(1)} %copy-done.3), channel_id=1, source_target_pairs={{0,16},{1,17},{2,18},{3,19},{4,20},{5,21},{6,22},{7,23},{8,24},{9,... | collective-permute-start | bytes 656 | tf_op jit(solution)/shard_map/ppermute | solution.py:88
  19.5 0.1 collective-permute-start.2
  19.6 0.1 reshape.15
  19.7 5.9 %arrange.3 = bf16[8,2,2,96,384]{4,3,2,1,0:T(8,128)(2,1)} custom-call(bf16[2,96,3072]{2,1,0:T(8,128)(2,1)} %refs_0_.2, bf16[2,96,3072]{2,1,0:T(8,128)(2,1)} %refs_1_), custom_call_target="tpu_custom_call" | custom-call | tf_op jit(solution)/shard_map/arrange/pallas_call | solution.py:119
  25.6 0.0 collective-permute-done
  25.6 0.1 reshape.16
  25.7 5.7 %collective-permute-done.1 = s32[2,27]{1,0:T(2,128)S(1)} collective-permute-done((s32[2,27]{1,0:T(2,128)S(1)}, s32[2,27]{1,0:T(2,128)S(1)}, u32[]{:S(2)}, u32[]{:S(2)}) %collective-permute-start.1) | collective-permute-done | bytes 248 | tf_op jit(solution)/shard_map/ppermute | solution.py:88
  31.4 0.1 reshape.17
  31.4 2.3 %collective-permute-done.2 = s32[2,27]{1,0:T(2,128)S(1)} collective-permute-done((s32[2,27]{1,0:T(2,128)S(1)}, s32[2,27]{1,0:T(2,128)S(1)}, u32[]{:S(2)}, u32[]{:S(2)}) %collective-permute-start.2) | collective-permute-done | bytes 248 | tf_op jit(solution)/shard_map/ppermute | solution.py:88
  33.7 0.1 reshape.18
  33.8 0.1 concatenate.3.lists
  33.9 0.0 all-to-all-done.q_ref
  33.9 0.0 collective-permute-start.3
  34.0 35.1 %all_to_all.15.refs_0_ = bf16[8,2,2,96,384]{4,3,2,1,0:T(8,128)(2,1)S(1)} all-to-all(bf16[8,2,2,96,384]{4,3,2,1,0:T(8,128)(2,1)} %arrange.3), channel_id=1, replica_groups=mesh['yl'=2,'c'=2,'yh'=2,'zh'=2,'zl'=2,'x'=4] {'yh','zh','yl'}, dimensions={0} | all-to-all | bytes 4718592 | tf_op jit(solution)/shard_map/all_to_all | solution.py:92
  69.1 0.0 collective-permute-done.3.refs_2_.refs_3_
  69.1 0.0 copy-start
  69.1 2.1 %copy-done = bf16[768,3072]{1,0:T(8,128)(2,1)} copy-done((bf16[768,3072]{1,0:T(8,128)(2,1)}, bf16[768,3072]{1,0:T(8,128)(2,1)S(1)}, u32[]{:S(2)}) %copy-start) | copy-done | bytes 4718616
  71.2 1.1 collective-permute-start.7
  72.3 0.0 collective-permute-start.6
  72.3 2.8 %collective-permute-start.4 = (bf16[8,2,2,96,384]{4,3,2,1,0:T(8,128)(2,1)S(1)}, bf16[8,2,2,96,384]{4,3,2,1,0:T(8,128)(2,1)S(1)}, u32[]{:S(2)}, u32[]{:S(2)}) collective-permute-start(bf16[8,2,2,96,384]{4,3,2,1,0:T(8,128)(2,1)S(1)} %all_to_all.15.refs_0_), channel_id=1, source_target_pairs={{0,1},{1,2},{2,3},{3,4},{4,5},{5,6},{6,7},{8,9},{9,10},{10,11},{11... | collective-permute-start | bytes 7077896 | tf_op jit(solution)/shard_map/ppermute | solution.py:88
  75.2 3.0 %collective-permute-start.5 = (bf16[8,2,2,96,384]{4,3,2,1,0:T(8,128)(2,1)S(1)}, bf16[8,2,2,96,384]{4,3,2,1,0:T(8,128)(2,1)S(1)}, u32[]{:S(2)}, u32[]{:S(2)}) collective-permute-start(bf16[8,2,2,96,384]{4,3,2,1,0:T(8,128)(2,1)S(1)} %all_to_all.15.refs_0_), channel_id=1, source_target_pairs={{1,0},{2,1},{3,2},{4,3},{5,4},{6,5},{7,6},{9,8},{10,9},{11,10},{12... | collective-permute-start | bytes 7077896 | tf_op jit(solution)/shard_map/ppermute | solution.py:88
  78.2 0.0 collective-permute-done.6.refs_1_
  78.2 13.7 %attend.3 = (f32[12,1,384]{2,1,0:T(1,128)S(1)}, f32[12,8,384]{2,1,0:T(8,128)S(1)}, f32[12,128,384]{2,1,0:T(8,128)S(1)}) custom-call(s32[217]{0:T(256)S(1)} %concatenate.3.lists, bf16[8,2,96,384]{3,2,1,0:T(8,128)(2,1)S(1)} %all-to-all-done.q_ref, bf16[8,2,2,96,384]{4,3,2,1,0:T(8,128)(2,1)S(1)} %all_to_all.15.refs_0_, ...), custom_call_target="tpu_custom_call" | custom-call | flops 4529848320 | bytes 4718592 | tf_op jit(solution)/shard_map/attend/pallas_call | solution.py:289
  91.9 36.0 %collective-permute-done.4.refs_0_ = bf16[8,2,2,96,384]{4,3,2,1,0:T(8,128)(2,1)S(1)} collective-permute-done((bf16[8,2,2,96,384]{4,3,2,1,0:T(8,128)(2,1)S(1)}, bf16[8,2,2,96,384]{4,3,2,1,0:T(8,128)(2,1)S(1)}, u32[]{:S(2)}, u32[]{:S(2)}) %collective-permute-start.4) | collective-permute-done | bytes 2359328 | tf_op jit(solution)/shard_map/ppermute | solution.py:88
  127.9 4.7 %collective-permute-done.5.refs_1_ = bf16[8,2,2,96,384]{4,3,2,1,0:T(8,128)(2,1)S(1)} collective-permute-done((bf16[8,2,2,96,384]{4,3,2,1,0:T(8,128)(2,1)S(1)}, bf16[8,2,2,96,384]{4,3,2,1,0:T(8,128)(2,1)S(1)}, u32[]{:S(2)}, u32[]{:S(2)}) %collective-permute-start.5) | collective-permute-done | bytes 2359328 | tf_op jit(solution)/shard_map/ppermute | solution.py:88
  132.6 0.0 collective-permute-done.7.refs_4_.refs_5_
  132.6 0.0 copy-start.1
  132.6 0.0 collective-permute-start.8
  132.6 0.5 collective-permute-start.9
  133.1 13.9 %attend.4 = (f32[12,1,384]{2,1,0:T(1,128)S(1)}, f32[12,8,384]{2,1,0:T(8,128)S(1)}, f32[12,128,384]{2,1,0:T(8,128)S(1)}) custom-call(s32[217]{0:T(256)S(1)} %concatenate.3.lists, bf16[8,2,96,384]{3,2,1,0:T(8,128)(2,1)S(1)} %all-to-all-done.q_ref, bf16[8,2,2,96,384]{4,3,2,1,0:T(8,128)(2,1)S(1)} %collective-permute-done.4.refs_0_, ...), custom_call_target="tpu_custom_call" | custom-call | flops 4529848320 | bytes 4718592 | tf_op jit(solution)/shard_map/attend/pallas_call | solution.py:289
  147.0 0.0 collective-permute-done.8.refs_0_
  147.0 0.0 collective-permute-done.9.refs_1_
  147.0 0.0 copy-done.1
  147.0 0.3 collective-permute-start.10
  147.4 15.5 %attend.5 = bf16[8,2,96,384]{3,2,1,0:T(8,128)(2,1)} custom-call(s32[217]{0:T(256)S(1)} %concatenate.3.lists, bf16[8,2,96,384]{3,2,1,0:T(8,128)(2,1)S(1)} %all-to-all-done.q_ref, bf16[8,2,2,96,384]{4,3,2,1,0:T(8,128)(2,1)S(1)} %collective-permute-done.8.refs_0_, bf16[8,2,2,96,384]{4,3,2,1,0:T(8,128)(2,1)S(1)} %collective-permute-done.9.refs_1_, ...), custom_call_target="tpu_custom_call" | custom-call | flops 4529848320 | bytes 4718592 | tf_op jit(solution)/shard_map/attend/pallas_call | solution.py:289
  162.8 0.0 collective-permute-done.10.refs_6_.refs_7_
  162.9 4.3 %all-to-all-start.2 = ((bf16[8,2,96,384]{3,2,1,0:T(8,128)(2,1)}), bf16[8,2,96,384]{3,2,1,0:T(8,128)(2,1)S(1)}, u32[]{:S(2)}, u32[]{:S(2)}) async-start(bf16[8,2,96,384]{3,2,1,0:T(8,128)(2,1)} %attend.5), calls=%async_computation.2 | async-start | bytes 2359296 | tf_op jit(solution)/shard_map/all_to_all | solution.py:92
  167.1 0.6 pad_add_fusion.ids
  167.7 18.6 %all-to-all-done.2.att_ref = bf16[8,2,96,384]{3,2,1,0:T(8,128)(2,1)S(1)} async-done(((bf16[8,2,96,384]{3,2,1,0:T(8,128)(2,1)}), bf16[8,2,96,384]{3,2,1,0:T(8,128)(2,1)S(1)}, u32[]{:S(2)}, u32[]{:S(2)}) %all-to-all-start.2) | async-done | bytes 1179680 | tf_op jit(solution)/shard_map/all_to_all | solution.py:92
  186.3 0.0 copy-start.2
  186.3 1.0 copy-done.2
  187.3 12.3 %project.1 = bf16[2,96,3072]{2,1,0:T(8,128)(2,1)} custom-call(s32[4]{0:T(128)} %pad_add_fusion.ids, bf16[8,2,96,384]{3,2,1,0:T(8,128)(2,1)} %copy-done.2, bf16[768,3072]{1,0:T(8,128)(2,1)} %refs_1_.1, bf16[768,3072]{1,0:T(8,128)(2,1)} %refs_1_.1, bf16[768,3072]{1,0:T(8,128)(2,1)} %copy-done, bf16[768,3072]{1,0:T(8,128)(2,1)} %copy-done, ...), custom_call_target="tpu_custom_call" | custom-call | flops 3623878656 | bytes 18874368 | tf_op jit(solution)/shard_map/project/pallas_call | solution.py:334
Async XLA Ops:
  0.0 13.0 %copy-start.3 = (s32[2,27]{1,0:T(2,128)S(1)}, s32[2,27]{1,0:T(2,128)}, u32[]{:S(2)}) copy-start(s32[2,27]{1,0:T(2,128)} %param.8) | copy-start | bytes 652
  5.3 28.6 %all-to-all-start = ((bf16[8,2,96,384]{3,2,1,0:T(8,128)(2,1)}), bf16[8,2,96,384]{3,2,1,0:T(8,128)(2,1)S(1)}, u32[]{:S(2)}, u32[]{:S(2)}) async-start(bf16[8,2,96,384]{3,2,1,0:T(8,128)(2,1)} %arrange.2), calls=%async_computation | async-start | bytes 2359296 | tf_op jit(solution)/shard_map/all_to_all | solution.py:92
  13.0 12.6 %collective-permute-start = (s32[2,27]{1,0:T(2,128)S(1)}, s32[2,27]{1,0:T(2,128)S(1)}, u32[]{:S(2)}, u32[]{:S(2)}) collective-permute-start(s32[2,27]{1,0:T(2,128)S(1)} %copy-done.3), channel_id=1, source_target_pairs={{0,8},{1,9},{2,10},{3,11},{4,12},{5,13},{6,14},{7,15},{8,0},{9,1},... | collective-permute-start | bytes 656 | tf_op jit(solution)/shard_map/ppermute | solution.py:88
  16.6 14.8 %collective-permute-start.1 = (s32[2,27]{1,0:T(2,128)S(1)}, s32[2,27]{1,0:T(2,128)S(1)}, u32[]{:S(2)}, u32[]{:S(2)}) collective-permute-start(s32[2,27]{1,0:T(2,128)S(1)} %copy-done.3), channel_id=1, source_target_pairs={{0,16},{1,17},{2,18},{3,19},{4,20},{5,21},{6,22},{7,23},{8,24},{9,... | collective-permute-start | bytes 656 | tf_op jit(solution)/shard_map/ppermute | solution.py:88
  19.5 14.2 %collective-permute-start.2 = (s32[2,27]{1,0:T(2,128)S(1)}, s32[2,27]{1,0:T(2,128)S(1)}, u32[]{:S(2)}, u32[]{:S(2)}) collective-permute-start(s32[2,27]{1,0:T(2,128)S(1)} %copy-done.3), channel_id=1, source_target_pairs={{0,24},{1,25},{2,26},{3,27},{4,28},{5,29},{6,30},{7,31},{8,16},{9,... | collective-permute-start | bytes 656 | tf_op jit(solution)/shard_map/ppermute | solution.py:88
  33.9 35.2 %collective-permute-start.3 = (bf16[768,3072]{1,0:T(8,128)(2,1)}, bf16[768,3072]{1,0:T(8,128)(2,1)S(1)}, u32[]{:S(2)}, u32[]{:S(2)}) collective-permute-start(bf16[768,3072]{1,0:T(8,128)(2,1)} %refs_1_.1), channel_id=1, source_target_pairs={{0,32},{1,33},{2,34},{3,35},{4,36},{5,37},{6,38},{7,39},{8,40},{9,... | collective-permute-start | bytes 14155784 | tf_op jit(solution)/shard_map/ppermute | solution.py:88
  69.1 2.1 %copy-start = (bf16[768,3072]{1,0:T(8,128)(2,1)}, bf16[768,3072]{1,0:T(8,128)(2,1)S(1)}, u32[]{:S(2)}) copy-start(bf16[768,3072]{1,0:T(8,128)(2,1)S(1)} %collective-permute-done.3.refs_2_.refs_3_) | copy-start | bytes 14155780
  71.2 61.4 %collective-permute-start.7 = (bf16[768,3072]{1,0:T(8,128)(2,1)}, bf16[768,3072]{1,0:T(8,128)(2,1)S(1)}, u32[]{:S(2)}, u32[]{:S(2)}) collective-permute-start(bf16[768,3072]{1,0:T(8,128)(2,1)} %refs_1_.1), channel_id=1, source_target_pairs={{0,80},{1,81},{2,82},{3,83},{4,84},{5,85},{6,86},{7,87},{8,88},{9,... | collective-permute-start | bytes 14155784 | tf_op jit(solution)/shard_map/ppermute | solution.py:88
  72.3 5.9 %collective-permute-start.6 = (bf16[8,2,2,96,384]{4,3,2,1,0:T(8,128)(2,1)S(1)}, bf16[8,2,2,96,384]{4,3,2,1,0:T(8,128)(2,1)S(1)}, u32[]{:S(2)}, u32[]{:S(2)}) collective-permute-start(bf16[8,2,2,96,384]{4,3,2,1,0:T(8,128)(2,1)S(1)} %all_to_all.15.refs_0_), channel_id=1, source_target_pairs={{0,32},{1,33},{2,34},{3,35},{4,36},{5,37},{6,38},{7,39},{8,40},{9,... | collective-permute-start | bytes 7077896 | tf_op jit(solution)/shard_map/ppermute | solution.py:88
  72.3 55.5 %collective-permute-start.4 = (bf16[8,2,2,96,384]{4,3,2,1,0:T(8,128)(2,1)S(1)}, bf16[8,2,2,96,384]{4,3,2,1,0:T(8,128)(2,1)S(1)}, u32[]{:S(2)}, u32[]{:S(2)}) collective-permute-start(bf16[8,2,2,96,384]{4,3,2,1,0:T(8,128)(2,1)S(1)} %all_to_all.15.refs_0_), channel_id=1, source_target_pairs={{0,1},{1,2},{2,3},{3,4},{4,5},{5,6},{6,7},{8,9},{9,10},{10,11},{11... | collective-permute-start | bytes 7077896 | tf_op jit(solution)/shard_map/ppermute | solution.py:88
  75.2 57.4 %collective-permute-start.5 = (bf16[8,2,2,96,384]{4,3,2,1,0:T(8,128)(2,1)S(1)}, bf16[8,2,2,96,384]{4,3,2,1,0:T(8,128)(2,1)S(1)}, u32[]{:S(2)}, u32[]{:S(2)}) collective-permute-start(bf16[8,2,2,96,384]{4,3,2,1,0:T(8,128)(2,1)S(1)} %all_to_all.15.refs_0_), channel_id=1, source_target_pairs={{1,0},{2,1},{3,2},{4,3},{5,4},{6,5},{7,6},{9,8},{10,9},{11,10},{12... | collective-permute-start | bytes 7077896 | tf_op jit(solution)/shard_map/ppermute | solution.py:88
  132.6 14.5 %copy-start.1 = (bf16[768,3072]{1,0:T(8,128)(2,1)}, bf16[768,3072]{1,0:T(8,128)(2,1)S(1)}, u32[]{:S(2)}) copy-start(bf16[768,3072]{1,0:T(8,128)(2,1)S(1)} %collective-permute-done.7.refs_4_.refs_5_) | copy-start | bytes 14155780
  132.6 14.4 %collective-permute-start.8 = (bf16[8,2,2,96,384]{4,3,2,1,0:T(8,128)(2,1)S(1)}, bf16[8,2,2,96,384]{4,3,2,1,0:T(8,128)(2,1)S(1)}, u32[]{:S(2)}, u32[]{:S(2)}) collective-permute-start(bf16[8,2,2,96,384]{4,3,2,1,0:T(8,128)(2,1)S(1)} %collective-permute-done.4.refs_0_), channel_id=1, source_target_pairs={{0,32},{1,33},{2,34},{3,35},{4,36},{5,37},{6,38},{7,39},{8,40},{9,... | collective-permute-start | bytes 7077896 | tf_op jit(solution)/shard_map/ppermute | solution.py:88
  132.6 14.4 %collective-permute-start.9 = (bf16[8,2,2,96,384]{4,3,2,1,0:T(8,128)(2,1)S(1)}, bf16[8,2,2,96,384]{4,3,2,1,0:T(8,128)(2,1)S(1)}, u32[]{:S(2)}, u32[]{:S(2)}) collective-permute-start(bf16[8,2,2,96,384]{4,3,2,1,0:T(8,128)(2,1)S(1)} %collective-permute-done.5.refs_1_), channel_id=1, source_target_pairs={{0,32},{1,33},{2,34},{3,35},{4,36},{5,37},{6,38},{7,39},{8,40},{9,... | collective-permute-start | bytes 7077896 | tf_op jit(solution)/shard_map/ppermute | solution.py:88
  147.0 15.8 %collective-permute-start.10 = (bf16[768,3072]{1,0:T(8,128)(2,1)S(1)}, bf16[768,3072]{1,0:T(8,128)(2,1)}, u32[]{:S(2)}, u32[]{:S(2)}) collective-permute-start(bf16[768,3072]{1,0:T(8,128)(2,1)S(1)} %collective-permute-done.7.refs_4_.refs_5_), channel_id=1, source_target_pairs={{0,32},{1,33},{2,34},{3,35},{4,36},{5,37},{6,38},{7,39},{8,40},{9,... | collective-permute-start | bytes 14155784 | tf_op jit(solution)/shard_map/ppermute | solution.py:88
  162.9 23.5 %all-to-all-start.2 = ((bf16[8,2,96,384]{3,2,1,0:T(8,128)(2,1)}), bf16[8,2,96,384]{3,2,1,0:T(8,128)(2,1)S(1)}, u32[]{:S(2)}, u32[]{:S(2)}) async-start(bf16[8,2,96,384]{3,2,1,0:T(8,128)(2,1)} %attend.5), calls=%async_computation.2 | async-start | bytes 2359296 | tf_op jit(solution)/shard_map/all_to_all | solution.py:92
  186.3 1.0 copy-start.2

commit v4 on v3

--- a/solution.py
+++ b/solution.py
@@ -22,10 +22,10 @@
 TILE = 4 * PART
 CELL = TIMES * TILE
 PAIRS = 10
-ALL = tuple(range(GROUP_HEADS))
 QUARTER = 2 * PART
-ATT_VMEM = 32
+ATT_VMEM = 24
 PROJ_VMEM = 58
+ARRANGE_VMEM = 8
 
 AXES = ("yl", "c", "yh", "zh", "zl", "x")
 SIZES = (2, 2, 2, 2, 2, 4)
@@ -92,65 +92,51 @@
     return lax.all_to_all(array, COLUMN_AXES, 0, 0)
 
 
-def arrange(*arrays):
-    ins, outs, shapes, count = [], [], [], []
-    for stack, heads in arrays:
-        lanes = len(heads) * HEAD_DIM
-        inner = (TIMES, PART, lanes) if len(stack) == 1 else (len(stack), TIMES, PART, lanes)
-        shapes.append(jax.ShapeDtypeStruct((GROUPS,) + inner, jnp.bfloat16))
-        outs.append(pl.BlockSpec((1,) + inner, lambda g, size=len(inner): (g,) + (0,) * size))
-        for array in stack:
-            ins.append(array)
-        count.append((len(stack), heads))
-
-    def kernel(*refs):
-        at = 0
-        for out_ref, (size, heads) in zip(refs[len(ins) :], count):
-            lanes = pl.ds(heads[0] * HEAD_DIM, len(heads) * HEAD_DIM)
-            for which in range(size):
-                value = refs[at][:, :, lanes]
-                if size == 1:
-                    out_ref[0] = value
-                else:
-                    out_ref[0, which] = value
-                at += 1
-
-    block = pl.BlockSpec((TIMES, PART, GROUP_HEADS * HEAD_DIM), lambda g: (0, 0, g))
+def arrange_kernel(stack, *refs):
+    in_refs, out_ref, sems = refs[:stack], refs[stack], refs[stack + 1]
+    copies = []
+    for g in range(GROUPS):
+        lanes = pl.ds(g * GROUP_HEADS * HEAD_DIM, GROUP_HEADS * HEAD_DIM)
+        for at, ref in enumerate(in_refs):
+            to = out_ref.at[g] if stack == 1 else out_ref.at[g, at]
+            copies.append(pltpu.make_async_copy(ref.at[:, :, lanes], to, sems.at[g, at]))
+    for copy in copies:
+        copy.start()
+    for copy in copies:
+        copy.wait()
+
+
+def arrange(*stack):
+    inner = (TIMES, PART, GROUP_HEADS * HEAD_DIM)
+    shape = (GROUPS,) + (inner if len(stack) == 1 else (len(stack),) + inner)
     return pl.pallas_call(
-        kernel,
-        grid=(GROUPS,),
-        in_specs=[block] * len(ins),
-        out_specs=outs,
-        out_shape=shapes,
-        compiler_params=pltpu.CompilerParams(vmem_limit_bytes=58 * 1024 * 1024),
+        functools.partial(arrange_kernel, len(stack)),
+        in_specs=[pl.BlockSpec(memory_space=pl.ANY)] * len(stack),
+        out_specs=pl.BlockSpec(memory_space=pltpu.VMEM),
+        scratch_shapes=[pltpu.SemaphoreType.DMA((GROUPS, len(stack)))],
+        out_shape=jax.ShapeDtypeStruct(shape, jnp.bfloat16),
+        compiler_params=pltpu.CompilerParams(vmem_limit_bytes=ARRANGE_VMEM * 1024 * 1024),
         name="arrange",
-    )(*ins)
-
-
-def attend_kernel(plan, lists, q_ref, *refs):
+    )(*stack)
+
+
+def attend_kernel(plan, mine, *refs):
     sides, taken, last = plan
+    near_refs, q_ref, refs = refs[:ROWS], refs[ROWS], refs[ROWS + 1 :]
+    lists, refs = refs[-1], refs[:-1]
+    for flip, near in enumerate(near_refs):
+        start = (mine[0] ^ flip) * (TIMES * NEIGH)
+        for t in range(TIMES):
+            for entry in range(NEIGH):
+                lists[start + (t * NEIGH + entry)] = near[t, entry]
     kv_refs, refs = refs[:2], refs[2:]
     state_in, refs = refs[:taken], refs[taken:]
     if last:
         o_ref, m_ref, l_ref, acc_ref = refs[:4]
     else:
         m_ref, l_ref, acc_ref = refs[:3]
-    kv_ref, vt_ref, qt_ref, s_refs, p_refs, top_refs, factor_refs, sems = refs[-8:]
-    heads = kv_ref.shape[0]
-
-    def load(head, which):
-        lanes = pl.ds(head * HEAD_DIM, HEAD_DIM)
-        return [
-            pltpu.make_async_copy(
-                kv_refs[side].at[:, which, :, :, lanes], kv_ref.at[head, which, side], sems.at[head, which, side]
-            )
-            for side in range(2)
-        ]
-
-    for head in range(heads):
-        for which in range(2):
-            for copy in load(head, which):
-                copy.start()
+    vt_ref, qt_ref, s_refs, p_refs, top_refs, factor_refs = refs[-6:]
+    heads = q_ref.shape[-1] // HEAD_DIM
 
     if taken:
         for ref, given in zip((m_ref, l_ref, acc_ref), state_in):
@@ -171,10 +157,11 @@
 
     def cell(which, head, key_row):
         parts = []
+        lanes = pl.ds(pl.multiple_of(head * HEAD_DIM, HEAD_DIM), HEAD_DIM)
         for side in range(2):
             for t2 in range(TIMES):
                 for yl in range(2):
-                    parts.append(kv_ref[head, which, side, 2 * key_row + yl, t2])
+                    parts.append(kv_refs[side][2 * key_row + yl, which, t2, :, lanes])
         return jnp.concatenate(parts, axis=0)
 
     def turn(head):
@@ -201,12 +188,12 @@
         row, key_row, step = place(at)
         s_ref, top_ref, p_ref = s_refs[at % 2], top_refs[at % 2], p_refs[at % 2]
         spot = head * ROWS + row
-        start = (lists[ROWS * TIMES * NEIGH] ^ row) * (TIMES * NEIGH) + step * 3
+        start = row * TIMES * NEIGH + step * 3
         oks = []
         for side in range(2):
             for t2 in range(TIMES):
-                entry = start + (sides[side] + 1)
-                use = [lists[entry + (t * NEIGH + (t2 - t + 1) * 9)] for t in range(TIMES)]
+                entry = start + sides[side] + 1
+                use = [lists[entry + t * NEIGH + (t2 - t + 1) * 9] for t in range(TIMES)]
                 oks.append(jnp.where(first, use[0], use[1]) >= 0)
         m_old = m_ref[spot]
         best = m_old
@@ -231,22 +218,10 @@
         update = jnp.dot(vt_ref[head * ROWS + key_row], p_refs[at % 2][...], preferred_element_type=jnp.float32)
         acc_ref[spot] = acc_ref[spot] * factor_refs[at % 2][...] + update
 
-    for copy in load(0, 0):
-        copy.wait()
     score(0, 0)
     score(0, 1)
 
     def per_head(index, carry):
-        for head in range(heads):
-
-            @pl.when(index == head)
-            def _(head=head):
-                for copy in load(head, 1):
-                    copy.wait()
-                if head + 1 < heads:
-                    for copy in load(head + 1, 0):
-                        copy.wait()
-
         turn(index)
         before, following = jnp.maximum(index - 1, 0), jnp.minimum(index + 1, heads - 1)
         for at in range(PAIRS):
@@ -279,7 +254,7 @@
     heads = q.shape[-1] // HEAD_DIM
     spots = heads * ROWS
     state_shapes = [(spots, 1, TILE), (spots, 8, TILE), (spots, HEAD_DIM, TILE)]
-    vmem, anywhere = pl.BlockSpec(memory_space=pltpu.VMEM), pl.BlockSpec(memory_space=pl.ANY)
+    vmem = pl.BlockSpec(memory_space=pltpu.VMEM)
     scratch = []
     if last:
         shapes = [jax.ShapeDtypeStruct(q.shape, jnp.bfloat16)]
@@ -288,18 +263,17 @@
         shapes = [jax.ShapeDtypeStruct(shape, jnp.float32) for shape in state_shapes]
     return pl.pallas_call(
         functools.partial(attend_kernel, (sides, len(state), last)),
-        in_specs=[pl.BlockSpec(memory_space=pltpu.SMEM), vmem] + [anywhere] * 2 + [vmem] * len(state),
+        in_specs=[pl.BlockSpec(memory_space=pltpu.SMEM)] * (1 + ROWS) + [vmem] * (3 + len(state)),
         out_specs=[vmem] * len(shapes),
         scratch_shapes=scratch
         + [
-            pltpu.VMEM((heads, 2, 2, GROUPS, TIMES, PART, HEAD_DIM), jnp.bfloat16),
             pltpu.VMEM((spots, HEAD_DIM, CELL), jnp.bfloat16),
             pltpu.VMEM((spots, HEAD_DIM, TILE), jnp.bfloat16),
             [pltpu.VMEM((CELL, TILE), jnp.float32)] * 2,
             [pltpu.VMEM((CELL, TILE), jnp.bfloat16)] * 2,
             [pltpu.VMEM((4, 8, TILE), jnp.float32)] * 2,
             [pltpu.VMEM((1, TILE), jnp.float32)] * 2,
-            pltpu.SemaphoreType.DMA((heads, 2, 2)),
+            pltpu.SMEM((ROWS * TIMES * NEIGH,), jnp.int32),
         ],
         out_shape=shapes,
         compiler_params=pltpu.CompilerParams(vmem_limit_bytes=ATT_VMEM * 1024 * 1024),
@@ -309,52 +283,61 @@
             transcendentals=heads * PAIRS * 384 * 768,
         ),
         name="attend",
-    )(lists, q, *blocks, *state)
+    )(*lists, q, *blocks, *state)
 
 
 def project_kernel(ids, att_ref, *refs):
-    w_refs, o_ref = refs[:-1], refs[-1]
-    total = None
+    w_refs, o_ref, w_ref, sum_ref, sems = refs[:4], refs[4], refs[5], refs[6], refs[7]
+    rows = D // GROUPS
+    copies = []
     for shard in range(4):
         for part in range(2):
-            rows = att_ref[ids[shard] * 2 + part].reshape(TIMES * PART, GROUP_HEADS * HEAD_DIM)
-            term = jnp.dot(rows, w_refs[2 * shard + part][...], preferred_element_type=jnp.float32)
-            total = term if total is None else total + term
-    o_ref[...] = total.astype(jnp.bfloat16).reshape(TIMES, PART, total.shape[1])
+            source = w_refs[shard].at[pl.ds(part * rows, rows)]
+            at = 2 * shard + part
+            copies.append(pltpu.make_async_copy(source, w_ref.at[at], sems.at[at]))
+    for copy in copies:
+        copy.start()
+    block = 512
+    for at, copy in enumerate(copies):
+        copy.wait()
+        left = att_ref[ids[at // 2] * 2 + at % 2].reshape(TIMES * PART, rows)
+        for start in range(0, D, block):
+            lanes = slice(start, start + block)
+            term = jnp.dot(left, w_ref[at, :, lanes], preferred_element_type=jnp.float32)
+            if at > 0:
+                term = sum_ref[:, lanes] + term
+            if at + 1 < len(copies):
+                sum_ref[:, lanes] = term
+            else:
+                o_ref[:, :, lanes] = term.astype(jnp.bfloat16).reshape(TIMES, PART, block)
 
 
 def project(ids, att, *shards):
-    block = 512
+    vmem, anywhere = pl.BlockSpec(memory_space=pltpu.VMEM), pl.BlockSpec(memory_space=pl.ANY)
     rows = D // GROUPS
-    specs, pieces = [pl.BlockSpec(att.shape, lambda n, s: (0, 0, 0, 0))], []
-    for shard in shards:
-        for part in range(2):
-            specs.append(pl.BlockSpec((rows, block), lambda n, s, part=part: (part, n)))
-            pieces.append(shard)
     return pl.pallas_call(
         project_kernel,
-        grid_spec=pltpu.PrefetchScalarGridSpec(
-            num_scalar_prefetch=1,
-            grid=(D // block,),
-            in_specs=specs,
-            out_specs=pl.BlockSpec((TIMES, PART, block), lambda n, s: (0, 0, n)),
-        ),
+        in_specs=[pl.BlockSpec(memory_space=pltpu.SMEM), vmem] + [anywhere] * len(shards),
+        out_specs=vmem,
+        scratch_shapes=[
+            pltpu.VMEM((GROUPS, rows, D), jnp.bfloat16),
+            pltpu.VMEM((TIMES * PART, D), jnp.float32),
+            pltpu.SemaphoreType.DMA((GROUPS,)),
+        ],
         out_shape=jax.ShapeDtypeStruct((TIMES, PART, D), jnp.bfloat16),
         compiler_params=pltpu.CompilerParams(vmem_limit_bytes=PROJ_VMEM * 1024 * 1024),
         cost_estimate=pl.CostEstimate(
             flops=2 * TIMES * PART * D * D, bytes_accessed=2 * D * D, transcendentals=0
         ),
         name="project",
-    )(ids, att, *pieces)
+    )(ids, att, *shards)
 
 
 def on_device(queries, keys, values, neighbours, w_out):
     live = {"w": w_out, "near": neighbours, "queries": queries, "keys": keys, "values": values}
 
     def fence():
-        names = list(live)
-        for name, value in zip(names, lax.optimization_barrier([live[name] for name in names])):
-            live[name] = value
+        live.update(lax.optimization_barrier(dict(live)))
 
     def swap(name):
         live[name + "_other"] = permute(live[name], OTHER_CORE)
@@ -363,34 +346,36 @@
         blocks = [live[left[0]], live[right[0]]]
         return attend(live["lists"], live["q"], blocks, (left[1], right[1]), state, last)
 
-    (live["q"],) = arrange(((live.pop("queries"),), ALL))
+    live["q"] = arrange(live.pop("queries"))
     fence()
     live["q"] = exchange(live["q"])
-    (live["kv"],) = arrange(((live.pop("keys"), live.pop("values")), ALL))
+    live["kv"] = arrange(live.pop("keys"), live.pop("values"))
+    near = live.pop("near")
     row = lax.axis_index("yh") * 2 + lax.axis_index("zh")
-    flips = [live["near"].reshape(-1)]
+    lists = [row.astype(jnp.int32).reshape(1), near]
     for pairs in (FLIP_Z, FLIP_Y, FLIP_BOTH):
-        flips.append(permute(live["near"], pairs).reshape(-1))
-    live["lists"] = jnp.concatenate(flips + [row.astype(jnp.int32).reshape(1)])
+        lists.append(permute(near, pairs))
+    live["lists"] = lists
     fence()
     live["kv"] = exchange(live["kv"])
-    swap("w")
     fence()
     live["left"], live["right"] = permute(live["kv"], RIGHT), permute(live["kv"], LEFT)
     swap("kv")
-    live["far"] = permute(live["w"], FAR)
+    late = lax.optimization_barrier((live["w"], live["kv_other"]))[0]
+    far, w_other = permute(late, FAR), permute(late, OTHER_CORE)
     state = work(("kv", 0), ("kv_other", 0))
     for at in range(3):
-        live["state", at] = state[at]
+        live["state%d" % at] = state[at]
     fence()
     swap("left")
     swap("right")
-    state = work(("left", -1), ("right", 1), [live.pop(("state", at)) for at in range(3)])
+    state = work(("left", -1), ("right", 1), [live.pop("state%d" % at) for at in range(3)])
     for at in range(3):
-        live["state", at] = state[at]
+        live["state%d" % at] = state[at]
+    live["far"], live["w_other"] = far, w_other
     fence()
     swap("far")
-    (live["att"],) = work(("left_other", -1), ("right_other", 1), [live.pop(("state", at)) for at in range(3)], True)
+    (live["att"],) = work(("left_other", -1), ("right_other", 1), [live.pop("state%d" % at) for at in range(3)], True)
     fence()
     att = exchange(live["att"])
     yl, c = lax.axis_index("yl"), lax.axis_index("c")

time: 200 us -> 189 us (0.945); the launches traced: 200 us -> 186 us
  Pallas kernels: 66.5 us -> 53.3 us
  blocking collectives: 35.1 us -> 32.4 us
    pallas_call x3, Pallas kernels: 23.5 us -> 11.7 us  [the longest x1 9.9 us: project(): pl.pallas_call(project_kernel, in_specs=[pl.BlockSpec(memory_space=pltpu....]
    all_to_all x1, blocking collectives: 35.1 us -> 32.4 us  [exchange(): return lax.all_to_all(array, COLUMN_AXES, 0, 0)]
    unnamed x8 -> x14, local copies, waits for them, and re-layouts: 3.14 us -> 4.84 us
  transfers between devices with their start and end apart: 13 -> 13, of which waited for: 5 -> 4; matrix products, arithmetic and copies ran while one was open for 1% -> 0% of each run, Pallas kernels for 25% -> 23%
where the time goes in v4:
time: 189 us; the launch traced here: 186 us
  waiting for transfers between devices  66.5 us (35%)
  Pallas kernels  53.3 us (28%)
  blocking collectives  32.4 us (17%)
  starting transfers between devices  28 us (15%)
  local copies, waits for them, and re-layouts  4.84 us (3%)
    ppermute x11, waiting for transfers between devices, permute(): return lax.ppermute(array, AXES, pairs)  47.2 us
    pallas_call x3, Pallas kernels, attend(): pl.pallas_call(functools.partial(attend_kernel, (sides, len(state), last)...  41.6 us
    all_to_all x1, blocking collectives, exchange(): return lax.all_to_all(array, COLUMN_AXES, 0, 0)  32.4 us
    all_to_all x2, waiting for transfers between devices, exchange(): return lax.all_to_all(array, COLUMN_AXES, 0, 0)  19.3 us
    ppermute x11, starting transfers between devices, permute(): return lax.ppermute(array, AXES, pairs)  16.4 us
    all_to_all x2, starting transfers between devices, exchange(): return lax.all_to_all(array, COLUMN_AXES, 0, 0)  11.6 us
    pallas_call x1, Pallas kernels, project(): pl.pallas_call(project_kernel, in_specs=[pl.BlockSpec(memory_space=pltpu....  9.9 us
    unnamed x14, local copies, waits for them, and re-layouts  4.84 us
  transfers between devices with their start and end apart: 13, of which 4 were waited for; matrix products, arithmetic and copies ran while one was open for 0% of the time, Pallas kernels for 23%

profile of v4, /device:TPU:6, one launch (start us, length us, event | category | flops | bytes accessed | tf_op | source)
XLA Modules:
  0.0 185.9 jit_solution(14081061415628014467)
XLA Ops:
  0.0 0.0 copy-start
  0.0 1.3 copy-done
  1.3 0.0 copy-start.3
  1.3 1.3 arrange.2
  2.6 7.8 %all-to-all-start = ((bf16[8,2,96,384]{3,2,1,0:T(8,128)(2,1)}), bf16[8,2,96,384]{3,2,1,0:T(8,128)(2,1)S(1)}, u32[]{:S(2)}, u32[]{:S(2)}) async-start(bf16[8,2,96,384]{3,2,1,0:T(8,128)(2,1)} %arrange.2), calls=%async_computation | async-start | bytes 2359296 | tf_op jit(solution)/shard_map/all_to_all | solution.py:92
  10.3 0.0 copy-done.3
  10.4 5.9 %collective-permute-start.2 = (s32[2,27]{1,0:T(2,128)S(1)}, s32[2,27]{1,0:T(2,128)S(1)}, u32[]{:S(2)}, u32[]{:S(2)}) collective-permute-start(s32[2,27]{1,0:T(2,128)S(1)} %copy-done.3), channel_id=1, source_target_pairs={{0,24},{1,25},{2,26},{3,27},{4,28},{5,29},{6,30},{7,31},{8,16},{9,... | collective-permute-start | bytes 656 | tf_op jit(solution)/shard_map/ppermute | solution.py:88
  16.3 0.6 collective-permute-start.1
  16.8 0.1 collective-permute-start
  16.9 0.0 copy-start.1
  16.9 1.3 copy-done.1
  18.2 0.0 copy-start.2
  18.2 1.3 copy-done.2
  19.5 0.5 arrange.3
  20.0 11.0 %collective-permute-done.2.refs_3_ = s32[2,27]{1,0:T(2,128)S(1)} collective-permute-done((s32[2,27]{1,0:T(2,128)S(1)}, s32[2,27]{1,0:T(2,128)S(1)}, u32[]{:S(2)}, u32[]{:S(2)}) %collective-permute-start.2) | collective-permute-done | bytes 248 | tf_op jit(solution)/shard_map/ppermute | solution.py:88
  31.0 0.0 collective-permute-done.1.refs_2_
  31.0 0.0 collective-permute-done.refs_1_
  31.0 0.0 all-to-all-done.refs_4_
  31.0 32.4 %all_to_all.15.refs_5_ = bf16[8,2,2,96,384]{4,3,2,1,0:T(8,128)(2,1)S(1)} all-to-all(bf16[8,2,2,96,384]{4,3,2,1,0:T(8,128)(2,1)S(1)} %arrange.3), channel_id=1, replica_groups=mesh['yl'=2,'c'=2,'yh'=2,'zh'=2,'zl'=2,'x'=4] {'yh','zh','yl'}, dimensions={0} | all-to-all | bytes 4718592 | tf_op jit(solution)/shard_map/all_to_all | solution.py:92
  63.4 0.0 collective-permute-start.3
  63.4 2.7 %collective-permute-start.6 = (bf16[8,2,2,96,384]{4,3,2,1,0:T(8,128)(2,1)S(1)}, bf16[8,2,2,96,384]{4,3,2,1,0:T(8,128)(2,1)S(1)}, u32[]{:S(2)}, u32[]{:S(2)}) collective-permute-start(bf16[8,2,2,96,384]{4,3,2,1,0:T(8,128)(2,1)S(1)} %all_to_all.15.refs_5_), channel_id=1, source_target_pairs={{1,0},{2,1},{3,2},{4,3},{5,4},{6,5},{7,6},{9,8},{10,9},{11,10},{12... | collective-permute-start | bytes 7077896 | tf_op jit(solution)/shard_map/ppermute | solution.py:88
  66.1 5.2 %collective-permute-start.5 = (bf16[8,2,2,96,384]{4,3,2,1,0:T(8,128)(2,1)S(1)}, bf16[8,2,2,96,384]{4,3,2,1,0:T(8,128)(2,1)S(1)}, u32[]{:S(2)}, u32[]{:S(2)}) collective-permute-start(bf16[8,2,2,96,384]{4,3,2,1,0:T(8,128)(2,1)S(1)} %all_to_all.15.refs_5_), channel_id=1, source_target_pairs={{0,1},{1,2},{2,3},{3,4},{4,5},{5,6},{6,7},{8,9},{9,10},{10,11},{11... | collective-permute-start | bytes 7077896 | tf_op jit(solution)/shard_map/ppermute | solution.py:88
  71.4 0.0 collective-permute-done.3.refs_6_
  71.4 0.1 collective-permute-start.9
  71.5 1.2 collective-permute-start.4
  72.6 13.5 %attend.3 = (f32[12,1,384]{2,1,0:T(1,128)S(1)}, f32[12,8,384]{2,1,0:T(8,128)S(1)}, f32[12,128,384]{2,1,0:T(8,128)S(1)}) custom-call(s32[1]{0:T(128)} %bitcast.4.mine, s32[2,27]{1,0:T(2,128)S(1)} %copy-done.3, s32[2,27]{1,0:T(2,128)S(1)} %collective-permute-done.refs_1_, s32[2,27]{1,0:T(2,128)S(1)} %collective-permute-done.1.refs_2_, ...), custom_call_target="tpu_custom_call" | custom-call | flops 4529848320 | bytes 4718592 | tf_op jit(solution)/shard_map/attend/pallas_call | solution.py:264
  86.1 34.9 %collective-permute-done.6.refs_6_ = bf16[8,2,2,96,384]{4,3,2,1,0:T(8,128)(2,1)S(1)} collective-permute-done((bf16[8,2,2,96,384]{4,3,2,1,0:T(8,128)(2,1)S(1)}, bf16[8,2,2,96,384]{4,3,2,1,0:T(8,128)(2,1)S(1)}, u32[]{:S(2)}, u32[]{:S(2)}) %collective-permute-start.6) | collective-permute-done | bytes 2359328 | tf_op jit(solution)/shard_map/ppermute | solution.py:88
  121.1 1.2 collective-permute-done.5.refs_5_
  122.2 0.0 collective-permute-start.7
  122.2 0.5 collective-permute-start.8
  122.8 13.5 %attend.4 = (f32[12,1,384]{2,1,0:T(1,128)S(1)}, f32[12,8,384]{2,1,0:T(8,128)S(1)}, f32[12,128,384]{2,1,0:T(8,128)S(1)}) custom-call(s32[1]{0:T(128)} %bitcast.4.mine, s32[2,27]{1,0:T(2,128)S(1)} %copy-done.3, s32[2,27]{1,0:T(2,128)S(1)} %collective-permute-done.refs_1_, s32[2,27]{1,0:T(2,128)S(1)} %collective-permute-done.1.refs_2_, ...), custom_call_target="tpu_custom_call" | custom-call | flops 4529848320 | bytes 4718592 | tf_op jit(solution)/shard_map/attend/pallas_call | solution.py:264
  136.2 0.0 collective-permute-done.7.refs_5_
  136.3 0.0 collective-permute-done.8.refs_6_
  136.3 0.0 collective-permute-done.9.refs_1_
  136.3 0.0 copy-start.5
  136.3 0.0 collective-permute-done.4.refs_2_
  136.3 0.0 copy-start.6
  136.3 0.1 collective-permute-start.10
  136.4 14.7 %attend.5 = bf16[8,2,96,384]{3,2,1,0:T(8,128)(2,1)} custom-call(s32[1]{0:T(128)} %bitcast.4.mine, s32[2,27]{1,0:T(2,128)S(1)} %copy-done.3, s32[2,27]{1,0:T(2,128)S(1)} %collective-permute-done.refs_1_, s32[2,27]{1,0:T(2,128)S(1)} %collective-permute-done.1.refs_2_, s32[2,27]{1,0:T(2,128)S(1)} %collective-permute-done.2.refs_3_, ...), custom_call_target="tpu_custom_call" | custom-call | flops 4529848320 | bytes 4718592 | tf_op jit(solution)/shard_map/attend/pallas_call | solution.py:264
  151.1 0.0 copy-done.5
  151.1 0.0 copy-done.6
  151.1 0.0 collective-permute-done.10.refs_3_
  151.1 3.8 %all-to-all-start.2 = ((bf16[8,2,96,384]{3,2,1,0:T(8,128)(2,1)}), bf16[8,2,96,384]{3,2,1,0:T(8,128)(2,1)S(1)}, u32[]{:S(2)}, u32[]{:S(2)}) async-start(bf16[8,2,96,384]{3,2,1,0:T(8,128)(2,1)} %attend.5), calls=%async_computation.2 | async-start | bytes 2359296 | tf_op jit(solution)/shard_map/all_to_all | solution.py:92
  154.9 0.6 pad_add_fusion.ids
  155.5 19.3 %all-to-all-done.2.att_ref = bf16[8,2,96,384]{3,2,1,0:T(8,128)(2,1)S(1)} async-done(((bf16[8,2,96,384]{3,2,1,0:T(8,128)(2,1)}), bf16[8,2,96,384]{3,2,1,0:T(8,128)(2,1)S(1)}, u32[]{:S(2)}, u32[]{:S(2)}) %all-to-all-start.2) | async-done | bytes 1179680 | tf_op jit(solution)/shard_map/all_to_all | solution.py:92
  174.8 0.0 copy-start.4
  174.8 1.0 copy-done.4
  175.8 9.9 %project.1 = bf16[2,96,3072]{2,1,0:T(8,128)(2,1)} custom-call(s32[4]{0:T(128)} %pad_add_fusion.ids, bf16[8,2,96,384]{3,2,1,0:T(8,128)(2,1)} %copy-done.4, bf16[768,3072]{1,0:T(8,128)(2,1)} %refs_0_.6, bf16[768,3072]{1,0:T(8,128)(2,1)} %copy-done.5, bf16[768,3072]{1,0:T(8,128)(2,1)} %copy-done.6, bf16[768,3072]{1,0:T(8,128)(2,1)} %collective-permute-done.10.refs_3_), custom_call_target="tpu_custom_call" | custom-call | flops 3623878656 | bytes 18874368 | tf_op jit(solution)/shard_map/project/pallas_call | solution.py:318
Async XLA Ops:
  0.0 1.3 copy-start
  1.3 9.1 %copy-start.3 = (s32[2,27]{1,0:T(2,128)S(1)}, s32[2,27]{1,0:T(2,128)}, u32[]{:S(2)}) copy-start(s32[2,27]{1,0:T(2,128)} %refs_0_.5) | copy-start | bytes 652
  2.6 28.5 %all-to-all-start = ((bf16[8,2,96,384]{3,2,1,0:T(8,128)(2,1)}), bf16[8,2,96,384]{3,2,1,0:T(8,128)(2,1)S(1)}, u32[]{:S(2)}, u32[]{:S(2)}) async-start(bf16[8,2,96,384]{3,2,1,0:T(8,128)(2,1)} %arrange.2), calls=%async_computation | async-start | bytes 2359296 | tf_op jit(solution)/shard_map/all_to_all | solution.py:92
  10.4 20.7 %collective-permute-start.2 = (s32[2,27]{1,0:T(2,128)S(1)}, s32[2,27]{1,0:T(2,128)S(1)}, u32[]{:S(2)}, u32[]{:S(2)}) collective-permute-start(s32[2,27]{1,0:T(2,128)S(1)} %copy-done.3), channel_id=1, source_target_pairs={{0,24},{1,25},{2,26},{3,27},{4,28},{5,29},{6,30},{7,31},{8,16},{9,... | collective-permute-start | bytes 656 | tf_op jit(solution)/shard_map/ppermute | solution.py:88
  16.3 14.7 %collective-permute-start.1 = (s32[2,27]{1,0:T(2,128)S(1)}, s32[2,27]{1,0:T(2,128)S(1)}, u32[]{:S(2)}, u32[]{:S(2)}) collective-permute-start(s32[2,27]{1,0:T(2,128)S(1)} %copy-done.3), channel_id=1, source_target_pairs={{0,16},{1,17},{2,18},{3,19},{4,20},{5,21},{6,22},{7,23},{8,24},{9,... | collective-permute-start | bytes 656 | tf_op jit(solution)/shard_map/ppermute | solution.py:88
  16.8 14.2 %collective-permute-start = (s32[2,27]{1,0:T(2,128)S(1)}, s32[2,27]{1,0:T(2,128)S(1)}, u32[]{:S(2)}, u32[]{:S(2)}) collective-permute-start(s32[2,27]{1,0:T(2,128)S(1)} %copy-done.3), channel_id=1, source_target_pairs={{0,8},{1,9},{2,10},{3,11},{4,12},{5,13},{6,14},{7,15},{8,0},{9,1},... | collective-permute-start | bytes 656 | tf_op jit(solution)/shard_map/ppermute | solution.py:88
  16.9 1.3 copy-start.1
  18.2 1.3 copy-start.2
  63.4 8.0 %collective-permute-start.3 = (bf16[8,2,2,96,384]{4,3,2,1,0:T(8,128)(2,1)S(1)}, bf16[8,2,2,96,384]{4,3,2,1,0:T(8,128)(2,1)S(1)}, u32[]{:S(2)}, u32[]{:S(2)}) collective-permute-start(bf16[8,2,2,96,384]{4,3,2,1,0:T(8,128)(2,1)S(1)} %all_to_all.15.refs_5_), channel_id=1, source_target_pairs={{0,32},{1,33},{2,34},{3,35},{4,36},{5,37},{6,38},{7,39},{8,40},{9,... | collective-permute-start | bytes 7077896 | tf_op jit(solution)/shard_map/ppermute | solution.py:88
  63.4 57.7 %collective-permute-start.6 = (bf16[8,2,2,96,384]{4,3,2,1,0:T(8,128)(2,1)S(1)}, bf16[8,2,2,96,384]{4,3,2,1,0:T(8,128)(2,1)S(1)}, u32[]{:S(2)}, u32[]{:S(2)}) collective-permute-start(bf16[8,2,2,96,384]{4,3,2,1,0:T(8,128)(2,1)S(1)} %all_to_all.15.refs_5_), channel_id=1, source_target_pairs={{1,0},{2,1},{3,2},{4,3},{5,4},{6,5},{7,6},{9,8},{10,9},{11,10},{12... | collective-permute-start | bytes 7077896 | tf_op jit(solution)/shard_map/ppermute | solution.py:88
  66.1 56.1 %collective-permute-start.5 = (bf16[8,2,2,96,384]{4,3,2,1,0:T(8,128)(2,1)S(1)}, bf16[8,2,2,96,384]{4,3,2,1,0:T(8,128)(2,1)S(1)}, u32[]{:S(2)}, u32[]{:S(2)}) collective-permute-start(bf16[8,2,2,96,384]{4,3,2,1,0:T(8,128)(2,1)S(1)} %all_to_all.15.refs_5_), channel_id=1, source_target_pairs={{0,1},{1,2},{2,3},{3,4},{4,5},{5,6},{6,7},{8,9},{9,10},{10,11},{11... | collective-permute-start | bytes 7077896 | tf_op jit(solution)/shard_map/ppermute | solution.py:88
  71.4 64.9 %collective-permute-start.9 = (bf16[768,3072]{1,0:T(8,128)(2,1)}, bf16[768,3072]{1,0:T(8,128)(2,1)S(1)}, u32[]{:S(2)}, u32[]{:S(2)}) collective-permute-start(bf16[768,3072]{1,0:T(8,128)(2,1)} %refs_0_.6), channel_id=1, source_target_pairs={{0,32},{1,33},{2,34},{3,35},{4,36},{5,37},{6,38},{7,39},{8,40},{9,... | collective-permute-start | bytes 14155784 | tf_op jit(solution)/shard_map/ppermute | solution.py:88
  71.5 64.8 %collective-permute-start.4 = (bf16[768,3072]{1,0:T(8,128)(2,1)}, bf16[768,3072]{1,0:T(8,128)(2,1)S(1)}, u32[]{:S(2)}, u32[]{:S(2)}) collective-permute-start(bf16[768,3072]{1,0:T(8,128)(2,1)} %refs_0_.6), channel_id=1, source_target_pairs={{0,80},{1,81},{2,82},{3,83},{4,84},{5,85},{6,86},{7,87},{8,88},{9,... | collective-permute-start | bytes 14155784 | tf_op jit(solution)/shard_map/ppermute | solution.py:88
  122.2 14.0 %collective-permute-start.7 = (bf16[8,2,2,96,384]{4,3,2,1,0:T(8,128)(2,1)S(1)}, bf16[8,2,2,96,384]{4,3,2,1,0:T(8,128)(2,1)S(1)}, u32[]{:S(2)}, u32[]{:S(2)}) collective-permute-start(bf16[8,2,2,96,384]{4,3,2,1,0:T(8,128)(2,1)S(1)} %collective-permute-done.5.refs_5_), channel_id=1, source_target_pairs={{0,32},{1,33},{2,34},{3,35},{4,36},{5,37},{6,38},{7,39},{8,40},{9,... | collective-permute-start | bytes 7077896 | tf_op jit(solution)/shard_map/ppermute | solution.py:88
  122.2 14.0 %collective-permute-start.8 = (bf16[8,2,2,96,384]{4,3,2,1,0:T(8,128)(2,1)S(1)}, bf16[8,2,2,96,384]{4,3,2,1,0:T(8,128)(2,1)S(1)}, u32[]{:S(2)}, u32[]{:S(2)}) collective-permute-start(bf16[8,2,2,96,384]{4,3,2,1,0:T(8,128)(2,1)S(1)} %collective-permute-done.6.refs_6_), channel_id=1, source_target_pairs={{0,32},{1,33},{2,34},{3,35},{4,36},{5,37},{6,38},{7,39},{8,40},{9,... | collective-permute-start | bytes 7077896 | tf_op jit(solution)/shard_map/ppermute | solution.py:88
  136.3 14.8 %copy-start.5 = (bf16[768,3072]{1,0:T(8,128)(2,1)}, bf16[768,3072]{1,0:T(8,128)(2,1)S(1)}, u32[]{:S(2)}) copy-start(bf16[768,3072]{1,0:T(8,128)(2,1)S(1)} %collective-permute-done.9.refs_1_) | copy-start | bytes 14155780
  136.3 14.8 %copy-start.6 = (bf16[768,3072]{1,0:T(8,128)(2,1)}, bf16[768,3072]{1,0:T(8,128)(2,1)S(1)}, u32[]{:S(2)}) copy-start(bf16[768,3072]{1,0:T(8,128)(2,1)S(1)} %collective-permute-done.4.refs_2_) | copy-start | bytes 14155780
  136.3 14.8 %collective-permute-start.10 = (bf16[768,3072]{1,0:T(8,128)(2,1)S(1)}, bf16[768,3072]{1,0:T(8,128)(2,1)}, u32[]{:S(2)}, u32[]{:S(2)}) collective-permute-start(bf16[768,3072]{1,0:T(8,128)(2,1)S(1)} %collective-permute-done.4.refs_2_), channel_id=1, source_target_pairs={{0,32},{1,33},{2,34},{3,35},{4,36},{5,37},{6,38},{7,39},{8,40},{9,... | collective-permute-start | bytes 14155784 | tf_op jit(solution)/shard_map/ppermute | solution.py:88
  151.1 23.7 %all-to-all-start.2 = ((bf16[8,2,96,384]{3,2,1,0:T(8,128)(2,1)}), bf16[8,2,96,384]{3,2,1,0:T(8,128)(2,1)S(1)}, u32[]{:S(2)}, u32[]{:S(2)}) async-start(bf16[8,2,96,384]{3,2,1,0:T(8,128)(2,1)} %attend.5), calls=%async_computation.2 | async-start | bytes 2359296 | tf_op jit(solution)/shard_map/all_to_all | solution.py:92
  174.8 1.0 copy-start.4

commit v5 on v4

--- a/solution.py
+++ b/solution.py
@@ -286,43 +286,59 @@
     )(*lists, q, *blocks, *state)
 
 
-def project_kernel(ids, att_ref, *refs):
-    w_refs, o_ref, w_ref, sum_ref, sems = refs[:4], refs[4], refs[5], refs[6], refs[7]
+def project_kernel(ids, att_in, *refs):
+    w_refs, o_ref, att_ref, w_ref, sum_ref, out_ref, sems, out_sems = refs[:4], *refs[4:]
     rows = D // GROUPS
+    bring = pltpu.make_async_copy(att_in, att_ref, sems.at[GROUPS])
+    bring.start()
     copies = []
-    for shard in range(4):
-        for part in range(2):
-            source = w_refs[shard].at[pl.ds(part * rows, rows)]
-            at = 2 * shard + part
-            copies.append(pltpu.make_async_copy(source, w_ref.at[at], sems.at[at]))
-    for copy in copies:
+    for at in range(GROUPS):
+        source = w_refs[at // 2].at[pl.ds(at % 2 * rows, rows)]
+        copies.append(pltpu.make_async_copy(source, w_ref.at[at], sems.at[at]))
+    ahead = 3
+    for copy in copies[:ahead]:
         copy.start()
+    bring.wait()
     block = 512
+    results = []
     for at, copy in enumerate(copies):
         copy.wait()
+        if at + ahead < GROUPS:
+            copies[at + ahead].start()
         left = att_ref[ids[at // 2] * 2 + at % 2].reshape(TIMES * PART, rows)
         for start in range(0, D, block):
             lanes = slice(start, start + block)
             term = jnp.dot(left, w_ref[at, :, lanes], preferred_element_type=jnp.float32)
             if at > 0:
                 term = sum_ref[:, lanes] + term
-            if at + 1 < len(copies):
+            if at + 1 < GROUPS:
                 sum_ref[:, lanes] = term
             else:
-                o_ref[:, :, lanes] = term.astype(jnp.bfloat16).reshape(TIMES, PART, block)
+                out_ref[:, :, lanes] = term.astype(jnp.bfloat16).reshape(TIMES, PART, block)
+                spot = pl.ds(start, block)
+                done = pltpu.make_async_copy(
+                    out_ref.at[:, :, spot], o_ref.at[:, :, spot], out_sems.at[start // block]
+                )
+                done.start()
+                results.append(done)
+    for done in results:
+        done.wait()
 
 
 def project(ids, att, *shards):
-    vmem, anywhere = pl.BlockSpec(memory_space=pltpu.VMEM), pl.BlockSpec(memory_space=pl.ANY)
+    anywhere = pl.BlockSpec(memory_space=pl.ANY)
     rows = D // GROUPS
     return pl.pallas_call(
         project_kernel,
-        in_specs=[pl.BlockSpec(memory_space=pltpu.SMEM), vmem] + [anywhere] * len(shards),
-        out_specs=vmem,
+        in_specs=[pl.BlockSpec(memory_space=pltpu.SMEM)] + [anywhere] * (1 + len(shards)),
+        out_specs=anywhere,
         scratch_shapes=[
+            pltpu.VMEM(att.shape, jnp.bfloat16),
             pltpu.VMEM((GROUPS, rows, D), jnp.bfloat16),
             pltpu.VMEM((TIMES * PART, D), jnp.float32),
-            pltpu.SemaphoreType.DMA((GROUPS,)),
+            pltpu.VMEM((TIMES, PART, D), jnp.bfloat16),
+            pltpu.SemaphoreType.DMA((GROUPS + 1,)),
+            pltpu.SemaphoreType.DMA((D // 512,)),
         ],
         out_shape=jax.ShapeDtypeStruct((TIMES, PART, D), jnp.bfloat16),
         compiler_params=pltpu.CompilerParams(vmem_limit_bytes=PROJ_VMEM * 1024 * 1024),

time: 189 us -> 189 us (level)
  no operation moved by 1% of the time
where the time goes in v5:
time: 189 us; the launch traced here: 186 us
  waiting for transfers between devices  66.5 us (35%)
  Pallas kernels  52.9 us (28%)
  blocking collectives  32.4 us (17%)
  starting transfers between devices  28 us (15%)
  local copies, waits for them, and re-layouts  4.84 us (3%)
    ppermute x11, waiting for transfers between devices, permute(): return lax.ppermute(array, AXES, pairs)  47.2 us
    pallas_call x3, Pallas kernels, attend(): pl.pallas_call(functools.partial(attend_kernel, (sides, len(state), last)...  41.6 us
    all_to_all x1, blocking collectives, exchange(): return lax.all_to_all(array, COLUMN_AXES, 0, 0)  32.4 us
    all_to_all x2, waiting for transfers between devices, exchange(): return lax.all_to_all(array, COLUMN_AXES, 0, 0)  19.3 us
    ppermute x11, starting transfers between devices, permute(): return lax.ppermute(array, AXES, pairs)  16.4 us
    all_to_all x2, starting transfers between devices, exchange(): return lax.all_to_all(array, COLUMN_AXES, 0, 0)  11.6 us
    pallas_call x1, Pallas kernels, project(): pl.pallas_call(project_kernel, in_specs=[pl.BlockSpec(memory_space=pltpu....  9.52 us
    unnamed x14, local copies, waits for them, and re-layouts  4.84 us
  transfers between devices with their start and end apart: 13, of which 4 were waited for; matrix products, arithmetic and copies ran while one was open for 0% of the time, Pallas kernels for 23%

profile of v5, /device:TPU:6, one launch (start us, length us, event | category | flops | bytes accessed | tf_op | source)
XLA Modules:
  0.0 185.5 jit_solution(8971851619985335833)
XLA Ops:
  0.0 0.0 copy-start
  0.0 1.3 copy-done
  1.3 0.0 copy-start.3
  1.3 1.3 arrange.2
  2.6 7.8 %all-to-all-start = ((bf16[8,2,96,384]{3,2,1,0:T(8,128)(2,1)}), bf16[8,2,96,384]{3,2,1,0:T(8,128)(2,1)S(1)}, u32[]{:S(2)}, u32[]{:S(2)}) async-start(bf16[8,2,96,384]{3,2,1,0:T(8,128)(2,1)} %arrange.2), calls=%async_computation | async-start | bytes 2359296 | tf_op jit(solution)/shard_map/all_to_all | solution.py:92
  10.3 0.0 copy-done.3
  10.4 5.9 %collective-permute-start.2 = (s32[2,27]{1,0:T(2,128)S(1)}, s32[2,27]{1,0:T(2,128)S(1)}, u32[]{:S(2)}, u32[]{:S(2)}) collective-permute-start(s32[2,27]{1,0:T(2,128)S(1)} %copy-done.3), channel_id=1, source_target_pairs={{0,24},{1,25},{2,26},{3,27},{4,28},{5,29},{6,30},{7,31},{8,16},{9,... | collective-permute-start | bytes 656 | tf_op jit(solution)/shard_map/ppermute | solution.py:88
  16.3 0.6 collective-permute-start.1
  16.8 0.1 collective-permute-start
  16.9 0.0 copy-start.1
  16.9 1.3 copy-done.1
  18.2 0.0 copy-start.2
  18.2 1.3 copy-done.2
  19.5 0.5 arrange.3
  20.0 11.0 %collective-permute-done.2.refs_3_ = s32[2,27]{1,0:T(2,128)S(1)} collective-permute-done((s32[2,27]{1,0:T(2,128)S(1)}, s32[2,27]{1,0:T(2,128)S(1)}, u32[]{:S(2)}, u32[]{:S(2)}) %collective-permute-start.2) | collective-permute-done | bytes 248 | tf_op jit(solution)/shard_map/ppermute | solution.py:88
  31.0 0.0 collective-permute-done.1.refs_2_
  31.0 0.0 collective-permute-done.refs_1_
  31.0 0.0 all-to-all-done.refs_4_
  31.0 32.4 %all_to_all.15.refs_5_ = bf16[8,2,2,96,384]{4,3,2,1,0:T(8,128)(2,1)S(1)} all-to-all(bf16[8,2,2,96,384]{4,3,2,1,0:T(8,128)(2,1)S(1)} %arrange.3), channel_id=1, replica_groups=mesh['yl'=2,'c'=2,'yh'=2,'zh'=2,'zl'=2,'x'=4] {'yh','zh','yl'}, dimensions={0} | all-to-all | bytes 4718592 | tf_op jit(solution)/shard_map/all_to_all | solution.py:92
  63.4 0.0 collective-permute-start.3
  63.4 2.7 %collective-permute-start.6 = (bf16[8,2,2,96,384]{4,3,2,1,0:T(8,128)(2,1)S(1)}, bf16[8,2,2,96,384]{4,3,2,1,0:T(8,128)(2,1)S(1)}, u32[]{:S(2)}, u32[]{:S(2)}) collective-permute-start(bf16[8,2,2,96,384]{4,3,2,1,0:T(8,128)(2,1)S(1)} %all_to_all.15.refs_5_), channel_id=1, source_target_pairs={{1,0},{2,1},{3,2},{4,3},{5,4},{6,5},{7,6},{9,8},{10,9},{11,10},{12... | collective-permute-start | bytes 7077896 | tf_op jit(solution)/shard_map/ppermute | solution.py:88
  66.1 5.2 %collective-permute-start.5 = (bf16[8,2,2,96,384]{4,3,2,1,0:T(8,128)(2,1)S(1)}, bf16[8,2,2,96,384]{4,3,2,1,0:T(8,128)(2,1)S(1)}, u32[]{:S(2)}, u32[]{:S(2)}) collective-permute-start(bf16[8,2,2,96,384]{4,3,2,1,0:T(8,128)(2,1)S(1)} %all_to_all.15.refs_5_), channel_id=1, source_target_pairs={{0,1},{1,2},{2,3},{3,4},{4,5},{5,6},{6,7},{8,9},{9,10},{10,11},{11... | collective-permute-start | bytes 7077896 | tf_op jit(solution)/shard_map/ppermute | solution.py:88
  71.4 0.0 collective-permute-done.3.refs_6_
  71.4 0.1 collective-permute-start.9
  71.5 1.2 collective-permute-start.4
  72.6 13.5 %attend.3 = (f32[12,1,384]{2,1,0:T(1,128)S(1)}, f32[12,8,384]{2,1,0:T(8,128)S(1)}, f32[12,128,384]{2,1,0:T(8,128)S(1)}) custom-call(s32[1]{0:T(128)} %bitcast.4.mine, s32[2,27]{1,0:T(2,128)S(1)} %copy-done.3, s32[2,27]{1,0:T(2,128)S(1)} %collective-permute-done.refs_1_, s32[2,27]{1,0:T(2,128)S(1)} %collective-permute-done.1.refs_2_, ...), custom_call_target="tpu_custom_call" | custom-call | flops 4529848320 | bytes 4718592 | tf_op jit(solution)/shard_map/attend/pallas_call | solution.py:264
  86.1 34.9 %collective-permute-done.6.refs_6_ = bf16[8,2,2,96,384]{4,3,2,1,0:T(8,128)(2,1)S(1)} collective-permute-done((bf16[8,2,2,96,384]{4,3,2,1,0:T(8,128)(2,1)S(1)}, bf16[8,2,2,96,384]{4,3,2,1,0:T(8,128)(2,1)S(1)}, u32[]{:S(2)}, u32[]{:S(2)}) %collective-permute-start.6) | collective-permute-done | bytes 2359328 | tf_op jit(solution)/shard_map/ppermute | solution.py:88
  121.1 1.2 collective-permute-done.5.refs_5_
  122.2 0.0 collective-permute-start.7
  122.2 0.5 collective-permute-start.8
  122.8 13.5 %attend.4 = (f32[12,1,384]{2,1,0:T(1,128)S(1)}, f32[12,8,384]{2,1,0:T(8,128)S(1)}, f32[12,128,384]{2,1,0:T(8,128)S(1)}) custom-call(s32[1]{0:T(128)} %bitcast.4.mine, s32[2,27]{1,0:T(2,128)S(1)} %copy-done.3, s32[2,27]{1,0:T(2,128)S(1)} %collective-permute-done.refs_1_, s32[2,27]{1,0:T(2,128)S(1)} %collective-permute-done.1.refs_2_, ...), custom_call_target="tpu_custom_call" | custom-call | flops 4529848320 | bytes 4718592 | tf_op jit(solution)/shard_map/attend/pallas_call | solution.py:264
  136.2 0.0 collective-permute-done.7.refs_5_
  136.3 0.0 collective-permute-done.8.refs_6_
  136.3 0.0 collective-permute-done.9.refs_1_
  136.3 0.0 copy-start.5
  136.3 0.0 collective-permute-done.4.refs_2_
  136.3 0.0 copy-start.6
  136.3 0.1 collective-permute-start.10
  136.4 14.7 %attend.5 = bf16[8,2,96,384]{3,2,1,0:T(8,128)(2,1)} custom-call(s32[1]{0:T(128)} %bitcast.4.mine, s32[2,27]{1,0:T(2,128)S(1)} %copy-done.3, s32[2,27]{1,0:T(2,128)S(1)} %collective-permute-done.refs_1_, s32[2,27]{1,0:T(2,128)S(1)} %collective-permute-done.1.refs_2_, s32[2,27]{1,0:T(2,128)S(1)} %collective-permute-done.2.refs_3_, ...), custom_call_target="tpu_custom_call" | custom-call | flops 4529848320 | bytes 4718592 | tf_op jit(solution)/shard_map/attend/pallas_call | solution.py:264
  151.1 0.0 copy-done.5
  151.1 0.0 copy-done.6
  151.1 0.0 collective-permute-done.10.refs_3_
  151.1 3.8 %all-to-all-start.2 = ((bf16[8,2,96,384]{3,2,1,0:T(8,128)(2,1)}), bf16[8,2,96,384]{3,2,1,0:T(8,128)(2,1)S(1)}, u32[]{:S(2)}, u32[]{:S(2)}) async-start(bf16[8,2,96,384]{3,2,1,0:T(8,128)(2,1)} %attend.5), calls=%async_computation.2 | async-start | bytes 2359296 | tf_op jit(solution)/shard_map/all_to_all | solution.py:92
  154.9 0.6 pad_add_fusion.ids
  155.5 19.3 %all-to-all-done.2.att_in = bf16[8,2,96,384]{3,2,1,0:T(8,128)(2,1)S(1)} async-done(((bf16[8,2,96,384]{3,2,1,0:T(8,128)(2,1)}), bf16[8,2,96,384]{3,2,1,0:T(8,128)(2,1)S(1)}, u32[]{:S(2)}, u32[]{:S(2)}) %all-to-all-start.2) | async-done | bytes 1179680 | tf_op jit(solution)/shard_map/all_to_all | solution.py:92
  174.8 0.0 copy-start.4
  174.8 1.0 copy-done.4
  175.8 9.5 %project.1 = bf16[2,96,3072]{2,1,0:T(8,128)(2,1)} custom-call(s32[4]{0:T(128)} %pad_add_fusion.ids, bf16[8,2,96,384]{3,2,1,0:T(8,128)(2,1)} %copy-done.4, bf16[768,3072]{1,0:T(8,128)(2,1)} %refs_0_.6, bf16[768,3072]{1,0:T(8,128)(2,1)} %copy-done.5, bf16[768,3072]{1,0:T(8,128)(2,1)} %copy-done.6, bf16[768,3072]{1,0:T(8,128)(2,1)} %collective-permute-done.10.refs_3_), custom_call_target="tpu_custom_call" | custom-call | flops 3623878656 | bytes 18874368 | tf_op jit(solution)/shard_map/project/pallas_call | solution.py:331
Async XLA Ops:
  0.0 1.3 copy-start
  1.3 9.1 %copy-start.3 = (s32[2,27]{1,0:T(2,128)S(1)}, s32[2,27]{1,0:T(2,128)}, u32[]{:S(2)}) copy-start(s32[2,27]{1,0:T(2,128)} %refs_0_.5) | copy-start | bytes 652
  2.6 28.5 %all-to-all-start = ((bf16[8,2,96,384]{3,2,1,0:T(8,128)(2,1)}), bf16[8,2,96,384]{3,2,1,0:T(8,128)(2,1)S(1)}, u32[]{:S(2)}, u32[]{:S(2)}) async-start(bf16[8,2,96,384]{3,2,1,0:T(8,128)(2,1)} %arrange.2), calls=%async_computation | async-start | bytes 2359296 | tf_op jit(solution)/shard_map/all_to_all | solution.py:92
  10.4 20.7 %collective-permute-start.2 = (s32[2,27]{1,0:T(2,128)S(1)}, s32[2,27]{1,0:T(2,128)S(1)}, u32[]{:S(2)}, u32[]{:S(2)}) collective-permute-start(s32[2,27]{1,0:T(2,128)S(1)} %copy-done.3), channel_id=1, source_target_pairs={{0,24},{1,25},{2,26},{3,27},{4,28},{5,29},{6,30},{7,31},{8,16},{9,... | collective-permute-start | bytes 656 | tf_op jit(solution)/shard_map/ppermute | solution.py:88
  16.3 14.7 %collective-permute-start.1 = (s32[2,27]{1,0:T(2,128)S(1)}, s32[2,27]{1,0:T(2,128)S(1)}, u32[]{:S(2)}, u32[]{:S(2)}) collective-permute-start(s32[2,27]{1,0:T(2,128)S(1)} %copy-done.3), channel_id=1, source_target_pairs={{0,16},{1,17},{2,18},{3,19},{4,20},{5,21},{6,22},{7,23},{8,24},{9,... | collective-permute-start | bytes 656 | tf_op jit(solution)/shard_map/ppermute | solution.py:88
  16.8 14.2 %collective-permute-start = (s32[2,27]{1,0:T(2,128)S(1)}, s32[2,27]{1,0:T(2,128)S(1)}, u32[]{:S(2)}, u32[]{:S(2)}) collective-permute-start(s32[2,27]{1,0:T(2,128)S(1)} %copy-done.3), channel_id=1, source_target_pairs={{0,8},{1,9},{2,10},{3,11},{4,12},{5,13},{6,14},{7,15},{8,0},{9,1},... | collective-permute-start | bytes 656 | tf_op jit(solution)/shard_map/ppermute | solution.py:88
  16.9 1.3 copy-start.1
  18.2 1.3 copy-start.2
  63.4 8.0 %collective-permute-start.3 = (bf16[8,2,2,96,384]{4,3,2,1,0:T(8,128)(2,1)S(1)}, bf16[8,2,2,96,384]{4,3,2,1,0:T(8,128)(2,1)S(1)}, u32[]{:S(2)}, u32[]{:S(2)}) collective-permute-start(bf16[8,2,2,96,384]{4,3,2,1,0:T(8,128)(2,1)S(1)} %all_to_all.15.refs_5_), channel_id=1, source_target_pairs={{0,32},{1,33},{2,34},{3,35},{4,36},{5,37},{6,38},{7,39},{8,40},{9,... | collective-permute-start | bytes 7077896 | tf_op jit(solution)/shard_map/ppermute | solution.py:88
  63.4 57.7 %collective-permute-start.6 = (bf16[8,2,2,96,384]{4,3,2,1,0:T(8,128)(2,1)S(1)}, bf16[8,2,2,96,384]{4,3,2,1,0:T(8,128)(2,1)S(1)}, u32[]{:S(2)}, u32[]{:S(2)}) collective-permute-start(bf16[8,2,2,96,384]{4,3,2,1,0:T(8,128)(2,1)S(1)} %all_to_all.15.refs_5_), channel_id=1, source_target_pairs={{1,0},{2,1},{3,2},{4,3},{5,4},{6,5},{7,6},{9,8},{10,9},{11,10},{12... | collective-permute-start | bytes 7077896 | tf_op jit(solution)/shard_map/ppermute | solution.py:88
  66.1 56.1 %collective-permute-start.5 = (bf16[8,2,2,96,384]{4,3,2,1,0:T(8,128)(2,1)S(1)}, bf16[8,2,2,96,384]{4,3,2,1,0:T(8,128)(2,1)S(1)}, u32[]{:S(2)}, u32[]{:S(2)}) collective-permute-start(bf16[8,2,2,96,384]{4,3,2,1,0:T(8,128)(2,1)S(1)} %all_to_all.15.refs_5_), channel_id=1, source_target_pairs={{0,1},{1,2},{2,3},{3,4},{4,5},{5,6},{6,7},{8,9},{9,10},{10,11},{11... | collective-permute-start | bytes 7077896 | tf_op jit(solution)/shard_map/ppermute | solution.py:88
  71.4 64.9 %collective-permute-start.9 = (bf16[768,3072]{1,0:T(8,128)(2,1)}, bf16[768,3072]{1,0:T(8,128)(2,1)S(1)}, u32[]{:S(2)}, u32[]{:S(2)}) collective-permute-start(bf16[768,3072]{1,0:T(8,128)(2,1)} %refs_0_.6), channel_id=1, source_target_pairs={{0,32},{1,33},{2,34},{3,35},{4,36},{5,37},{6,38},{7,39},{8,40},{9,... | collective-permute-start | bytes 14155784 | tf_op jit(solution)/shard_map/ppermute | solution.py:88
  71.5 64.8 %collective-permute-start.4 = (bf16[768,3072]{1,0:T(8,128)(2,1)}, bf16[768,3072]{1,0:T(8,128)(2,1)S(1)}, u32[]{:S(2)}, u32[]{:S(2)}) collective-permute-start(bf16[768,3072]{1,0:T(8,128)(2,1)} %refs_0_.6), channel_id=1, source_target_pairs={{0,80},{1,81},{2,82},{3,83},{4,84},{5,85},{6,86},{7,87},{8,88},{9,... | collective-permute-start | bytes 14155784 | tf_op jit(solution)/shard_map/ppermute | solution.py:88
  122.2 14.0 %collective-permute-start.7 = (bf16[8,2,2,96,384]{4,3,2,1,0:T(8,128)(2,1)S(1)}, bf16[8,2,2,96,384]{4,3,2,1,0:T(8,128)(2,1)S(1)}, u32[]{:S(2)}, u32[]{:S(2)}) collective-permute-start(bf16[8,2,2,96,384]{4,3,2,1,0:T(8,128)(2,1)S(1)} %collective-permute-done.5.refs_5_), channel_id=1, source_target_pairs={{0,32},{1,33},{2,34},{3,35},{4,36},{5,37},{6,38},{7,39},{8,40},{9,... | collective-permute-start | bytes 7077896 | tf_op jit(solution)/shard_map/ppermute | solution.py:88
  122.2 14.0 %collective-permute-start.8 = (bf16[8,2,2,96,384]{4,3,2,1,0:T(8,128)(2,1)S(1)}, bf16[8,2,2,96,384]{4,3,2,1,0:T(8,128)(2,1)S(1)}, u32[]{:S(2)}, u32[]{:S(2)}) collective-permute-start(bf16[8,2,2,96,384]{4,3,2,1,0:T(8,128)(2,1)S(1)} %collective-permute-done.6.refs_6_), channel_id=1, source_target_pairs={{0,32},{1,33},{2,34},{3,35},{4,36},{5,37},{6,38},{7,39},{8,40},{9,... | collective-permute-start | bytes 7077896 | tf_op jit(solution)/shard_map/ppermute | solution.py:88
  136.3 14.8 %copy-start.5 = (bf16[768,3072]{1,0:T(8,128)(2,1)}, bf16[768,3072]{1,0:T(8,128)(2,1)S(1)}, u32[]{:S(2)}) copy-start(bf16[768,3072]{1,0:T(8,128)(2,1)S(1)} %collective-permute-done.9.refs_1_) | copy-start | bytes 14155780
  136.3 14.8 %copy-start.6 = (bf16[768,3072]{1,0:T(8,128)(2,1)}, bf16[768,3072]{1,0:T(8,128)(2,1)S(1)}, u32[]{:S(2)}) copy-start(bf16[768,3072]{1,0:T(8,128)(2,1)S(1)} %collective-permute-done.4.refs_2_) | copy-start | bytes 14155780
  136.3 14.8 %collective-permute-start.10 = (bf16[768,3072]{1,0:T(8,128)(2,1)S(1)}, bf16[768,3072]{1,0:T(8,128)(2,1)}, u32[]{:S(2)}, u32[]{:S(2)}) collective-permute-start(bf16[768,3072]{1,0:T(8,128)(2,1)S(1)} %collective-permute-done.4.refs_2_), channel_id=1, source_target_pairs={{0,32},{1,33},{2,34},{3,35},{4,36},{5,37},{6,38},{7,39},{8,40},{9,... | collective-permute-start | bytes 14155784 | tf_op jit(solution)/shard_map/ppermute | solution.py:88
  151.1 23.7 %all-to-all-start.2 = ((bf16[8,2,96,384]{3,2,1,0:T(8,128)(2,1)}), bf16[8,2,96,384]{3,2,1,0:T(8,128)(2,1)S(1)}, u32[]{:S(2)}, u32[]{:S(2)}) async-start(bf16[8,2,96,384]{3,2,1,0:T(8,128)(2,1)} %attend.5), calls=%async_computation.2 | async-start | bytes 2359296 | tf_op jit(solution)/shard_map/all_to_all | solution.py:92
  174.8 1.0 copy-start.4
